TPU v7x, 32 devices: a whole 2x2x4 slice. The times are simulated.
32 devices in a mesh: groups: 2 (over y), tok: 16 (over z, x, core).
Axes of the slice: x: 2, y: 2, z: 4, core: 2. Of those that a mesh axis runs over, the one named last changes fastest.
Arguments:
- queries: bfloat16 [2048, 2048], P(('groups', 'tok')), parts along dimension 0, may hold values from -256 to 256, as said below
- fresh_keys: bfloat16 [2048, 2048], P(('groups', 'tok')), parts along dimension 0, may hold values from -6 to 6, as said below
- fresh_values: bfloat16 [2048, 2048], P(('groups', 'tok')), parts along dimension 0, may hold values from -6 to 6
- stale_keys: bfloat16 [2048, 2048], P(('groups', 'tok')), parts along dimension 0, may hold values from -6 to 6
- stale_values: bfloat16 [2048, 2048], P(('groups', 'tok')), parts along dimension 0, may hold values from -6 to 6
- patch_starts: int32 [32], P('groups'), parts along dimension 0, may hold values from 0 to 1023, as said below
- order_starts: int32 [32], P('groups'), parts along dimension 0, may hold values from 0 to 1023, as said below
Outputs:
- attended: bfloat16 [2048, 2048], P(('groups', 'tok')), parts along dimension 0
There are 2 independent parts, one for each index of `groups`. A program takes and returns all parts, laid end to end along the dimension named above; each array names one. Nothing has to cross between parts.
Inputs may be any that keep to these rules, and one draw needn't show every extreme that they name: `patch_starts`: strictly increasing; the first entry is 0. `order_starts`: the entries of patch_starts, each once, in processing order. `queries`: entries are finite. `fresh_keys`: entries are finite.
All inputs are finite; a program needn't handle non-finite values.
Results may differ from a plain program's by a relative error of at most 0.0049.
Values may be sent and summed in bfloat16 or wider, within the bound.
No kernel may reach another device: no remote copies, remote signals or barrier semaphores. Data moves between devices by JAX's collectives and lax.ppermute only.
A program may use at most 128 MiB of HBM per device.

v0:
```python
import math

import jax
import jax.numpy as jnp
from jax import lax
from jax.sharding import PartitionSpec as P

HEADS = 16
HEAD_DIM = 128


def token_ranks(positions, patch_starts, order_starts):
    patch_count = patch_starts.shape[0]
    slot_ids = jnp.arange(patch_count, dtype=jnp.int32)
    patch_of = jnp.sum((patch_starts[None, :] <= positions[:, None]).astype(jnp.int32), axis=1) - 1
    matches = (order_starts[:, None] == patch_starts[None, :]).astype(jnp.int32)
    rank_of = jnp.sum(matches * slot_ids[:, None], axis=0)
    one_hot = (patch_of[:, None] == slot_ids[None, :]).astype(jnp.int32)
    return jnp.sum(one_hot * rank_of[None, :], axis=1)


def masked_scores(query_block, query_rank, key_stack, key_rank):
    dims = (((1,), (1,)), ((), ()))
    score_scale = 1.0 / math.sqrt(query_block.shape[-1])
    fresh_scores = (
        lax.dot_general(query_block, key_stack[0], dims, preferred_element_type=jnp.float32)
        * score_scale
    )
    stale_scores = (
        lax.dot_general(query_block, key_stack[2], dims, preferred_element_type=jnp.float32)
        * score_scale
    )
    fresh_ok = key_rank[None, :] <= query_rank[:, None]
    fresh_scores = jnp.where(fresh_ok, fresh_scores, -jnp.inf)
    stale_scores = jnp.where(fresh_ok, -jnp.inf, stale_scores)
    return (fresh_scores, stale_scores)


def attend_block(query_block, query_rank, key_stack, key_rank):
    fresh_scores, stale_scores = masked_scores(query_block, query_rank, key_stack, key_rank)
    row_max = jnp.maximum(jnp.max(fresh_scores, axis=1), jnp.max(stale_scores, axis=1))[:, None]
    fresh_exp = jnp.exp(fresh_scores - row_max)
    stale_exp = jnp.exp(stale_scores - row_max)
    row_total = jnp.sum(fresh_exp, axis=1, keepdims=True) + jnp.sum(
        stale_exp, axis=1, keepdims=True
    )
    fresh_probs = (fresh_exp / row_total).astype(jnp.bfloat16)
    stale_probs = (stale_exp / row_total).astype(jnp.bfloat16)
    mixed = jnp.dot(fresh_probs, key_stack[1], preferred_element_type=jnp.float32)
    mixed = mixed + jnp.dot(stale_probs, key_stack[3], preferred_element_type=jnp.float32)
    return mixed.astype(jnp.bfloat16)


def attend_rows(query_rows, query_rank, key_stack, key_rank):
    row_count = query_rows.shape[0]
    block_rows = 512
    blocks = row_count // block_rows

    def one_block(inputs):
        return attend_block(inputs[0], inputs[1], key_stack, key_rank)

    result = lax.map(
        one_block,
        (
            query_rows.reshape(blocks, block_rows, query_rows.shape[1]),
            query_rank.reshape(blocks, block_rows),
        ),
    )
    return result.reshape(row_count, query_rows.shape[1])


def shards(queries, fresh_keys, fresh_values, stale_keys, stale_values, patch_starts, order_starts):
    devices = lax.axis_size("tok")
    tok_dev, row_width = queries.shape
    group_size = devices // HEADS
    slab_rows = tok_dev // group_size
    my_index = lax.axis_index("tok")
    member = my_index % group_size
    query_slabs = (
        queries.reshape(group_size, slab_rows, HEADS, HEAD_DIM)
        .transpose(2, 0, 1, 3)
        .reshape(devices, slab_rows, HEAD_DIM)
    )
    query_rows = lax.all_to_all(query_slabs, "tok", split_axis=0, concat_axis=0, tiled=True)
    stacked = jnp.stack([fresh_keys, fresh_values, stale_keys, stale_values]).reshape(
        4, tok_dev, HEADS, HEAD_DIM
    )
    sender_base = jnp.arange(devices, dtype=jnp.int32)[:, None] * tok_dev
    slab_offsets = jnp.arange(slab_rows, dtype=jnp.int32)[None, :]
    query_pos = (sender_base + member * slab_rows + slab_offsets).reshape(-1)
    by_head = stacked.transpose(0, 2, 1, 3)[:, :, None]
    spread = jnp.broadcast_to(by_head, (4, HEADS, group_size, tok_dev, HEAD_DIM)).reshape(
        4, devices, tok_dev, HEAD_DIM
    )
    arrived = lax.all_to_all(spread, "tok", split_axis=1, concat_axis=1, tiled=True)
    key_stack = arrived.reshape(4, devices * tok_dev, HEAD_DIM)
    key_rank = token_ranks(
        jnp.arange(devices * tok_dev, dtype=jnp.int32), patch_starts, order_starts
    )
    query_rank = token_ranks(query_pos, patch_starts, order_starts)
    attended = attend_rows(
        query_rows.reshape(devices * slab_rows, HEAD_DIM), query_rank, key_stack, key_rank
    )
    returned = lax.all_to_all(
        attended.reshape(devices, slab_rows, HEAD_DIM),
        "tok",
        split_axis=0,
        concat_axis=0,
        tiled=True,
    )
    return (
        returned.reshape(HEADS, group_size, slab_rows, HEAD_DIM)
        .transpose(1, 2, 0, 3)
        .reshape(tok_dev, row_width)
    )


def solution(mesh):
    placed = (
        P(("groups", "tok"), None),
        P(("groups", "tok"), None),
        P(("groups", "tok"), None),
        P(("groups", "tok"), None),
        P(("groups", "tok"), None),
        P("groups"),
        P("groups"),
    )
    return jax.shard_map(
        shards, mesh=mesh, in_specs=placed, out_specs=P(("groups", "tok"), None), check_vma=False
    )
```

profile of v0, /device:TPU:0, one launch (start us, length us, event | category | flops | bytes accessed | tf_op | source)
XLA Modules:
  0.0 72.6 jit_solution(15579702160136215881)
XLA Ops:
  0.0 1.0 %copy.24 = bf16[8,8,16,128]{3,2,1,0:T(8,128)(2,1)S(1)} copy(bf16[8,8,16,128]{3,1,2,0:T(8,128)(2,1)} %bitcast.87) | data formatting | bytes 524288
  1.0 1.0 %copy.25 = bf16[8,8,16,128]{3,2,1,0:T(8,128)(2,1)S(1)} copy(bf16[8,8,16,128]{3,1,2,0:T(8,128)(2,1)} %bitcast.88) | data formatting | bytes 524288
  2.0 1.0 %copy.26 = bf16[8,8,16,128]{3,2,1,0:T(8,128)(2,1)S(1)} copy(bf16[8,8,16,128]{3,1,2,0:T(8,128)(2,1)} %bitcast.89) | data formatting | bytes 524288
  3.0 1.0 %copy.27 = bf16[8,8,16,128]{3,2,1,0:T(8,128)(2,1)S(1)} copy(bf16[8,8,16,128]{3,1,2,0:T(8,128)(2,1)} %bitcast.90) | data formatting | bytes 524288
  4.0 0.1 maximum_bitcast_fusion
  4.1 0.0 copy-start
  4.1 1.3 %copy.20 = bf16[4,16,64,128]{3,2,0,1:T(8,128)(2,1)} copy(bf16[4,16,64,128]{3,1,2,0:T(8,128)(2,1)S(1)} %maximum_bitcast_fusion) | data formatting | bytes 2097152 | tf_op jit(solution)/shard_map/transpose | solution.py:91
  5.4 7.5 %all-to-all-start.1 = ((bf16[4,16,64,128]{3,2,0,1:T(8,128)(2,1)}), bf16[4,16,64,128]{3,2,0,1:T(8,128)(2,1)S(1)}, u32[]{:S(2)}, u32[]{:S(2)}) async-start(bf16[4,16,64,128]{3,2,0,1:T(8,128)(2,1)} %copy.20), calls=%async_computation.1 | async-start | bytes 2097152 | tf_op jit(solution)/shard_map/all_to_all | solution.py:95
  13.0 0.8 %copy.32 = bf16[1,64,16,128]{3,1,2,0:T(8,128)(2,1)} copy(bf16[1,64,16,128]{3,2,1,0:T(8,128)(2,1)S(1)} %bitcast.82) | data formatting | bytes 524288 | tf_op jit(solution)/shard_map/reshape | solution.py:80
  13.7 0.1 iota_add_fusion
  13.8 22.0 %all-to-all-done.1 = bf16[4,16,64,128]{3,2,0,1:T(8,128)(2,1)S(1)} async-done(((bf16[4,16,64,128]{3,2,0,1:T(8,128)(2,1)}), bf16[4,16,64,128]{3,2,0,1:T(8,128)(2,1)S(1)}, u32[]{:S(2)}, u32[]{:S(2)}) %all-to-all-start.1) | async-done | bytes 1048608 | tf_op jit(solution)/shard_map/all_to_all | solution.py:95
  35.8 6.9 %all-to-all-start = ((bf16[16,64,128]{2,1,0:T(8,128)(2,1)}), bf16[16,64,128]{2,1,0:T(8,128)(2,1)S(1)}, u32[]{:S(2)}, u32[]{:S(2)}) async-start(bf16[16,64,128]{2,1,0:T(8,128)(2,1)} %bitcast.62), calls=%async_computation | async-start | bytes 524288 | tf_op jit(solution)/shard_map/all_to_all | solution.py:84
  42.7 0.1 select_reduce_fusion.2
  42.8 0.1 add.53
  42.9 0.1 convert_reduce_fusion
  43.0 0.1 select_reduce_fusion
  43.1 0.1 copy.21
  43.2 9.5 %all-to-all-done = bf16[16,64,128]{2,1,0:T(8,128)(2,1)S(1)} async-done(((bf16[16,64,128]{2,1,0:T(8,128)(2,1)}), bf16[16,64,128]{2,1,0:T(8,128)(2,1)S(1)}, u32[]{:S(2)}, u32[]{:S(2)}) %all-to-all-start) | async-done | bytes 262176 | tf_op jit(solution)/shard_map/all_to_all | solution.py:84
  52.8 6.0 %while.10 = (s32[]{:T(128)}, bf16[2,512,128]{2,1,0:T(8,128)(2,1)S(1)}, s32[1024]{0:T(1024)S(1)}, s32[2,512]{1,0:T(2,128)S(1)}, bf16[2,512,128]{2,1,0:T(8,128)(2,...) while((s32[]{:T(128)}, bf16[2,512,128]{2,1,0:T(8,128)(2,1)S(1)}, s32[1024]{0:T(1024)S(1)}, ...), condition=%wide.region_10.11_spmd, body=%wide.region_5.10_spmd.sunk | while | flops 546438144 | bytes 14596189 | solution.py:62
  52.8 0.5 fusion.31
  53.3 0.5 fusion.32
  53.9 0.7 fusion.33
  54.6 0.6 fusion.34
  55.1 0.6 fusion.35
  55.8 0.5 fusion.31
  56.3 0.5 fusion.32
  56.9 0.7 fusion.33
  57.6 0.6 fusion.34
  58.2 0.6 fusion.35
  58.8 12.8 %all_to_all.15 = bf16[16,64,128]{2,1,0:T(8,128)(2,1)S(1)} all-to-all(bf16[16,64,128]{2,1,0:T(8,128)(2,1)S(1)} %bitcast.93), channel_id=1, replica_groups=mesh['groups'=2,'tok'=16] {'tok'}, dimensions={0} | all-to-all | bytes 524288 | tf_op jit(solution)/shard_map/all_to_all | solution.py:104
  71.6 0.2 copy.22
  71.8 0.8 %copy.31 = bf16[8,8,16,128]{3,1,2,0:T(8,128)(2,1)} copy(bf16[8,8,16,128]{3,2,1,0:T(8,128)(2,1)S(1)} %bitcast.81) | data formatting | bytes 524288
  (16 shorter events, 0.1 us)
Async XLA Ops:
  4.1 8.8 %copy-start = (bf16[64,2048]{1,0:T(8,128)(2,1)S(1)}, bf16[64,2048]{1,0:T(8,128)(2,1)}, u32[]{:S(2)}) copy-start(bf16[64,2048]{1,0:T(8,128)(2,1)} %param.9) | copy-start | bytes 786436
  5.4 37.3 %copy-start.1 = (s32[16]{0:T(128)S(1)}, s32[16]{0:T(128)}, u32[]{:S(2)}) copy-start(s32[16]{0:T(128)} %param.14) | copy-start | bytes 196
  5.4 37.3 %copy-start.2 = (s32[16]{0:T(128)S(1)}, s32[16]{0:T(128)}, u32[]{:S(2)}) copy-start(s32[16]{0:T(128)} %param.15) | copy-start | bytes 196
  5.4 30.4 %all-to-all-start.1 = ((bf16[4,16,64,128]{3,2,0,1:T(8,128)(2,1)}), bf16[4,16,64,128]{3,2,0,1:T(8,128)(2,1)S(1)}, u32[]{:S(2)}, u32[]{:S(2)}) async-start(bf16[4,16,64,128]{3,2,0,1:T(8,128)(2,1)} %copy.20), calls=%async_computation.1 | async-start | bytes 2097152 | tf_op jit(solution)/shard_map/all_to_all | solution.py:95
  35.8 16.9 %all-to-all-start = ((bf16[16,64,128]{2,1,0:T(8,128)(2,1)}), bf16[16,64,128]{2,1,0:T(8,128)(2,1)S(1)}, u32[]{:S(2)}, u32[]{:S(2)}) async-start(bf16[16,64,128]{2,1,0:T(8,128)(2,1)} %bitcast.62), calls=%async_computation | async-start | bytes 524288 | tf_op jit(solution)/shard_map/all_to_all | solution.py:84
where the time goes:
time: 73 us; the launch traced here: 72.6 us
  waiting for transfers between devices  31.6 us (43%)
  starting transfers between devices  14.4 us (20%)
  blocking collectives  12.8 us (18%)
  local copies, waits for them, and re-layouts  7.16 us (10%)
  matrix products  4.49 us (6%)
  other arithmetic  1.96 us (3%)
    all_to_all x1, waiting for transfers between devices, shards(): lax.all_to_all(spread, 'tok', split_axis=1, concat_axis=1, tiled=True)  22 us
    all_to_all x1, blocking collectives, shards(): lax.all_to_all(attended.reshape(devices, slab_rows, HEAD_DIM), 'tok', spl...  12.8 us
    all_to_all x1, waiting for transfers between devices, shards(): lax.all_to_all(query_slabs, 'tok', split_axis=0, concat_axis=0, tiled=True)  9.54 us
    all_to_all x1, starting transfers between devices, shards(): lax.all_to_all(spread, 'tok', split_axis=1, concat_axis=1, tiled=True)  7.49 us
    all_to_all x1, starting transfers between devices, shards(): lax.all_to_all(query_slabs, 'tok', split_axis=0, concat_axis=0, tiled=True)  6.86 us
    unnamed x12, local copies, waits for them, and re-layouts  4.77 us
  transfers between devices with their start and end apart: 2, of which 2 were waited for; matrix products, arithmetic and copies ran while one was open for 2% of the time, Pallas kernels for 0%

commit v1 on v0

v1 whole, which is shorter than its diff:
```python
import functools
import math

import jax
import jax.numpy as jnp
from jax import lax
from jax.experimental import pallas as pl
from jax.experimental.pallas import tpu as pltpu
from jax.sharding import PartitionSpec as P

HEADS = 16
HEAD_DIM = 128
CORES = 2
STAT_ROWS = 16
STAT_TERMS = 4
CHUNK = 4
VMEM_LIMIT = 48 * 1024 * 1024


def token_ranks(positions, patch_starts, order_starts):
    patch_count = patch_starts.shape[0]
    slot_ids = jnp.arange(patch_count, dtype=jnp.int32)
    patch_of = jnp.sum((patch_starts[None, :] <= positions[:, None]).astype(jnp.int32), axis=1) - 1
    matches = (order_starts[:, None] == patch_starts[None, :]).astype(jnp.int32)
    rank_of = jnp.sum(matches * slot_ids[:, None], axis=0)
    one_hot = (patch_of[:, None] == slot_ids[None, :]).astype(jnp.int32)
    return jnp.sum(one_hot * rank_of[None, :], axis=1)


def split_kernel(members, width, where, queries, *rest):
    tensors, outs, sems = rest[:4], rest[4:-1], rest[-1]
    copies = []
    for step in range(members):
        start = pl.multiple_of((where[0] ^ step) * width, width)
        for at, tensor in enumerate(tensors):
            copies.append((tensor.at[:, pl.ds(start, width)], outs[step].at[at]))
        copies.append((queries.at[:, pl.ds(start, width)], outs[members + step]))
    started = [
        pltpu.make_async_copy(src, dst, sems.at[i]) for i, (src, dst) in enumerate(copies)
    ]
    for copy in started:
        copy.start()
    for copy in started:
        copy.wait()


def split_columns(member, members, queries, tensors):
    rows, columns = queries.shape
    width = columns // members
    kinds = len(tensors)
    outs = [jax.ShapeDtypeStruct((kinds, rows, width), queries.dtype)] * members
    outs += [jax.ShapeDtypeStruct((rows, width), queries.dtype)] * members
    anywhere = pl.BlockSpec(memory_space=pl.ANY)
    size = (kinds + 1) * rows * columns * 2
    result = pl.pallas_call(
        functools.partial(split_kernel, members, width),
        out_shape=outs,
        in_specs=[pl.BlockSpec(memory_space=pltpu.SMEM)] + [anywhere] * (kinds + 1),
        out_specs=[anywhere] * len(outs),
        scratch_shapes=[pltpu.SemaphoreType.DMA((members * (kinds + 1),))],
        cost_estimate=pl.CostEstimate(flops=0, bytes_accessed=2 * size, transcendentals=0),
        name="split_columns",
    )(member, queries, *tensors)
    return result[:members], result[members:]


def attend_kernel(sources, blocks, heads, key_rank, query_rank, *refs):
    queries, keys = refs[:sources], refs[sources : sources + blocks]
    outs, stats = refs[sources + blocks : -1], refs[-1]
    head = pl.program_id(0)
    rows = queries[0].shape[0]
    dims = (((1,), (1,)), ((), ()))
    scale = math.log2(math.e) / math.sqrt(HEAD_DIM)
    query = jnp.concatenate([ref[...] for ref in queries], axis=0)
    fresh_keys, fresh_values, stale_keys, stale_values = (
        jnp.concatenate([ref[kind] for ref in keys], axis=0) for kind in range(4)
    )
    fresh_ok = key_rank[...] <= query_rank[...]
    fresh = lax.dot_general(query, fresh_keys, dims, preferred_element_type=jnp.float32)
    stale = lax.dot_general(query, stale_keys, dims, preferred_element_type=jnp.float32)
    scores = jnp.where(fresh_ok, fresh, stale)
    row_max = jnp.max(scores, axis=1, keepdims=True)
    weights = jnp.exp2((scores - row_max) * scale)
    total = jnp.sum(weights, axis=1, keepdims=True)
    fresh_weights = jnp.where(fresh_ok, weights, 0.0).astype(jnp.bfloat16)
    stale_weights = jnp.where(fresh_ok, 0.0, weights).astype(jnp.bfloat16)
    mixed = jnp.dot(fresh_weights, fresh_values, preferred_element_type=jnp.float32)
    mixed = mixed + jnp.dot(stale_weights, stale_values, preferred_element_type=jnp.float32)
    mixed = (mixed / total).astype(jnp.bfloat16)
    at = pl.multiple_of(head * rows, rows)
    for i, out in enumerate(outs):
        out[pl.ds(at, rows), :] = mixed[i * rows : (i + 1) * rows]
    level = row_max * scale + jnp.log2(total)
    high = level.astype(jnp.bfloat16).astype(jnp.float32)
    middle = (level - high).astype(jnp.bfloat16).astype(jnp.float32)
    low = level - high - middle
    lane = lax.broadcasted_iota(jnp.int32, stats.shape, 1) - head * STAT_TERMS
    kept = jnp.where(head == 0, 0.0, stats[...])
    kept = jnp.where(lane == 0, high, kept)
    kept = jnp.where(lane == 1, middle, kept)
    kept = jnp.where(lane == 2, low, kept)
    stats[...] = kept

    @pl.when(head == heads - 1)
    def _():
        turned = kept.T[:STAT_ROWS]
        for i, out in enumerate(outs):
            mine = turned[:, i * rows : (i + 1) * rows].astype(jnp.bfloat16)
            filler = jnp.zeros((STAT_ROWS, HEAD_DIM - rows), jnp.bfloat16)
            out[heads * rows :, :] = jnp.concatenate([mine, filler], axis=1)


def attend(queries, query_rank, keys, key_rank):
    sources, blocks = len(queries), len(keys)
    rows, width = queries[0].shape
    kinds = keys[0].shape[0]
    heads = width // HEAD_DIM
    query_count, key_count = sources * rows, blocks * rows
    whole = lambda *shape: pl.BlockSpec(shape, lambda h: (0,) * len(shape))
    out_rows = heads * rows + STAT_ROWS
    return pl.pallas_call(
        functools.partial(attend_kernel, sources, blocks, heads),
        grid=(heads,),
        out_shape=[jax.ShapeDtypeStruct((out_rows, HEAD_DIM), jnp.bfloat16)] * sources,
        in_specs=[whole(1, key_count), whole(query_count, 1)]
        + [pl.BlockSpec((rows, HEAD_DIM), lambda h: (0, h))] * sources
        + [pl.BlockSpec((kinds, rows, HEAD_DIM), lambda h: (0, 0, h))] * blocks,
        out_specs=[whole(out_rows, HEAD_DIM)] * sources,
        scratch_shapes=[pltpu.VMEM((query_count, HEAD_DIM), jnp.float32)],
        compiler_params=pltpu.CompilerParams(vmem_limit_bytes=VMEM_LIMIT),
        cost_estimate=pl.CostEstimate(
            flops=8 * heads * query_count * key_count * HEAD_DIM,
            bytes_accessed=2 * width * (query_count * 2 + key_count * kinds),
            transcendentals=heads * query_count * key_count,
        ),
        name="attend",
    )(key_rank[None, :], query_rank[:, None], *queries, *keys)


def merge_kernel(parts, members, heads, where, *refs):
    partials, out = refs[:-1], refs[-1]
    rows = out.shape[0]
    for step in range(members):
        group = partials[step * parts : (step + 1) * parts]
        start = (where[0] ^ step) * heads * HEAD_DIM
        levels = []
        for ref in group:
            stats = ref[heads * rows :, :].astype(jnp.float32)
            levels.append(stats.T[:rows])
        for head in range(heads):
            lane = head * STAT_TERMS
            level = [
                one[:, lane : lane + 1] + one[:, lane + 1 : lane + 2] + one[:, lane + 2 : lane + 3]
                for one in levels
            ]
            top = functools.reduce(jnp.maximum, level)
            shares = [jnp.exp2(one - top) for one in level]
            total = functools.reduce(jnp.add, shares)
            mixed = functools.reduce(
                jnp.add,
                [
                    ref[head * rows : (head + 1) * rows, :].astype(jnp.float32) * (share / total)
                    for ref, share in zip(group, shares)
                ],
            )
            at = pl.multiple_of(start + head * HEAD_DIM, HEAD_DIM)
            out[:, pl.ds(at, HEAD_DIM)] = mixed.astype(out.dtype)


def merge(member, partials, rows, heads):
    members, parts = len(partials), len(partials[0])
    flat = [one for group in partials for one in group]
    vmem = pl.BlockSpec(memory_space=pltpu.VMEM)
    return pl.pallas_call(
        functools.partial(merge_kernel, parts, members, heads),
        out_shape=jax.ShapeDtypeStruct((rows, members * heads * HEAD_DIM), jnp.bfloat16),
        in_specs=[pl.BlockSpec(memory_space=pltpu.SMEM)] + [vmem] * len(flat),
        out_specs=vmem,
        compiler_params=pltpu.CompilerParams(vmem_limit_bytes=VMEM_LIMIT),
        name="merge",
    )(member, *flat)


def shards(queries, fresh_keys, fresh_values, stale_keys, stale_values, patch_starts, order_starts):
    devices = lax.axis_size("tok")
    rows = queries.shape[0]
    chips = devices // CORES
    members = min(chips // 2, HEADS)
    groups = chips // members
    heads = HEADS // members
    me = lax.axis_index("tok")
    core, chip = me % CORES, me // CORES
    group, member = chip // members, chip % members
    where = member[None].astype(jnp.int32)

    def hop(array, far, near, side=0):
        flip = (far * members + near) * CORES + side
        if flip == 0:
            return array
        return lax.ppermute(array, "tok", [(i, i ^ flip) for i in range(devices)])

    def positions(far, near, side):
        base = (((group ^ far) * members + (member ^ near)) * CORES + (core ^ side)) * rows
        return base + jnp.arange(rows, dtype=jnp.int32)

    def ranks(places):
        spots = jnp.concatenate([positions(*place) for place in places])
        return token_ranks(spots, patch_starts, order_starts)

    tensors = (fresh_keys, fresh_values, stale_keys, stale_values)
    key_parts, query_parts = split_columns(where, members, queries, tensors)
    order = list(range(members))[::-1]
    keys = {}
    for near in order:
        keys[near, 0] = hop(key_parts[near], 0, near)
    for near in order:
        keys[near, 1] = hop(keys[near, 0], 0, 0, 1)
    places = [(near, side) for near in range(members) for side in range(CORES)]
    key_rank = ranks([(0, near, side) for near, side in places])
    key_blocks = [keys[place] for place in places]
    partials = [[None] * groups for _ in range(members)]
    for far in list(range(groups))[::-1]:
        for first in range(0, members, CHUNK):
            chunk = order[first : first + CHUNK]
            arrived = [hop(query_parts[near], far, near) for near in chunk]
            query_rank = ranks([(far, near, 0) for near in chunk])
            results = attend(arrived, query_rank, key_blocks, key_rank)
            for near, result in zip(chunk, results):
                partials[near][far] = hop(result, far, near)
    return merge(where, partials, rows, heads)


def solution(mesh):
    placed = (P(("groups", "tok"), None),) * 5 + (P("groups"),) * 2
    return jax.shard_map(
        shards, mesh=mesh, in_specs=placed, out_specs=P(("groups", "tok"), None), check_vma=False
    )
```

time: 73 us -> 107 us (1.47)
  Pallas kernels: 0 us -> 49.6 us
  blocking collectives: 12.8 us -> 0 us
  starting transfers between devices: 14.4 us -> 26.3 us
  local copies, waits for them, and re-layouts: 7.16 us -> 0.36 us
  matrix products: 4.49 us -> 0 us
  waiting for transfers between devices: 31.6 us -> 29.5 us
  other arithmetic: 1.96 us -> 0.63 us
    pallas_call x0 -> x4, Pallas kernels: none -> 49.6 us  [the longest x1 41 us: split_columns(): pl.pallas_call(functools.partial(split_kernel, members, width), out_shape...]
    all_to_all x2 -> x0, waiting for transfers between devices: 31.6 us -> none  [the longest x1 22 us: shards(): lax.all_to_all(spread, 'tok', split_axis=1, concat_axis=1, tiled=True)]
    ppermute x0 -> x21, waiting for transfers between devices: none -> 29.5 us  [hop(): return lax.ppermute(array, 'tok', [(i, i ^ flip) for i in range(devices)])]
    ppermute x0 -> x21, starting transfers between devices: none -> 26.3 us  [hop(): return lax.ppermute(array, 'tok', [(i, i ^ flip) for i in range(devices)])]
    all_to_all x2 -> x0, starting transfers between devices: 14.4 us -> none  [the longest x1 7.49 us: shards(): lax.all_to_all(spread, 'tok', split_axis=1, concat_axis=1, tiled=True)]
    all_to_all x1 -> x0, blocking collectives: 12.8 us -> none  [shards(): lax.all_to_all(attended.reshape(devices, slab_rows, HEAD_DIM), 'tok', spl...]
    unnamed x12 -> x8, local copies, waits for them, and re-layouts: 4.77 us -> 0.02 us
    dot_general x8 -> x0, matrix products: 4.49 us -> none  [the longest x2 1.23 us: attend_block(): jnp.dot(stale_probs, key_stack[3], preferred_element_type=jnp.float32)]
  transfers between devices with their start and end apart: 2 -> 21, of which waited for: 2 -> 7; matrix products, arithmetic and copies ran while one was open for 2% -> 1% of each run, Pallas kernels for 0% -> 6%
where the time goes in v1:
time: 107 us; the launch traced here: 106 us
  Pallas kernels  49.6 us (46%)
  waiting for transfers between devices  29.5 us (28%)
  starting transfers between devices  26.3 us (25%)
    pallas_call x1, Pallas kernels, split_columns(): pl.pallas_call(functools.partial(split_kernel, members, width), out_shape...  41 us
    ppermute x21, waiting for transfers between devices, hop(): return lax.ppermute(array, 'tok', [(i, i ^ flip) for i in range(devices)])  29.5 us
    ppermute x21, starting transfers between devices, hop(): return lax.ppermute(array, 'tok', [(i, i ^ flip) for i in range(devices)])  26.3 us
    pallas_call x2, Pallas kernels, attend(): pl.pallas_call(functools.partial(attend_kernel, sources, blocks, heads),...  6.89 us
  transfers between devices with their start and end apart: 21, of which 7 were waited for; matrix products, arithmetic and copies ran while one was open for 1% of the time, Pallas kernels for 6%

profile of v1, /device:TPU:0, one launch (start us, length us, event | category | flops | bytes accessed | tf_op | source)
XLA Modules:
  0.0 106.5 jit_solution(6301818854024508863)
XLA Ops:
  0.0 41.0 %split_columns.1 = (bf16[4,64,512]{2,1,0:T(8,128)(2,1)}, bf16[4,64,512]{2,1,0:T(8,128)(2,1)}, bf16[4,64,512]{2,1,0:T(8,128)(2,1)}, bf16[4,64,512]{2,1,0:T(8,128)...) custom-call(s32[1]{0:T(128)} %bitcast.where, ...), custom_call_target="tpu_custom_call" | custom-call | bytes 2621440 | tf_op jit(solution)/shard_map/split_columns/pallas_call | solution.py:55
  41.0 3.0 %collective-permute-start.4 = (bf16[4,64,512]{2,1,0:T(8,128)(2,1)}, bf16[4,64,512]{2,1,0:T(8,128)(2,1)S(1)}, u32[]{:S(2)}, u32[]{:S(2)}) collective-permute-start(bf16[4,64,512]{2,1,0:T(8,128)(2,1)} %get-tuple-element.26), channel_id=1, source_target_pairs={{0,2},{1,3},{2,0},{3,1},{4,6},{5,7},{6,4},{7,5},{8,10},{9,11},{10,... | collective-permute-start | bytes 786440 | tf_op jit(solution)/shard_map/ppermute | solution.py:200
  44.0 1.6 %collective-permute-start.6 = (bf16[4,64,512]{2,1,0:T(8,128)(2,1)}, bf16[4,64,512]{2,1,0:T(8,128)(2,1)S(1)}, u32[]{:S(2)}, u32[]{:S(2)}) collective-permute-start(bf16[4,64,512]{2,1,0:T(8,128)(2,1)} %get-tuple-element.27), channel_id=1, source_target_pairs={{0,4},{1,5},{2,6},{3,7},{4,0},{5,1},{6,2},{7,3},{8,12},{9,13},{10,... | collective-permute-start | bytes 786440 | tf_op jit(solution)/shard_map/ppermute | solution.py:200
  45.6 4.9 %collective-permute-start.10 = (bf16[64,512]{1,0:T(8,128)(2,1)}, bf16[64,512]{1,0:T(8,128)(2,1)S(1)}, u32[]{:S(2)}, u32[]{:S(2)}) collective-permute-start(bf16[64,512]{1,0:T(8,128)(2,1)} %get-tuple-element.21), channel_id=1, source_target_pairs={{0,14},{1,15},{2,12},{3,13},{4,10},{5,11},{6,8},{7,9},{8,6},{9,7},... | collective-permute-start | bytes 196616 | tf_op jit(solution)/shard_map/ppermute | solution.py:200
  50.7 0.1 convert_reduce_fusion
  50.9 0.1 convert_reduce_fusion.1
  51.0 10.0 %collective-permute-done.10.refs_0_ = bf16[64,512]{1,0:T(8,128)(2,1)S(1)} collective-permute-done((bf16[64,512]{1,0:T(8,128)(2,1)}, bf16[64,512]{1,0:T(8,128)(2,1)S(1)}, u32[]{:S(2)}, u32[]{:S(2)}) %collective-permute-start.10) | collective-permute-done | bytes 65568 | tf_op jit(solution)/shard_map/ppermute | solution.py:200
  61.0 1.4 %collective-permute-start.11 = (bf16[64,512]{1,0:T(8,128)(2,1)}, bf16[64,512]{1,0:T(8,128)(2,1)S(1)}, u32[]{:S(2)}, u32[]{:S(2)}) collective-permute-start(bf16[64,512]{1,0:T(8,128)(2,1)} %get-tuple-element.22), channel_id=1, source_target_pairs={{0,12},{1,13},{2,14},{3,15},{4,8},{5,9},{6,10},{7,11},{8,4},{9,5},... | collective-permute-start | bytes 196616 | tf_op jit(solution)/shard_map/ppermute | solution.py:200
  62.5 0.5 collective-permute-start.7
  63.1 0.1 select_reduce_fusion.3
  63.1 4.4 %collective-permute-done.11.refs_1_ = bf16[64,512]{1,0:T(8,128)(2,1)S(1)} collective-permute-done((bf16[64,512]{1,0:T(8,128)(2,1)}, bf16[64,512]{1,0:T(8,128)(2,1)S(1)}, u32[]{:S(2)}, u32[]{:S(2)}) %collective-permute-start.11) | collective-permute-done | bytes 65568 | tf_op jit(solution)/shard_map/ppermute | solution.py:200
  67.5 0.1 select_reduce_fusion.1
  67.6 0.1 copy.11.query_rank
  67.8 6.9 %collective-permute-done.12.refs_2_ = bf16[64,512]{1,0:T(8,128)(2,1)S(1)} collective-permute-done((bf16[64,512]{1,0:T(8,128)(2,1)}, bf16[64,512]{1,0:T(8,128)(2,1)S(1)}, u32[]{:S(2)}, u32[]{:S(2)}) %collective-permute-start.12) | collective-permute-done | bytes 65568 | tf_op jit(solution)/shard_map/ppermute | solution.py:200
  74.7 0.1 select_reduce_fusion
  74.7 5.2 %collective-permute-done.13.refs_3_ = bf16[64,512]{1,0:T(8,128)(2,1)S(1)} collective-permute-done((bf16[64,512]{1,0:T(8,128)(2,1)S(1)}, bf16[64,512]{1,0:T(8,128)(2,1)S(1)}, u32[]{:S(2)}, u32[]{:S(2)}) %collective-permute-start.13) | collective-permute-done | bytes 65568 | tf_op jit(solution)/shard_map/ppermute | solution.py:200
  79.9 0.1 collective-permute-start
  80.0 2.6 %collective-permute-start.1 = (bf16[64,512]{1,0:T(8,128)(2,1)}, bf16[64,512]{1,0:T(8,128)(2,1)S(1)}, u32[]{:S(2)}, u32[]{:S(2)}) collective-permute-start(bf16[64,512]{1,0:T(8,128)(2,1)} %get-tuple-element.22), channel_id=1, source_target_pairs={{0,4},{1,5},{2,6},{3,7},{4,0},{5,1},{6,2},{7,3},{8,12},{9,13},{10,... | collective-permute-start | bytes 196616 | tf_op jit(solution)/shard_map/ppermute | solution.py:200
  82.6 0.8 collective-permute-start.2
  83.4 3.5 %attend.3 = (bf16[272,128]{1,0:T(8,128)(2,1)S(1)}, bf16[272,128]{1,0:T(8,128)(2,1)S(1)}, bf16[272,128]{1,0:T(8,128)(2,1)S(1)}, bf16[272,128]{1,0:T(8,128)(2,1)S(1)}) custom-call(s32[1,512]{1,0:T(1,128)S(1)} %bitcast.4, s32[256,1]{1,0:T(8,128)S(1)} %copy.11.query_rank, bf16[64,512]{1,0:T(8,128)(2,1)S(1)} %collective-permute-done.10.refs_0_, ...), custom_call_target="tpu_custom_call" | custom-call | flops 536870912 | bytes 2621440 | tf_op jit(solution)/shard_map/attend/pallas_call | solution.py:121
  86.9 0.4 collective-permute-start.14
  87.3 3.2 %collective-permute-start.16 = (bf16[272,128]{1,0:T(8,128)(2,1)S(1)}, bf16[272,128]{1,0:T(8,128)(2,1)S(1)}, u32[]{:S(2)}, u32[]{:S(2)}) collective-permute-start(bf16[272,128]{1,0:T(8,128)(2,1)S(1)} %get-tuple-element.32), channel_id=1, source_target_pairs={{0,10},{1,11},{2,8},{3,9},{4,14},{5,15},{6,12},{7,13},{8,2},{9,3},... | collective-permute-start | bytes 208904 | tf_op jit(solution)/shard_map/ppermute | solution.py:200
  90.5 0.1 copy.10.query_rank
  90.6 1.9 %collective-permute-start.18 = (bf16[272,128]{1,0:T(8,128)(2,1)S(1)}, bf16[272,128]{1,0:T(8,128)(2,1)S(1)}, u32[]{:S(2)}, u32[]{:S(2)}) collective-permute-start(bf16[272,128]{1,0:T(8,128)(2,1)S(1)} %get-tuple-element.34), channel_id=1, source_target_pairs={{0,12},{1,13},{2,14},{3,15},{4,8},{5,9},{6,10},{7,11},{8,4},{9,5},... | collective-permute-start | bytes 208904 | tf_op jit(solution)/shard_map/ppermute | solution.py:200
  92.5 2.3 %collective-permute-start.20 = (bf16[272,128]{1,0:T(8,128)(2,1)S(1)}, bf16[272,128]{1,0:T(8,128)(2,1)S(1)}, u32[]{:S(2)}, u32[]{:S(2)}) collective-permute-start(bf16[272,128]{1,0:T(8,128)(2,1)S(1)} %get-tuple-element.36), channel_id=1, source_target_pairs={{0,14},{1,15},{2,12},{3,13},{4,10},{5,11},{6,8},{7,9},{8,6},{9,7},... | collective-permute-start | bytes 208904 | tf_op jit(solution)/shard_map/ppermute | solution.py:200
  94.8 3.4 %attend.2 = (bf16[272,128]{1,0:T(8,128)(2,1)S(1)}, bf16[272,128]{1,0:T(8,128)(2,1)S(1)}, bf16[272,128]{1,0:T(8,128)(2,1)S(1)}, bf16[272,128]{1,0:T(8,128)(2,1)S(1)}) custom-call(s32[1,512]{1,0:T(1,128)S(1)} %bitcast.5, s32[256,1]{1,0:T(8,128)S(1)} %copy.10.query_rank, bf16[64,512]{1,0:T(8,128)(2,1)S(1)} %collective-permute-done.refs_0_, ...), custom_call_target="tpu_custom_call" | custom-call | flops 536870912 | bytes 2621440 | tf_op jit(solution)/shard_map/attend/pallas_call | solution.py:121
  98.2 1.2 %collective-permute-start.15 = (bf16[272,128]{1,0:T(8,128)(2,1)S(1)}, bf16[272,128]{1,0:T(8,128)(2,1)S(1)}, u32[]{:S(2)}, u32[]{:S(2)}) collective-permute-start(bf16[272,128]{1,0:T(8,128)(2,1)S(1)} %get-tuple-element.31), channel_id=1, source_target_pairs={{0,2},{1,3},{2,0},{3,1},{4,6},{5,7},{6,4},{7,5},{8,10},{9,11},{10,... | collective-permute-start | bytes 208904 | tf_op jit(solution)/shard_map/ppermute | solution.py:200
  99.5 2.3 %collective-permute-start.19 = (bf16[272,128]{1,0:T(8,128)(2,1)S(1)}, bf16[272,128]{1,0:T(8,128)(2,1)S(1)}, u32[]{:S(2)}, u32[]{:S(2)}) collective-permute-start(bf16[272,128]{1,0:T(8,128)(2,1)S(1)} %get-tuple-element.35), channel_id=1, source_target_pairs={{0,6},{1,7},{2,4},{3,5},{4,2},{5,3},{6,0},{7,1},{8,14},{9,15},{10,... | collective-permute-start | bytes 208904 | tf_op jit(solution)/shard_map/ppermute | solution.py:200
  101.7 0.8 collective-permute-done.15.refs_2_
  102.5 1.2 %collective-permute-done.17.refs_4_ = bf16[272,128]{1,0:T(8,128)(2,1)S(1)} collective-permute-done((bf16[272,128]{1,0:T(8,128)(2,1)S(1)}, bf16[272,128]{1,0:T(8,128)(2,1)S(1)}, u32[]{:S(2)}, u32[]{:S(2)}) %collective-permute-start.17) | collective-permute-done | bytes 69664 | tf_op jit(solution)/shard_map/ppermute | solution.py:200
  103.8 1.0 collective-permute-done.19.refs_6_
  104.8 1.7 %merge.1 = bf16[64,2048]{1,0:T(8,128)(2,1)} custom-call(s32[1]{0:T(128)} %bitcast.where, bf16[272,128]{1,0:T(8,128)(2,1)S(1)} %get-tuple-element.29.refs_0_, bf16[272,128]{1,0:T(8,128)(2,1)S(1)} %collective-permute-done.14.refs_1_, bf16[272,128]{1,0:T(8,128)(2,1)S(1)} %collective-permute-done.15.refs_2_, ...), custom_call_target="tpu_custom_call" | custom-call | tf_op jit(solution)/shard_map/merge/pallas_call | solution.py:174
  (41 shorter events, 0.4 us)
Async XLA Ops:
  0.0 50.7 %copy-start.2 = (s32[16]{0:T(128)S(1)}, s32[16]{0:T(128)}, u32[]{:S(2)}) copy-start(s32[16]{0:T(128)} %param.12) | copy-start | bytes 196
  0.0 63.0 %copy-start.3 = (s32[16]{0:T(128)S(1)}, s32[16]{0:T(128)}, u32[]{:S(2)}) copy-start(s32[16]{0:T(128)} %param.13) | copy-start | bytes 196
  41.0 42.4 %copy-start = (bf16[4,64,512]{2,1,0:T(8,128)(2,1)S(1)}, bf16[4,64,512]{2,1,0:T(8,128)(2,1)}, u32[]{:S(2)}) copy-start(bf16[4,64,512]{2,1,0:T(8,128)(2,1)} %get-tuple-element.25.refs_4_) | copy-start | bytes 786436
  41.0 21.5 %collective-permute-start.4 = (bf16[4,64,512]{2,1,0:T(8,128)(2,1)}, bf16[4,64,512]{2,1,0:T(8,128)(2,1)S(1)}, u32[]{:S(2)}, u32[]{:S(2)}) collective-permute-start(bf16[4,64,512]{2,1,0:T(8,128)(2,1)} %get-tuple-element.26), channel_id=1, source_target_pairs={{0,2},{1,3},{2,0},{3,1},{4,6},{5,7},{6,4},{7,5},{8,10},{9,11},{10,... | collective-permute-start | bytes 786440 | tf_op jit(solution)/shard_map/ppermute | solution.py:200
  44.0 18.5 %collective-permute-start.6 = (bf16[4,64,512]{2,1,0:T(8,128)(2,1)}, bf16[4,64,512]{2,1,0:T(8,128)(2,1)S(1)}, u32[]{:S(2)}, u32[]{:S(2)}) collective-permute-start(bf16[4,64,512]{2,1,0:T(8,128)(2,1)} %get-tuple-element.27), channel_id=1, source_target_pairs={{0,4},{1,5},{2,6},{3,7},{4,0},{5,1},{6,2},{7,3},{8,12},{9,13},{10,... | collective-permute-start | bytes 786440 | tf_op jit(solution)/shard_map/ppermute | solution.py:200
  45.6 17.4 %collective-permute-start.8 = (bf16[4,64,512]{2,1,0:T(8,128)(2,1)}, bf16[4,64,512]{2,1,0:T(8,128)(2,1)S(1)}, u32[]{:S(2)}, u32[]{:S(2)}) collective-permute-start(bf16[4,64,512]{2,1,0:T(8,128)(2,1)} %get-tuple-element.28), channel_id=1, source_target_pairs={{0,6},{1,7},{2,4},{3,5},{4,2},{5,3},{6,0},{7,1},{8,14},{9,15},{10,... | collective-permute-start | bytes 786440 | tf_op jit(solution)/shard_map/ppermute | solution.py:200
  45.6 34.4 %collective-permute-start.3 = (bf16[4,64,512]{2,1,0:T(8,128)(2,1)}, bf16[4,64,512]{2,1,0:T(8,128)(2,1)S(1)}, u32[]{:S(2)}, u32[]{:S(2)}) collective-permute-start(bf16[4,64,512]{2,1,0:T(8,128)(2,1)} %get-tuple-element.25.refs_4_), channel_id=1, source_target_pairs={{0,1},{1,0},{2,3},{3,2},{4,5},{5,4},{6,7},{7,6},{8,9},{9,8},{10,11... | collective-permute-start | bytes 786440 | tf_op jit(solution)/shard_map/ppermute | solution.py:200
  45.6 15.4 %collective-permute-start.10 = (bf16[64,512]{1,0:T(8,128)(2,1)}, bf16[64,512]{1,0:T(8,128)(2,1)S(1)}, u32[]{:S(2)}, u32[]{:S(2)}) collective-permute-start(bf16[64,512]{1,0:T(8,128)(2,1)} %get-tuple-element.21), channel_id=1, source_target_pairs={{0,14},{1,15},{2,12},{3,13},{4,10},{5,11},{6,8},{7,9},{8,6},{9,7},... | collective-permute-start | bytes 196616 | tf_op jit(solution)/shard_map/ppermute | solution.py:200
  61.0 6.5 %collective-permute-start.11 = (bf16[64,512]{1,0:T(8,128)(2,1)}, bf16[64,512]{1,0:T(8,128)(2,1)S(1)}, u32[]{:S(2)}, u32[]{:S(2)}) collective-permute-start(bf16[64,512]{1,0:T(8,128)(2,1)} %get-tuple-element.22), channel_id=1, source_target_pairs={{0,12},{1,13},{2,14},{3,15},{4,8},{5,9},{6,10},{7,11},{8,4},{9,5},... | collective-permute-start | bytes 196616 | tf_op jit(solution)/shard_map/ppermute | solution.py:200
  62.5 20.1 %collective-permute-start.5 = (bf16[4,64,512]{2,1,0:T(8,128)(2,1)S(1)}, bf16[4,64,512]{2,1,0:T(8,128)(2,1)S(1)}, u32[]{:S(2)}, u32[]{:S(2)}) collective-permute-start(bf16[4,64,512]{2,1,0:T(8,128)(2,1)S(1)} %collective-permute-done.4.refs_6_), channel_id=1, source_target_pairs={{0,1},{1,0},{2,3},{3,2},{4,5},{5,4},{6,7},{7,6},{8,9},{9,8},{10,11... | collective-permute-start | bytes 786440 | tf_op jit(solution)/shard_map/ppermute | solution.py:200
  62.5 21.0 %collective-permute-start.7 = (bf16[4,64,512]{2,1,0:T(8,128)(2,1)S(1)}, bf16[4,64,512]{2,1,0:T(8,128)(2,1)S(1)}, u32[]{:S(2)}, u32[]{:S(2)}) collective-permute-start(bf16[4,64,512]{2,1,0:T(8,128)(2,1)S(1)} %collective-permute-done.6.refs_8_), channel_id=1, source_target_pairs={{0,1},{1,0},{2,3},{3,2},{4,5},{5,4},{6,7},{7,6},{8,9},{9,8},{10,11... | collective-permute-start | bytes 786440 | tf_op jit(solution)/shard_map/ppermute | solution.py:200
  63.0 20.5 %collective-permute-start.9 = (bf16[4,64,512]{2,1,0:T(8,128)(2,1)S(1)}, bf16[4,64,512]{2,1,0:T(8,128)(2,1)S(1)}, u32[]{:S(2)}, u32[]{:S(2)}) collective-permute-start(bf16[4,64,512]{2,1,0:T(8,128)(2,1)S(1)} %collective-permute-done.8.refs_10_), channel_id=1, source_target_pairs={{0,1},{1,0},{2,3},{3,2},{4,5},{5,4},{6,7},{7,6},{8,9},{9,8},{10,11... | collective-permute-start | bytes 786440 | tf_op jit(solution)/shard_map/ppermute | solution.py:200
  67.5 7.1 %collective-permute-start.12 = (bf16[64,512]{1,0:T(8,128)(2,1)}, bf16[64,512]{1,0:T(8,128)(2,1)S(1)}, u32[]{:S(2)}, u32[]{:S(2)}) collective-permute-start(bf16[64,512]{1,0:T(8,128)(2,1)} %get-tuple-element.23), channel_id=1, source_target_pairs={{0,10},{1,11},{2,8},{3,9},{4,14},{5,15},{6,12},{7,13},{8,2},{9,3},... | collective-permute-start | bytes 196616 | tf_op jit(solution)/shard_map/ppermute | solution.py:200
  67.6 7.0 %copy-start.1 = (bf16[64,512]{1,0:T(8,128)(2,1)S(1)}, bf16[64,512]{1,0:T(8,128)(2,1)}, u32[]{:S(2)}) copy-start(bf16[64,512]{1,0:T(8,128)(2,1)} %get-tuple-element.24.refs_3_) | copy-start | bytes 196612
  74.7 5.3 %collective-permute-start.13 = (bf16[64,512]{1,0:T(8,128)(2,1)S(1)}, bf16[64,512]{1,0:T(8,128)(2,1)S(1)}, u32[]{:S(2)}, u32[]{:S(2)}) collective-permute-start(bf16[64,512]{1,0:T(8,128)(2,1)S(1)} %copy-done.1), channel_id=1, source_target_pairs={{0,8},{1,9},{2,10},{3,11},{4,12},{5,13},{6,14},{7,15},{8,0},{9,1},... | collective-permute-start | bytes 196616 | tf_op jit(solution)/shard_map/ppermute | solution.py:200
  79.9 10.7 %collective-permute-start = (bf16[64,512]{1,0:T(8,128)(2,1)}, bf16[64,512]{1,0:T(8,128)(2,1)S(1)}, u32[]{:S(2)}, u32[]{:S(2)}) collective-permute-start(bf16[64,512]{1,0:T(8,128)(2,1)} %get-tuple-element.21), channel_id=1, source_target_pairs={{0,6},{1,7},{2,4},{3,5},{4,2},{5,3},{6,0},{7,1},{8,14},{9,15},{10,... | collective-permute-start | bytes 196616 | tf_op jit(solution)/shard_map/ppermute | solution.py:200
  80.0 12.5 %collective-permute-start.1 = (bf16[64,512]{1,0:T(8,128)(2,1)}, bf16[64,512]{1,0:T(8,128)(2,1)S(1)}, u32[]{:S(2)}, u32[]{:S(2)}) collective-permute-start(bf16[64,512]{1,0:T(8,128)(2,1)} %get-tuple-element.22), channel_id=1, source_target_pairs={{0,4},{1,5},{2,6},{3,7},{4,0},{5,1},{6,2},{7,3},{8,12},{9,13},{10,... | collective-permute-start | bytes 196616 | tf_op jit(solution)/shard_map/ppermute | solution.py:200
  82.6 12.2 %collective-permute-start.2 = (bf16[64,512]{1,0:T(8,128)(2,1)}, bf16[64,512]{1,0:T(8,128)(2,1)S(1)}, u32[]{:S(2)}, u32[]{:S(2)}) collective-permute-start(bf16[64,512]{1,0:T(8,128)(2,1)} %get-tuple-element.23), channel_id=1, source_target_pairs={{0,2},{1,3},{2,0},{3,1},{4,6},{5,7},{6,4},{7,5},{8,10},{9,11},{10,... | collective-permute-start | bytes 196616 | tf_op jit(solution)/shard_map/ppermute | solution.py:200
  86.9 12.6 %collective-permute-start.14 = (bf16[272,128]{1,0:T(8,128)(2,1)S(1)}, bf16[272,128]{1,0:T(8,128)(2,1)S(1)}, u32[]{:S(2)}, u32[]{:S(2)}) collective-permute-start(bf16[272,128]{1,0:T(8,128)(2,1)S(1)} %get-tuple-element.30), channel_id=1, source_target_pairs={{0,8},{1,9},{2,10},{3,11},{4,12},{5,13},{6,14},{7,15},{8,0},{9,1},... | collective-permute-start | bytes 208904 | tf_op jit(solution)/shard_map/ppermute | solution.py:200
  87.3 12.2 %collective-permute-start.16 = (bf16[272,128]{1,0:T(8,128)(2,1)S(1)}, bf16[272,128]{1,0:T(8,128)(2,1)S(1)}, u32[]{:S(2)}, u32[]{:S(2)}) collective-permute-start(bf16[272,128]{1,0:T(8,128)(2,1)S(1)} %get-tuple-element.32), channel_id=1, source_target_pairs={{0,10},{1,11},{2,8},{3,9},{4,14},{5,15},{6,12},{7,13},{8,2},{9,3},... | collective-permute-start | bytes 208904 | tf_op jit(solution)/shard_map/ppermute | solution.py:200
  90.6 11.1 %collective-permute-start.18 = (bf16[272,128]{1,0:T(8,128)(2,1)S(1)}, bf16[272,128]{1,0:T(8,128)(2,1)S(1)}, u32[]{:S(2)}, u32[]{:S(2)}) collective-permute-start(bf16[272,128]{1,0:T(8,128)(2,1)S(1)} %get-tuple-element.34), channel_id=1, source_target_pairs={{0,12},{1,13},{2,14},{3,15},{4,8},{5,9},{6,10},{7,11},{8,4},{9,5},... | collective-permute-start | bytes 208904 | tf_op jit(solution)/shard_map/ppermute | solution.py:200
  92.5 9.2 %collective-permute-start.20 = (bf16[272,128]{1,0:T(8,128)(2,1)S(1)}, bf16[272,128]{1,0:T(8,128)(2,1)S(1)}, u32[]{:S(2)}, u32[]{:S(2)}) collective-permute-start(bf16[272,128]{1,0:T(8,128)(2,1)S(1)} %get-tuple-element.36), channel_id=1, source_target_pairs={{0,14},{1,15},{2,12},{3,13},{4,10},{5,11},{6,8},{7,9},{8,6},{9,7},... | collective-permute-start | bytes 208904 | tf_op jit(solution)/shard_map/ppermute | solution.py:200
  98.2 4.3 %collective-permute-start.15 = (bf16[272,128]{1,0:T(8,128)(2,1)S(1)}, bf16[272,128]{1,0:T(8,128)(2,1)S(1)}, u32[]{:S(2)}, u32[]{:S(2)}) collective-permute-start(bf16[272,128]{1,0:T(8,128)(2,1)S(1)} %get-tuple-element.31), channel_id=1, source_target_pairs={{0,2},{1,3},{2,0},{3,1},{4,6},{5,7},{6,4},{7,5},{8,10},{9,11},{10,... | collective-permute-start | bytes 208904 | tf_op jit(solution)/shard_map/ppermute | solution.py:200
  99.4 4.3 %collective-permute-start.17 = (bf16[272,128]{1,0:T(8,128)(2,1)S(1)}, bf16[272,128]{1,0:T(8,128)(2,1)S(1)}, u32[]{:S(2)}, u32[]{:S(2)}) collective-permute-start(bf16[272,128]{1,0:T(8,128)(2,1)S(1)} %get-tuple-element.33), channel_id=1, source_target_pairs={{0,4},{1,5},{2,6},{3,7},{4,0},{5,1},{6,2},{7,3},{8,12},{9,13},{10,... | collective-permute-start | bytes 208904 | tf_op jit(solution)/shard_map/ppermute | solution.py:200
  99.5 5.3 %collective-permute-start.19 = (bf16[272,128]{1,0:T(8,128)(2,1)S(1)}, bf16[272,128]{1,0:T(8,128)(2,1)S(1)}, u32[]{:S(2)}, u32[]{:S(2)}) collective-permute-start(bf16[272,128]{1,0:T(8,128)(2,1)S(1)} %get-tuple-element.35), channel_id=1, source_target_pairs={{0,6},{1,7},{2,4},{3,5},{4,2},{5,3},{6,0},{7,1},{8,14},{9,15},{10,... | collective-permute-start | bytes 208904 | tf_op jit(solution)/shard_map/ppermute | solution.py:200

commit v2 on v1

--- a/solution.py
+++ b/solution.py
@@ -15,6 +15,7 @@
 STAT_TERMS = 4
 CHUNK = 4
 VMEM_LIMIT = 48 * 1024 * 1024
+VMEM_WHOLE = 63 * 1024 * 1024
 
 
 def token_ranks(positions, patch_starts, order_starts):
@@ -28,19 +29,36 @@
 
 
 def split_kernel(members, width, where, queries, *rest):
-    tensors, outs, sems = rest[:4], rest[4:-1], rest[-1]
-    copies = []
-    for step in range(members):
-        start = pl.multiple_of((where[0] ^ step) * width, width)
-        for at, tensor in enumerate(tensors):
-            copies.append((tensor.at[:, pl.ds(start, width)], outs[step].at[at]))
-        copies.append((queries.at[:, pl.ds(start, width)], outs[members + step]))
-    started = [
-        pltpu.make_async_copy(src, dst, sems.at[i]) for i, (src, dst) in enumerate(copies)
+    kinds = 4
+    tensors, outs = rest[:kinds], rest[kinds : kinds + 2 * members]
+    whole_room, key_room, query_room, into, out_of = rest[kinds + 2 * members :]
+    arriving = [
+        pltpu.make_async_copy(src, whole_room.at[i], into.at[i])
+        for i, src in enumerate((queries,) + tensors)
     ]
-    for copy in started:
+    for copy in arriving:
         copy.start()
-    for copy in started:
+    steps = list(range(members))[::-1]
+    columns = {
+        step: pl.ds(pl.multiple_of((where[0] ^ step) * width, width), width) for step in steps
+    }
+    leaving = []
+
+    def send(room, out):
+        leaving.append(pltpu.make_async_copy(room, out, out_of.at[len(leaving)]))
+        leaving[-1].start()
+
+    arriving[0].wait()
+    for step in steps:
+        query_room[step] = whole_room[0, :, columns[step]]
+        send(query_room.at[step], outs[members + step])
+    for copy in arriving[1:]:
+        copy.wait()
+    for step in steps:
+        for kind in range(kinds):
+            key_room[step, kind] = whole_room[1 + kind, :, columns[step]]
+        send(key_room.at[step], outs[step])
+    for copy in leaving:
         copy.wait()
 
 
@@ -50,14 +68,21 @@
     kinds = len(tensors)
     outs = [jax.ShapeDtypeStruct((kinds, rows, width), queries.dtype)] * members
     outs += [jax.ShapeDtypeStruct((rows, width), queries.dtype)] * members
-    anywhere = pl.BlockSpec(memory_space=pl.ANY)
+    anywhere = pl.BlockSpec(memory_space=pltpu.HBM)
     size = (kinds + 1) * rows * columns * 2
     result = pl.pallas_call(
         functools.partial(split_kernel, members, width),
         out_shape=outs,
         in_specs=[pl.BlockSpec(memory_space=pltpu.SMEM)] + [anywhere] * (kinds + 1),
         out_specs=[anywhere] * len(outs),
-        scratch_shapes=[pltpu.SemaphoreType.DMA((members * (kinds + 1),))],
+        scratch_shapes=[
+            pltpu.VMEM((kinds + 1, rows, columns), queries.dtype),
+            pltpu.VMEM((members, kinds, rows, width), queries.dtype),
+            pltpu.VMEM((members, rows, width), queries.dtype),
+            pltpu.SemaphoreType.DMA((kinds + 1,)),
+            pltpu.SemaphoreType.DMA((2 * members,)),
+        ],
+        compiler_params=pltpu.CompilerParams(vmem_limit_bytes=VMEM_WHOLE),
         cost_estimate=pl.CostEstimate(flops=0, bytes_accessed=2 * size, transcendentals=0),
         name="split_columns",
     )(member, queries, *tensors)
@@ -66,48 +91,42 @@
 
 def attend_kernel(sources, blocks, heads, key_rank, query_rank, *refs):
     queries, keys = refs[:sources], refs[sources : sources + blocks]
-    outs, stats = refs[sources + blocks : -1], refs[-1]
-    head = pl.program_id(0)
+    outs = refs[sources + blocks :]
     rows = queries[0].shape[0]
     dims = (((1,), (1,)), ((), ()))
     scale = math.log2(math.e) / math.sqrt(HEAD_DIM)
-    query = jnp.concatenate([ref[...] for ref in queries], axis=0)
-    fresh_keys, fresh_values, stale_keys, stale_values = (
-        jnp.concatenate([ref[kind] for ref in keys], axis=0) for kind in range(4)
-    )
     fresh_ok = key_rank[...] <= query_rank[...]
-    fresh = lax.dot_general(query, fresh_keys, dims, preferred_element_type=jnp.float32)
-    stale = lax.dot_general(query, stale_keys, dims, preferred_element_type=jnp.float32)
-    scores = jnp.where(fresh_ok, fresh, stale)
-    row_max = jnp.max(scores, axis=1, keepdims=True)
-    weights = jnp.exp2((scores - row_max) * scale)
-    total = jnp.sum(weights, axis=1, keepdims=True)
-    fresh_weights = jnp.where(fresh_ok, weights, 0.0).astype(jnp.bfloat16)
-    stale_weights = jnp.where(fresh_ok, 0.0, weights).astype(jnp.bfloat16)
-    mixed = jnp.dot(fresh_weights, fresh_values, preferred_element_type=jnp.float32)
-    mixed = mixed + jnp.dot(stale_weights, stale_values, preferred_element_type=jnp.float32)
-    mixed = (mixed / total).astype(jnp.bfloat16)
-    at = pl.multiple_of(head * rows, rows)
+    lane = lax.broadcasted_iota(jnp.int32, (sources * rows, HEAD_DIM), 1)
+    kept = jnp.zeros((sources * rows, HEAD_DIM), jnp.float32)
+    for head in range(heads):
+        columns = slice(head * HEAD_DIM, (head + 1) * HEAD_DIM)
+        query = jnp.concatenate([ref[:, columns] for ref in queries], axis=0)
+        fresh_keys, fresh_values, stale_keys, stale_values = (
+            jnp.concatenate([ref[kind, :, columns] for ref in keys], axis=0) for kind in range(4)
+        )
+        fresh = lax.dot_general(query, fresh_keys, dims, preferred_element_type=jnp.float32)
+        stale = lax.dot_general(query, stale_keys, dims, preferred_element_type=jnp.float32)
+        scores = jnp.where(fresh_ok, fresh, stale)
+        row_max = jnp.max(scores, axis=1, keepdims=True)
+        weights = jnp.exp2((scores - row_max) * scale)
+        total = jnp.sum(weights, axis=1, keepdims=True)
+        fresh_weights = jnp.where(fresh_ok, weights, 0.0).astype(jnp.bfloat16)
+        stale_weights = jnp.where(fresh_ok, 0.0, weights).astype(jnp.bfloat16)
+        mixed = jnp.dot(fresh_weights, fresh_values, preferred_element_type=jnp.float32)
+        mixed = mixed + jnp.dot(stale_weights, stale_values, preferred_element_type=jnp.float32)
+        mixed = (mixed / total).astype(jnp.bfloat16)
+        for i, out in enumerate(outs):
+            out[head * rows : (head + 1) * rows, :] = mixed[i * rows : (i + 1) * rows]
+        level = row_max * scale + jnp.log2(total)
+        high = level.astype(jnp.bfloat16).astype(jnp.float32)
+        middle = (level - high).astype(jnp.bfloat16).astype(jnp.float32)
+        for term, value in enumerate((high, middle, level - high - middle)):
+            kept = jnp.where(lane == head * STAT_TERMS + term, value, kept)
+    turned = kept.T[:STAT_ROWS]
     for i, out in enumerate(outs):
-        out[pl.ds(at, rows), :] = mixed[i * rows : (i + 1) * rows]
-    level = row_max * scale + jnp.log2(total)
-    high = level.astype(jnp.bfloat16).astype(jnp.float32)
-    middle = (level - high).astype(jnp.bfloat16).astype(jnp.float32)
-    low = level - high - middle
-    lane = lax.broadcasted_iota(jnp.int32, stats.shape, 1) - head * STAT_TERMS
-    kept = jnp.where(head == 0, 0.0, stats[...])
-    kept = jnp.where(lane == 0, high, kept)
-    kept = jnp.where(lane == 1, middle, kept)
-    kept = jnp.where(lane == 2, low, kept)
-    stats[...] = kept
-
-    @pl.when(head == heads - 1)
-    def _():
-        turned = kept.T[:STAT_ROWS]
-        for i, out in enumerate(outs):
-            mine = turned[:, i * rows : (i + 1) * rows].astype(jnp.bfloat16)
-            filler = jnp.zeros((STAT_ROWS, HEAD_DIM - rows), jnp.bfloat16)
-            out[heads * rows :, :] = jnp.concatenate([mine, filler], axis=1)
+        mine = turned[:, i * rows : (i + 1) * rows].astype(jnp.bfloat16)
+        filler = jnp.zeros((STAT_ROWS, HEAD_DIM - rows), jnp.bfloat16)
+        out[heads * rows :, :] = jnp.concatenate([mine, filler], axis=1)
 
 
 def attend(queries, query_rank, keys, key_rank):
@@ -116,17 +135,13 @@
     kinds = keys[0].shape[0]
     heads = width // HEAD_DIM
     query_count, key_count = sources * rows, blocks * rows
-    whole = lambda *shape: pl.BlockSpec(shape, lambda h: (0,) * len(shape))
-    out_rows = heads * rows + STAT_ROWS
+    vmem = pl.BlockSpec(memory_space=pltpu.VMEM)
+    out = jax.ShapeDtypeStruct((heads * rows + STAT_ROWS, HEAD_DIM), jnp.bfloat16)
     return pl.pallas_call(
         functools.partial(attend_kernel, sources, blocks, heads),
-        grid=(heads,),
-        out_shape=[jax.ShapeDtypeStruct((out_rows, HEAD_DIM), jnp.bfloat16)] * sources,
-        in_specs=[whole(1, key_count), whole(query_count, 1)]
-        + [pl.BlockSpec((rows, HEAD_DIM), lambda h: (0, h))] * sources
-        + [pl.BlockSpec((kinds, rows, HEAD_DIM), lambda h: (0, 0, h))] * blocks,
-        out_specs=[whole(out_rows, HEAD_DIM)] * sources,
-        scratch_shapes=[pltpu.VMEM((query_count, HEAD_DIM), jnp.float32)],
+        out_shape=[out] * sources,
+        in_specs=[vmem] * (2 + sources + blocks),
+        out_specs=[vmem] * sources,
         compiler_params=pltpu.CompilerParams(vmem_limit_bytes=VMEM_LIMIT),
         cost_estimate=pl.CostEstimate(
             flops=8 * heads * query_count * key_count * HEAD_DIM,
@@ -181,6 +196,10 @@
     )(member, *flat)
 
 
+def after(array, earlier):
+    return lax.optimization_barrier((array, earlier))[0]
+
+
 def shards(queries, fresh_keys, fresh_values, stale_keys, stale_values, patch_starts, order_starts):
     devices = lax.axis_size("tok")
     rows = queries.shape[0]
@@ -210,11 +229,21 @@
     tensors = (fresh_keys, fresh_values, stale_keys, stale_values)
     key_parts, query_parts = split_columns(where, members, queries, tensors)
     order = list(range(members))[::-1]
+    arrived = {
+        (far, near): hop(query_parts[near], far, near)
+        for far in range(1, groups)
+        for near in order
+    }
+    first_far = [arrived[1, near] for near in order]
     keys = {}
+    for at, near in enumerate(order):
+        part = key_parts[near]
+        if at > 0:
+            part = after(part, first_far[at - 1])
+        keys[near, 0] = hop(part, 0, near)
+        keys[near, 1] = hop(keys[near, 0], 0, 0, 1)
     for near in order:
-        keys[near, 0] = hop(key_parts[near], 0, near)
-    for near in order:
-        keys[near, 1] = hop(keys[near, 0], 0, 0, 1)
+        arrived[0, near] = hop(after(query_parts[near], keys[order[1], 0]), 0, near)
     places = [(near, side) for near in range(members) for side in range(CORES)]
     key_rank = ranks([(0, near, side) for near, side in places])
     key_blocks = [keys[place] for place in places]
@@ -222,9 +251,9 @@
     for far in list(range(groups))[::-1]:
         for first in range(0, members, CHUNK):
             chunk = order[first : first + CHUNK]
-            arrived = [hop(query_parts[near], far, near) for near in chunk]
             query_rank = ranks([(far, near, 0) for near in chunk])
-            results = attend(arrived, query_rank, key_blocks, key_rank)
+            waiting = [arrived[far, near] for near in chunk]
+            results = attend(waiting, query_rank, key_blocks, key_rank)
             for near, result in zip(chunk, results):
                 partials[near][far] = hop(result, far, near)
     return merge(where, partials, rows, heads)

time: 107 us -> 53.9 us (0.50)
  Pallas kernels: 49.6 us -> 8.5 us
  waiting for transfers between devices: 29.5 us -> 16.3 us
  starting transfers between devices: 26.3 us -> 27.8 us
    pallas_call x1, Pallas kernels: 41 us -> 2.38 us  [split_columns(): pl.pallas_call(functools.partial(split_kernel, members, width), out_shape...]
    ppermute x21, waiting for transfers between devices: 29.5 us -> 16.3 us  [hop(): return lax.ppermute(array, 'tok', [(i, i ^ flip) for i in range(devices)])]
    pallas_call x2, Pallas kernels: 6.89 us -> 4.41 us  [attend(): pl.pallas_call(functools.partial(attend_kernel, sources, blocks, heads),...]
    ppermute x21, starting transfers between devices: 26.3 us -> 27.8 us  [hop(): return lax.ppermute(array, 'tok', [(i, i ^ flip) for i in range(devices)])]
  transfers between devices with their start and end apart: 21 -> 21, of which waited for: 7 -> 8; matrix products, arithmetic and copies ran while one was open for 1% -> 2% of each run, Pallas kernels for 6% -> 8%
where the time goes in v2:
time: 53.9 us; the launch traced here: 53.8 us
  starting transfers between devices  27.8 us (52%)
  waiting for transfers between devices  16.3 us (30%)
  Pallas kernels  8.5 us (16%)
  other arithmetic  0.64 us (1%)
    ppermute x21, starting transfers between devices, hop(): return lax.ppermute(array, 'tok', [(i, i ^ flip) for i in range(devices)])  27.8 us
    ppermute x21, waiting for transfers between devices, hop(): return lax.ppermute(array, 'tok', [(i, i ^ flip) for i in range(devices)])  16.3 us
    pallas_call x2, Pallas kernels, attend(): pl.pallas_call(functools.partial(attend_kernel, sources, blocks, heads),...  4.41 us
    pallas_call x1, Pallas kernels, split_columns(): pl.pallas_call(functools.partial(split_kernel, members, width), out_shape...  2.38 us
    pallas_call x1, Pallas kernels, merge(): pl.pallas_call(functools.partial(merge_kernel, parts, members, heads), ou...  1.71 us
  transfers between devices with their start and end apart: 21, of which 8 were waited for; matrix products, arithmetic and copies ran while one was open for 2% of the time, Pallas kernels for 8%

profile of v2, /device:TPU:0, one launch (start us, length us, event | category | flops | bytes accessed | tf_op | source)
XLA Modules:
  0.0 53.8 jit_solution(8443809353887148234)
XLA Ops:
  0.0 2.4 %split_columns.1 = (bf16[4,64,512]{2,1,0:T(8,128)(2,1)}, bf16[4,64,512]{2,1,0:T(8,128)(2,1)}, bf16[4,64,512]{2,1,0:T(8,128)(2,1)}, bf16[4,64,512]{2,1,0:T(8,128)...) custom-call(s32[1]{0:T(128)} %bitcast.where, ...), custom_call_target="tpu_custom_call" | custom-call | bytes 2621440 | tf_op jit(solution)/shard_map/split_columns/pallas_call | solution.py:73
  2.4 5.1 %collective-permute-start.7 = (bf16[64,512]{1,0:T(8,128)(2,1)}, bf16[64,512]{1,0:T(8,128)(2,1)S(1)}, u32[]{:S(2)}, u32[]{:S(2)}) collective-permute-start(bf16[64,512]{1,0:T(8,128)(2,1)} %get-tuple-element.33), channel_id=1, source_target_pairs={{0,12},{1,13},{2,14},{3,15},{4,8},{5,9},{6,10},{7,11},{8,4},{9,5},... | collective-permute-start | bytes 196616 | tf_op jit(solution)/shard_map/ppermute | solution.py:219
  7.5 0.4 collective-permute-start.5
  7.9 2.4 %collective-permute-start = (bf16[64,512]{1,0:T(8,128)(2,1)}, bf16[64,512]{1,0:T(8,128)(2,1)S(1)}, u32[]{:S(2)}, u32[]{:S(2)}) collective-permute-start(bf16[64,512]{1,0:T(8,128)(2,1)} %get-tuple-element.31), channel_id=1, source_target_pairs={{0,14},{1,15},{2,12},{3,13},{4,10},{5,11},{6,8},{7,9},{8,6},{9,7},... | collective-permute-start | bytes 196616 | tf_op jit(solution)/shard_map/ppermute | solution.py:219
  10.3 2.5 %collective-permute-start.11 = (bf16[4,64,512]{2,1,0:T(8,128)(2,1)}, bf16[4,64,512]{2,1,0:T(8,128)(2,1)S(1)}, u32[]{:S(2)}, u32[]{:S(2)}) collective-permute-start(bf16[4,64,512]{2,1,0:T(8,128)(2,1)} %get-tuple-element.42), channel_id=1, source_target_pairs={{0,6},{1,7},{2,4},{3,5},{4,2},{5,3},{6,0},{7,1},{8,14},{9,15},{10,... | collective-permute-start | bytes 786440 | tf_op jit(solution)/shard_map/ppermute | solution.py:219
  12.8 0.3 collective-permute-start.13
  13.5 1.2 %collective-permute-start.8 = (bf16[4,64,512]{2,1,0:T(8,128)(2,1)}, bf16[4,64,512]{2,1,0:T(8,128)(2,1)S(1)}, u32[]{:S(2)}, u32[]{:S(2)}) collective-permute-start(bf16[4,64,512]{2,1,0:T(8,128)(2,1)} %get-tuple-element.41), channel_id=1, source_target_pairs={{0,2},{1,3},{2,0},{3,1},{4,6},{5,7},{6,4},{7,5},{8,10},{9,11},{10,... | collective-permute-start | bytes 786440 | tf_op jit(solution)/shard_map/ppermute | solution.py:219
  14.7 1.1 %collective-permute-done.refs_0_ = bf16[64,512]{1,0:T(8,128)(2,1)S(1)} collective-permute-done((bf16[64,512]{1,0:T(8,128)(2,1)}, bf16[64,512]{1,0:T(8,128)(2,1)S(1)}, u32[]{:S(2)}, u32[]{:S(2)}) %collective-permute-start) | collective-permute-done | bytes 65568 | tf_op jit(solution)/shard_map/ppermute | solution.py:219
  15.8 3.0 %collective-permute-start.1 = (bf16[4,64,512]{2,1,0:T(8,128)(2,1)}, bf16[4,64,512]{2,1,0:T(8,128)(2,1)S(1)}, u32[]{:S(2)}, u32[]{:S(2)}) collective-permute-start(bf16[4,64,512]{2,1,0:T(8,128)(2,1)} %get-tuple-element.30), channel_id=1, source_target_pairs={{0,4},{1,5},{2,6},{3,7},{4,0},{5,1},{6,2},{7,3},{8,12},{9,13},{10,... | collective-permute-start | bytes 786440 | tf_op jit(solution)/shard_map/ppermute | solution.py:219
  18.9 0.1 select_reduce_fusion.1
  19.0 0.1 copy.11.query_rank
  19.2 0.1 convert_reduce_fusion
  19.4 3.3 %collective-permute-done.11.refs_10_ = bf16[4,64,512]{2,1,0:T(8,128)(2,1)S(1)} collective-permute-done((bf16[4,64,512]{2,1,0:T(8,128)(2,1)}, bf16[4,64,512]{2,1,0:T(8,128)(2,1)S(1)}, u32[]{:S(2)}, u32[]{:S(2)}) %collective-permute-start.11) | collective-permute-done | bytes 262176 | tf_op jit(solution)/shard_map/ppermute | solution.py:219
  22.8 4.0 %collective-permute-done.8.refs_6_ = bf16[4,64,512]{2,1,0:T(8,128)(2,1)S(1)} collective-permute-done((bf16[4,64,512]{2,1,0:T(8,128)(2,1)}, bf16[4,64,512]{2,1,0:T(8,128)(2,1)S(1)}, u32[]{:S(2)}, u32[]{:S(2)}) %collective-permute-start.8) | collective-permute-done | bytes 262176 | tf_op jit(solution)/shard_map/ppermute | solution.py:219
  26.8 1.1 %collective-permute-done.1.refs_8_ = bf16[4,64,512]{2,1,0:T(8,128)(2,1)S(1)} collective-permute-done((bf16[4,64,512]{2,1,0:T(8,128)(2,1)}, bf16[4,64,512]{2,1,0:T(8,128)(2,1)S(1)}, u32[]{:S(2)}, u32[]{:S(2)}) %collective-permute-start.1) | collective-permute-done | bytes 262176 | tf_op jit(solution)/shard_map/ppermute | solution.py:219
  27.9 1.0 %collective-permute-start.4 = (bf16[64,512]{1,0:T(8,128)(2,1)}, bf16[64,512]{1,0:T(8,128)(2,1)S(1)}, u32[]{:S(2)}, u32[]{:S(2)}) collective-permute-start(bf16[64,512]{1,0:T(8,128)(2,1)} %get-tuple-element.35), channel_id=1, source_target_pairs={{0,2},{1,3},{2,0},{3,1},{4,6},{5,7},{6,4},{7,5},{8,10},{9,11},{10,... | collective-permute-start | bytes 196616 | tf_op jit(solution)/shard_map/ppermute | solution.py:219
  29.0 0.9 %collective-permute-start.3 = (bf16[64,512]{1,0:T(8,128)(2,1)}, bf16[64,512]{1,0:T(8,128)(2,1)S(1)}, u32[]{:S(2)}, u32[]{:S(2)}) collective-permute-start(bf16[64,512]{1,0:T(8,128)(2,1)} %get-tuple-element.33), channel_id=1, source_target_pairs={{0,4},{1,5},{2,6},{3,7},{4,0},{5,1},{6,2},{7,3},{8,12},{9,13},{10,... | collective-permute-start | bytes 196616 | tf_op jit(solution)/shard_map/ppermute | solution.py:219
  29.9 1.6 %collective-permute-start.2 = (bf16[64,512]{1,0:T(8,128)(2,1)S(1)}, bf16[64,512]{1,0:T(8,128)(2,1)S(1)}, u32[]{:S(2)}, u32[]{:S(2)}) collective-permute-start(bf16[64,512]{1,0:T(8,128)(2,1)S(1)} %copy-done.3), channel_id=1, source_target_pairs={{0,6},{1,7},{2,4},{3,5},{4,2},{5,3},{6,0},{7,1},{8,14},{9,15},{10,... | collective-permute-start | bytes 196616 | tf_op jit(solution)/shard_map/ppermute | solution.py:219
  31.5 2.2 %attend.3 = (bf16[272,128]{1,0:T(8,128)(2,1)S(1)}, bf16[272,128]{1,0:T(8,128)(2,1)S(1)}, bf16[272,128]{1,0:T(8,128)(2,1)S(1)}, bf16[272,128]{1,0:T(8,128)(2,1)S(1)}) custom-call(s32[1,512]{1,0:T(1,128)S(1)} %bitcast.4, s32[256,1]{1,0:T(8,128)S(1)} %copy.11.query_rank, bf16[64,512]{1,0:T(8,128)(2,1)S(1)} %collective-permute-done.refs_0_, ...), custom_call_target="tpu_custom_call" | custom-call | flops 536870912 | bytes 2621440 | tf_op jit(solution)/shard_map/attend/pallas_call | solution.py:140
  33.7 1.1 %collective-permute-start.14 = (bf16[272,128]{1,0:T(8,128)(2,1)S(1)}, bf16[272,128]{1,0:T(8,128)(2,1)S(1)}, u32[]{:S(2)}, u32[]{:S(2)}) collective-permute-start(bf16[272,128]{1,0:T(8,128)(2,1)S(1)} %get-tuple-element.44), channel_id=1, source_target_pairs={{0,8},{1,9},{2,10},{3,11},{4,12},{5,13},{6,14},{7,15},{8,0},{9,1},... | collective-permute-start | bytes 208904 | tf_op jit(solution)/shard_map/ppermute | solution.py:219
  34.8 2.3 %collective-permute-start.16 = (bf16[272,128]{1,0:T(8,128)(2,1)S(1)}, bf16[272,128]{1,0:T(8,128)(2,1)S(1)}, u32[]{:S(2)}, u32[]{:S(2)}) collective-permute-start(bf16[272,128]{1,0:T(8,128)(2,1)S(1)} %get-tuple-element.46), channel_id=1, source_target_pairs={{0,10},{1,11},{2,8},{3,9},{4,14},{5,15},{6,12},{7,13},{8,2},{9,3},... | collective-permute-start | bytes 208904 | tf_op jit(solution)/shard_map/ppermute | solution.py:219
  37.1 0.1 copy.10.query_rank
  37.2 2.1 %collective-permute-start.18 = (bf16[272,128]{1,0:T(8,128)(2,1)S(1)}, bf16[272,128]{1,0:T(8,128)(2,1)S(1)}, u32[]{:S(2)}, u32[]{:S(2)}) collective-permute-start(bf16[272,128]{1,0:T(8,128)(2,1)S(1)} %get-tuple-element.48), channel_id=1, source_target_pairs={{0,12},{1,13},{2,14},{3,15},{4,8},{5,9},{6,10},{7,11},{8,4},{9,5},... | collective-permute-start | bytes 208904 | tf_op jit(solution)/shard_map/ppermute | solution.py:219
  39.3 2.3 %collective-permute-start.20 = (bf16[272,128]{1,0:T(8,128)(2,1)S(1)}, bf16[272,128]{1,0:T(8,128)(2,1)S(1)}, u32[]{:S(2)}, u32[]{:S(2)}) collective-permute-start(bf16[272,128]{1,0:T(8,128)(2,1)S(1)} %get-tuple-element.50), channel_id=1, source_target_pairs={{0,14},{1,15},{2,12},{3,13},{4,10},{5,11},{6,8},{7,9},{8,6},{9,7},... | collective-permute-start | bytes 208904 | tf_op jit(solution)/shard_map/ppermute | solution.py:219
  41.6 2.2 %attend.2 = (bf16[272,128]{1,0:T(8,128)(2,1)S(1)}, bf16[272,128]{1,0:T(8,128)(2,1)S(1)}, bf16[272,128]{1,0:T(8,128)(2,1)S(1)}, bf16[272,128]{1,0:T(8,128)(2,1)S(1)}) custom-call(s32[1,512]{1,0:T(1,128)S(1)} %bitcast.5, s32[256,1]{1,0:T(8,128)S(1)} %copy.10.query_rank, bf16[64,512]{1,0:T(8,128)(2,1)S(1)} %collective-permute-done.2.refs_0_, ...), custom_call_target="tpu_custom_call" | custom-call | flops 536870912 | bytes 2621440 | tf_op jit(solution)/shard_map/attend/pallas_call | solution.py:140
  43.8 1.0 %collective-permute-start.15 = (bf16[272,128]{1,0:T(8,128)(2,1)S(1)}, bf16[272,128]{1,0:T(8,128)(2,1)S(1)}, u32[]{:S(2)}, u32[]{:S(2)}) collective-permute-start(bf16[272,128]{1,0:T(8,128)(2,1)S(1)} %get-tuple-element.45), channel_id=1, source_target_pairs={{0,2},{1,3},{2,0},{3,1},{4,6},{5,7},{6,4},{7,5},{8,10},{9,11},{10,... | collective-permute-start | bytes 208904 | tf_op jit(solution)/shard_map/ppermute | solution.py:219
  44.8 2.1 %collective-permute-done.16.refs_3_ = bf16[272,128]{1,0:T(8,128)(2,1)S(1)} collective-permute-done((bf16[272,128]{1,0:T(8,128)(2,1)S(1)}, bf16[272,128]{1,0:T(8,128)(2,1)S(1)}, u32[]{:S(2)}, u32[]{:S(2)}) %collective-permute-start.16) | collective-permute-done | bytes 69664 | tf_op jit(solution)/shard_map/ppermute | solution.py:219
  46.8 0.5 collective-permute-start.19
  47.3 0.8 %collective-permute-done.15.refs_2_ = bf16[272,128]{1,0:T(8,128)(2,1)S(1)} collective-permute-done((bf16[272,128]{1,0:T(8,128)(2,1)S(1)}, bf16[272,128]{1,0:T(8,128)(2,1)S(1)}, u32[]{:S(2)}, u32[]{:S(2)}) %collective-permute-start.15) | collective-permute-done | bytes 69664 | tf_op jit(solution)/shard_map/ppermute | solution.py:219
  48.1 1.5 %collective-permute-done.17.refs_4_ = bf16[272,128]{1,0:T(8,128)(2,1)S(1)} collective-permute-done((bf16[272,128]{1,0:T(8,128)(2,1)S(1)}, bf16[272,128]{1,0:T(8,128)(2,1)S(1)}, u32[]{:S(2)}, u32[]{:S(2)}) %collective-permute-start.17) | collective-permute-done | bytes 69664 | tf_op jit(solution)/shard_map/ppermute | solution.py:219
  49.6 2.4 %collective-permute-done.19.refs_6_ = bf16[272,128]{1,0:T(8,128)(2,1)S(1)} collective-permute-done((bf16[272,128]{1,0:T(8,128)(2,1)S(1)}, bf16[272,128]{1,0:T(8,128)(2,1)S(1)}, u32[]{:S(2)}, u32[]{:S(2)}) %collective-permute-start.19) | collective-permute-done | bytes 69664 | tf_op jit(solution)/shard_map/ppermute | solution.py:219
  52.0 1.7 %merge.1 = bf16[64,2048]{1,0:T(8,128)(2,1)} custom-call(s32[1]{0:T(128)} %bitcast.where, bf16[272,128]{1,0:T(8,128)(2,1)S(1)} %get-tuple-element.43.refs_0_, bf16[272,128]{1,0:T(8,128)(2,1)S(1)} %collective-permute-done.14.refs_1_, bf16[272,128]{1,0:T(8,128)(2,1)S(1)} %collective-permute-done.15.refs_2_, ...), custom_call_target="tpu_custom_call" | custom-call | tf_op jit(solution)/shard_map/merge/pallas_call | solution.py:189
  (43 shorter events, 0.7 us)
Async XLA Ops:
  0.0 13.4 %copy-start.2 = (s32[16]{0:T(128)S(1)}, s32[16]{0:T(128)}, u32[]{:S(2)}) copy-start(s32[16]{0:T(128)} %param.12) | copy-start | bytes 196
  0.0 18.8 %copy-start.4 = (s32[16]{0:T(128)S(1)}, s32[16]{0:T(128)}, u32[]{:S(2)}) copy-start(s32[16]{0:T(128)} %param.13) | copy-start | bytes 196
  2.4 16.9 %copy-start = (bf16[4,64,512]{2,1,0:T(8,128)(2,1)S(1)}, bf16[4,64,512]{2,1,0:T(8,128)(2,1)}, u32[]{:S(2)}) copy-start(bf16[4,64,512]{2,1,0:T(8,128)(2,1)} %get-tuple-element.39.refs_4_) | copy-start | bytes 786436
  2.4 11.1 %collective-permute-start.7 = (bf16[64,512]{1,0:T(8,128)(2,1)}, bf16[64,512]{1,0:T(8,128)(2,1)S(1)}, u32[]{:S(2)}, u32[]{:S(2)}) collective-permute-start(bf16[64,512]{1,0:T(8,128)(2,1)} %get-tuple-element.33), channel_id=1, source_target_pairs={{0,12},{1,13},{2,14},{3,15},{4,8},{5,9},{6,10},{7,11},{8,4},{9,5},... | collective-permute-start | bytes 196616 | tf_op jit(solution)/shard_map/ppermute | solution.py:219
  7.5 11.8 %collective-permute-start.5 = (bf16[64,512]{1,0:T(8,128)(2,1)}, bf16[64,512]{1,0:T(8,128)(2,1)S(1)}, u32[]{:S(2)}, u32[]{:S(2)}) collective-permute-start(bf16[64,512]{1,0:T(8,128)(2,1)} %get-tuple-element.35), channel_id=1, source_target_pairs={{0,10},{1,11},{2,8},{3,9},{4,14},{5,15},{6,12},{7,13},{8,2},{9,3},... | collective-permute-start | bytes 196616 | tf_op jit(solution)/shard_map/ppermute | solution.py:219
  7.9 7.9 %collective-permute-start = (bf16[64,512]{1,0:T(8,128)(2,1)}, bf16[64,512]{1,0:T(8,128)(2,1)S(1)}, u32[]{:S(2)}, u32[]{:S(2)}) collective-permute-start(bf16[64,512]{1,0:T(8,128)(2,1)} %get-tuple-element.31), channel_id=1, source_target_pairs={{0,14},{1,15},{2,12},{3,13},{4,10},{5,11},{6,8},{7,9},{8,6},{9,7},... | collective-permute-start | bytes 196616 | tf_op jit(solution)/shard_map/ppermute | solution.py:219
  10.3 12.4 %collective-permute-start.11 = (bf16[4,64,512]{2,1,0:T(8,128)(2,1)}, bf16[4,64,512]{2,1,0:T(8,128)(2,1)S(1)}, u32[]{:S(2)}, u32[]{:S(2)}) collective-permute-start(bf16[4,64,512]{2,1,0:T(8,128)(2,1)} %get-tuple-element.42), channel_id=1, source_target_pairs={{0,6},{1,7},{2,4},{3,5},{4,2},{5,3},{6,0},{7,1},{8,14},{9,15},{10,... | collective-permute-start | bytes 786440 | tf_op jit(solution)/shard_map/ppermute | solution.py:219
  12.8 15.1 %collective-permute-start.13 = (bf16[64,512]{1,0:T(8,128)(2,1)}, bf16[64,512]{1,0:T(8,128)(2,1)S(1)}, u32[]{:S(2)}, u32[]{:S(2)}) collective-permute-start(bf16[64,512]{1,0:T(8,128)(2,1)} %get-tuple-element.37.refs_3_), channel_id=1, source_target_pairs={{0,8},{1,9},{2,10},{3,11},{4,12},{5,13},{6,14},{7,15},{8,0},{9,1},... | collective-permute-start | bytes 196616 | tf_op jit(solution)/shard_map/ppermute | solution.py:219
  13.5 13.3 %collective-permute-start.8 = (bf16[4,64,512]{2,1,0:T(8,128)(2,1)}, bf16[4,64,512]{2,1,0:T(8,128)(2,1)S(1)}, u32[]{:S(2)}, u32[]{:S(2)}) collective-permute-start(bf16[4,64,512]{2,1,0:T(8,128)(2,1)} %get-tuple-element.41), channel_id=1, source_target_pairs={{0,2},{1,3},{2,0},{3,1},{4,6},{5,7},{6,4},{7,5},{8,10},{9,11},{10,... | collective-permute-start | bytes 786440 | tf_op jit(solution)/shard_map/ppermute | solution.py:219
  15.8 12.0 %collective-permute-start.1 = (bf16[4,64,512]{2,1,0:T(8,128)(2,1)}, bf16[4,64,512]{2,1,0:T(8,128)(2,1)S(1)}, u32[]{:S(2)}, u32[]{:S(2)}) collective-permute-start(bf16[4,64,512]{2,1,0:T(8,128)(2,1)} %get-tuple-element.30), channel_id=1, source_target_pairs={{0,4},{1,5},{2,6},{3,7},{4,0},{5,1},{6,2},{7,3},{8,12},{9,13},{10,... | collective-permute-start | bytes 786440 | tf_op jit(solution)/shard_map/ppermute | solution.py:219
  19.0 10.8 %copy-start.3 = (bf16[64,512]{1,0:T(8,128)(2,1)S(1)}, bf16[64,512]{1,0:T(8,128)(2,1)}, u32[]{:S(2)}) copy-start(bf16[64,512]{1,0:T(8,128)(2,1)} %get-tuple-element.31) | copy-start | bytes 196612
  19.4 9.6 %collective-permute-start.6 = (bf16[4,64,512]{2,1,0:T(8,128)(2,1)S(1)}, bf16[4,64,512]{2,1,0:T(8,128)(2,1)S(1)}, u32[]{:S(2)}, u32[]{:S(2)}) collective-permute-start(bf16[4,64,512]{2,1,0:T(8,128)(2,1)S(1)} %copy-done), channel_id=1, source_target_pairs={{0,1},{1,0},{2,3},{3,2},{4,5},{5,4},{6,7},{7,6},{8,9},{9,8},{10,11... | collective-permute-start | bytes 786440 | tf_op jit(solution)/shard_map/ppermute | solution.py:219
  22.8 7.1 %collective-permute-start.12 = (bf16[4,64,512]{2,1,0:T(8,128)(2,1)S(1)}, bf16[4,64,512]{2,1,0:T(8,128)(2,1)S(1)}, u32[]{:S(2)}, u32[]{:S(2)}) collective-permute-start(bf16[4,64,512]{2,1,0:T(8,128)(2,1)S(1)} %collective-permute-done.11.refs_10_), channel_id=1, source_target_pairs={{0,1},{1,0},{2,3},{3,2},{4,5},{5,4},{6,7},{7,6},{8,9},{9,8},{10,11... | collective-permute-start | bytes 786440 | tf_op jit(solution)/shard_map/ppermute | solution.py:219
  26.8 4.7 %collective-permute-start.9 = (bf16[4,64,512]{2,1,0:T(8,128)(2,1)S(1)}, bf16[4,64,512]{2,1,0:T(8,128)(2,1)S(1)}, u32[]{:S(2)}, u32[]{:S(2)}) collective-permute-start(bf16[4,64,512]{2,1,0:T(8,128)(2,1)S(1)} %collective-permute-done.8.refs_6_), channel_id=1, source_target_pairs={{0,1},{1,0},{2,3},{3,2},{4,5},{5,4},{6,7},{7,6},{8,9},{9,8},{10,11... | collective-permute-start | bytes 786440 | tf_op jit(solution)/shard_map/ppermute | solution.py:219
  27.8 3.7 %collective-permute-start.10 = (bf16[4,64,512]{2,1,0:T(8,128)(2,1)S(1)}, bf16[4,64,512]{2,1,0:T(8,128)(2,1)S(1)}, u32[]{:S(2)}, u32[]{:S(2)}) collective-permute-start(bf16[4,64,512]{2,1,0:T(8,128)(2,1)S(1)} %collective-permute-done.1.refs_8_), channel_id=1, source_target_pairs={{0,1},{1,0},{2,3},{3,2},{4,5},{5,4},{6,7},{7,6},{8,9},{9,8},{10,11... | collective-permute-start | bytes 786440 | tf_op jit(solution)/shard_map/ppermute | solution.py:219
  27.9 9.3 %collective-permute-start.4 = (bf16[64,512]{1,0:T(8,128)(2,1)}, bf16[64,512]{1,0:T(8,128)(2,1)S(1)}, u32[]{:S(2)}, u32[]{:S(2)}) collective-permute-start(bf16[64,512]{1,0:T(8,128)(2,1)} %get-tuple-element.35), channel_id=1, source_target_pairs={{0,2},{1,3},{2,0},{3,1},{4,6},{5,7},{6,4},{7,5},{8,10},{9,11},{10,... | collective-permute-start | bytes 196616 | tf_op jit(solution)/shard_map/ppermute | solution.py:219
  29.0 10.3 %collective-permute-start.3 = (bf16[64,512]{1,0:T(8,128)(2,1)}, bf16[64,512]{1,0:T(8,128)(2,1)S(1)}, u32[]{:S(2)}, u32[]{:S(2)}) collective-permute-start(bf16[64,512]{1,0:T(8,128)(2,1)} %get-tuple-element.33), channel_id=1, source_target_pairs={{0,4},{1,5},{2,6},{3,7},{4,0},{5,1},{6,2},{7,3},{8,12},{9,13},{10,... | collective-permute-start | bytes 196616 | tf_op jit(solution)/shard_map/ppermute | solution.py:219
  29.9 11.7 %collective-permute-start.2 = (bf16[64,512]{1,0:T(8,128)(2,1)S(1)}, bf16[64,512]{1,0:T(8,128)(2,1)S(1)}, u32[]{:S(2)}, u32[]{:S(2)}) collective-permute-start(bf16[64,512]{1,0:T(8,128)(2,1)S(1)} %copy-done.3), channel_id=1, source_target_pairs={{0,6},{1,7},{2,4},{3,5},{4,2},{5,3},{6,0},{7,1},{8,14},{9,15},{10,... | collective-permute-start | bytes 196616 | tf_op jit(solution)/shard_map/ppermute | solution.py:219
  33.7 11.1 %collective-permute-start.14 = (bf16[272,128]{1,0:T(8,128)(2,1)S(1)}, bf16[272,128]{1,0:T(8,128)(2,1)S(1)}, u32[]{:S(2)}, u32[]{:S(2)}) collective-permute-start(bf16[272,128]{1,0:T(8,128)(2,1)S(1)} %get-tuple-element.44), channel_id=1, source_target_pairs={{0,8},{1,9},{2,10},{3,11},{4,12},{5,13},{6,14},{7,15},{8,0},{9,1},... | collective-permute-start | bytes 208904 | tf_op jit(solution)/shard_map/ppermute | solution.py:219
  34.8 12.0 %collective-permute-start.16 = (bf16[272,128]{1,0:T(8,128)(2,1)S(1)}, bf16[272,128]{1,0:T(8,128)(2,1)S(1)}, u32[]{:S(2)}, u32[]{:S(2)}) collective-permute-start(bf16[272,128]{1,0:T(8,128)(2,1)S(1)} %get-tuple-element.46), channel_id=1, source_target_pairs={{0,10},{1,11},{2,8},{3,9},{4,14},{5,15},{6,12},{7,13},{8,2},{9,3},... | collective-permute-start | bytes 208904 | tf_op jit(solution)/shard_map/ppermute | solution.py:219
  37.0 4.5 %copy-start.1 = (bf16[64,512]{1,0:T(8,128)(2,1)S(1)}, bf16[64,512]{1,0:T(8,128)(2,1)}, u32[]{:S(2)}) copy-start(bf16[64,512]{1,0:T(8,128)(2,1)} %get-tuple-element.37.refs_3_) | copy-start | bytes 196612
  37.2 10.1 %collective-permute-start.18 = (bf16[272,128]{1,0:T(8,128)(2,1)S(1)}, bf16[272,128]{1,0:T(8,128)(2,1)S(1)}, u32[]{:S(2)}, u32[]{:S(2)}) collective-permute-start(bf16[272,128]{1,0:T(8,128)(2,1)S(1)} %get-tuple-element.48), channel_id=1, source_target_pairs={{0,12},{1,13},{2,14},{3,15},{4,8},{5,9},{6,10},{7,11},{8,4},{9,5},... | collective-permute-start | bytes 208904 | tf_op jit(solution)/shard_map/ppermute | solution.py:219
  39.3 8.0 %collective-permute-start.20 = (bf16[272,128]{1,0:T(8,128)(2,1)S(1)}, bf16[272,128]{1,0:T(8,128)(2,1)S(1)}, u32[]{:S(2)}, u32[]{:S(2)}) collective-permute-start(bf16[272,128]{1,0:T(8,128)(2,1)S(1)} %get-tuple-element.50), channel_id=1, source_target_pairs={{0,14},{1,15},{2,12},{3,13},{4,10},{5,11},{6,8},{7,9},{8,6},{9,7},... | collective-permute-start | bytes 208904 | tf_op jit(solution)/shard_map/ppermute | solution.py:219
  43.8 4.3 %collective-permute-start.15 = (bf16[272,128]{1,0:T(8,128)(2,1)S(1)}, bf16[272,128]{1,0:T(8,128)(2,1)S(1)}, u32[]{:S(2)}, u32[]{:S(2)}) collective-permute-start(bf16[272,128]{1,0:T(8,128)(2,1)S(1)} %get-tuple-element.45), channel_id=1, source_target_pairs={{0,2},{1,3},{2,0},{3,1},{4,6},{5,7},{6,4},{7,5},{8,10},{9,11},{10,... | collective-permute-start | bytes 208904 | tf_op jit(solution)/shard_map/ppermute | solution.py:219
  44.8 4.8 %collective-permute-start.17 = (bf16[272,128]{1,0:T(8,128)(2,1)S(1)}, bf16[272,128]{1,0:T(8,128)(2,1)S(1)}, u32[]{:S(2)}, u32[]{:S(2)}) collective-permute-start(bf16[272,128]{1,0:T(8,128)(2,1)S(1)} %get-tuple-element.47), channel_id=1, source_target_pairs={{0,4},{1,5},{2,6},{3,7},{4,0},{5,1},{6,2},{7,3},{8,12},{9,13},{10,... | collective-permute-start | bytes 208904 | tf_op jit(solution)/shard_map/ppermute | solution.py:219
  46.8 5.2 %collective-permute-start.19 = (bf16[272,128]{1,0:T(8,128)(2,1)S(1)}, bf16[272,128]{1,0:T(8,128)(2,1)S(1)}, u32[]{:S(2)}, u32[]{:S(2)}) collective-permute-start(bf16[272,128]{1,0:T(8,128)(2,1)S(1)} %get-tuple-element.49), channel_id=1, source_target_pairs={{0,6},{1,7},{2,4},{3,5},{4,2},{5,3},{6,0},{7,1},{8,14},{9,15},{10,... | collective-permute-start | bytes 208904 | tf_op jit(solution)/shard_map/ppermute | solution.py:219

commit v3 on v2

v3 whole, which is shorter than its diff:
```python
import functools
import math

import jax
import jax.numpy as jnp
from jax import lax
from jax.experimental import pallas as pl
from jax.experimental.pallas import tpu as pltpu
from jax.sharding import PartitionSpec as P

HEADS = 16
HEAD_DIM = 128
CORES = 2
STAT_ROWS = 16
STAT_TERMS = 4
CHUNK = 4
VMEM_LIMIT = 48 * 1024 * 1024
VMEM_WHOLE = 63 * 1024 * 1024


def token_ranks(positions, patch_starts, order_starts):
    patch_count = patch_starts.shape[0]
    slot_ids = jnp.arange(patch_count, dtype=jnp.int32)
    patch_of = jnp.sum((patch_starts[None, :] <= positions[:, None]).astype(jnp.int32), axis=1) - 1
    matches = (order_starts[:, None] == patch_starts[None, :]).astype(jnp.int32)
    rank_of = jnp.sum(matches * slot_ids[:, None], axis=0)
    one_hot = (patch_of[:, None] == slot_ids[None, :]).astype(jnp.int32)
    return jnp.sum(one_hot * rank_of[None, :], axis=1)


def split_kernel(members, width, where, queries, *rest):
    kinds = 4
    tensors, outs = rest[:kinds], rest[kinds : kinds + members + 2]
    whole_room, near_room, far_room, into, out_of = rest[kinds + members + 2 :]
    member, core = where[0] // CORES % members, where[0] % CORES
    arriving = [
        pltpu.make_async_copy(src, whole_room.at[i], into.at[i])
        for i, src in enumerate(tensors + (queries,))
    ]
    for copy in arriving[::-1]:
        copy.start()

    def columns(step):
        return pl.ds(pl.multiple_of((member ^ step) * width, width), width)

    leaving = []

    def send(room, out):
        leaving.append(pltpu.make_async_copy(room, out, out_of.at[len(leaving)]))
        leaving[-1].start()

    arriving[kinds].wait()
    for side in range(CORES)[::-1]:
        for pair in range(members // CORES):
            picked = columns(pair * CORES + (core ^ side))
            far_room[side, pair] = whole_room[kinds, :, picked]
        send(far_room.at[side], outs[members + side])
    for copy in arriving[:kinds]:
        copy.wait()
    for step in range(members)[::-1]:
        for kind in range(kinds + 1):
            near_room[step, kind] = whole_room[kind, :, columns(step)]
        send(near_room.at[step], outs[step])
    for copy in leaving:
        copy.wait()


def split_columns(where, members, queries, tensors):
    rows, columns = queries.shape
    width = columns // members
    kinds = len(tensors) + 1
    near = (kinds, rows, width)
    far = (members // CORES, rows, width)
    anywhere = pl.BlockSpec(memory_space=pl.ANY)
    size = kinds * rows * columns * 2
    result = pl.pallas_call(
        functools.partial(split_kernel, members, width),
        out_shape=[jax.ShapeDtypeStruct(near, queries.dtype)] * members
        + [jax.ShapeDtypeStruct(far, queries.dtype)] * CORES,
        in_specs=[pl.BlockSpec(memory_space=pltpu.SMEM)] + [anywhere] * kinds,
        out_specs=[anywhere] * (members + CORES),
        scratch_shapes=[
            pltpu.VMEM((kinds, rows, columns), queries.dtype),
            pltpu.VMEM((members,) + near, queries.dtype),
            pltpu.VMEM((CORES,) + far, queries.dtype),
            pltpu.SemaphoreType.DMA((kinds,)),
            pltpu.SemaphoreType.DMA((members + CORES,)),
        ],
        compiler_params=pltpu.CompilerParams(vmem_limit_bytes=VMEM_WHOLE),
        cost_estimate=pl.CostEstimate(flops=0, bytes_accessed=2 * size, transcendentals=0),
        name="split_columns",
    )(where, queries, *tensors)
    return result[:members], result[members:]


def attend_kernel(picks, arrays, blocks, heads, key_rank, query_rank, *refs):
    queries = [refs[array].at[at] for array, at in picks]
    keys, outs = refs[arrays : arrays + blocks], refs[arrays + blocks :]
    places = [out.at[at] for out in outs for at in range(out.shape[0])]
    rows = queries[0].shape[0]
    dims = (((1,), (1,)), ((), ()))
    scale = math.log2(math.e) / math.sqrt(HEAD_DIM)
    fresh_ok = key_rank[...] <= query_rank[...]
    lane = lax.broadcasted_iota(jnp.int32, (len(picks) * rows, HEAD_DIM), 1)
    kept = jnp.zeros((len(picks) * rows, HEAD_DIM), jnp.float32)
    for head in range(heads):
        columns = slice(head * HEAD_DIM, (head + 1) * HEAD_DIM)
        query = jnp.concatenate([ref[:, columns] for ref in queries], axis=0)
        fresh_keys, fresh_values, stale_keys, stale_values = (
            jnp.concatenate([ref[kind, :, columns] for ref in keys], axis=0) for kind in range(4)
        )
        fresh = lax.dot_general(query, fresh_keys, dims, preferred_element_type=jnp.float32)
        stale = lax.dot_general(query, stale_keys, dims, preferred_element_type=jnp.float32)
        scores = jnp.where(fresh_ok, fresh, stale)
        row_max = jnp.max(scores, axis=1, keepdims=True)
        weights = jnp.exp2((scores - row_max) * scale)
        total = jnp.sum(weights, axis=1, keepdims=True)
        fresh_weights = jnp.where(fresh_ok, weights, 0.0).astype(jnp.bfloat16)
        stale_weights = jnp.where(fresh_ok, 0.0, weights).astype(jnp.bfloat16)
        mixed = jnp.dot(fresh_weights, fresh_values, preferred_element_type=jnp.float32)
        mixed = mixed + jnp.dot(stale_weights, stale_values, preferred_element_type=jnp.float32)
        mixed = (mixed / total).astype(jnp.bfloat16)
        for i, place in enumerate(places):
            place[head * rows : (head + 1) * rows, :] = mixed[i * rows : (i + 1) * rows]
        level = row_max * scale + jnp.log2(total)
        high = level.astype(jnp.bfloat16).astype(jnp.float32)
        middle = (level - high).astype(jnp.bfloat16).astype(jnp.float32)
        for term, value in enumerate((high, middle, level - high - middle)):
            kept = jnp.where(lane == head * STAT_TERMS + term, value, kept)
    turned = kept.T[:STAT_ROWS]
    for i, place in enumerate(places):
        mine = turned[:, i * rows : (i + 1) * rows].astype(jnp.bfloat16)
        filler = jnp.zeros((STAT_ROWS, HEAD_DIM - rows), jnp.bfloat16)
        place[heads * rows :, :] = jnp.concatenate([mine, filler], axis=1)


def attend(arrays, picks, per_out, query_rank, keys, key_rank):
    blocks = len(keys)
    kinds, rows, width = keys[0].shape
    heads = width // HEAD_DIM
    query_count, key_count = len(picks) * rows, blocks * rows
    vmem = pl.BlockSpec(memory_space=pltpu.VMEM)
    out = jax.ShapeDtypeStruct((per_out, heads * rows + STAT_ROWS, HEAD_DIM), jnp.bfloat16)
    outs = len(picks) // per_out
    return pl.pallas_call(
        functools.partial(attend_kernel, picks, len(arrays), blocks, heads),
        out_shape=[out] * outs,
        in_specs=[vmem] * (2 + len(arrays) + blocks),
        out_specs=[vmem] * outs,
        compiler_params=pltpu.CompilerParams(vmem_limit_bytes=VMEM_LIMIT),
        cost_estimate=pl.CostEstimate(
            flops=8 * heads * query_count * key_count * HEAD_DIM,
            bytes_accessed=2 * width * (query_count * 2 + key_count * kinds),
            transcendentals=heads * query_count * key_count,
        ),
        name="attend",
    )(key_rank[None, :], query_rank[:, None], *arrays, *keys)


def merge_kernel(parts, members, heads, where, *refs):
    out = refs[-1]
    rows = out.shape[0]
    near, far = refs[:members], refs[members:-1]
    member, core = where[0] // CORES % members, where[0] % CORES
    for step in range(members):
        pair, side = step // CORES, step % CORES
        group = [near[pair * CORES].at[0][...]]
        for other in range(1, CORES):
            wanted = (core ^ side) == other
            group[0] = jnp.where(wanted, near[pair * CORES + other].at[0][...], group[0])
        for part in range(parts - 1):
            group.append(far[(part * (members // CORES) + pair) * CORES + side].at[0][...])
        start = (member ^ (pair * CORES + (core ^ side))) * heads * HEAD_DIM
        levels = [one[heads * rows :].astype(jnp.float32).T[:rows] for one in group]
        for head in range(heads):
            lane = head * STAT_TERMS
            level = [
                one[:, lane : lane + 1] + one[:, lane + 1 : lane + 2] + one[:, lane + 2 : lane + 3]
                for one in levels
            ]
            top = functools.reduce(jnp.maximum, level)
            shares = [jnp.exp2(one - top) for one in level]
            total = functools.reduce(jnp.add, shares)
            mixed = functools.reduce(
                jnp.add,
                [
                    one[head * rows : (head + 1) * rows].astype(jnp.float32) * (share / total)
                    for one, share in zip(group, shares)
                ],
            )
            at = pl.multiple_of(start + head * HEAD_DIM, HEAD_DIM)
            out[:, pl.ds(at, HEAD_DIM)] = mixed.astype(out.dtype)


def merge(where, near, far, rows, heads):
    members = len(near)
    pairs = members // CORES
    parts = 1 + len(far) // (pairs * CORES)
    vmem = pl.BlockSpec(memory_space=pltpu.VMEM)
    return pl.pallas_call(
        functools.partial(merge_kernel, parts, members, heads),
        out_shape=jax.ShapeDtypeStruct((rows, members * heads * HEAD_DIM), jnp.bfloat16),
        in_specs=[pl.BlockSpec(memory_space=pltpu.SMEM)] + [vmem] * (len(near) + len(far)),
        out_specs=vmem,
        compiler_params=pltpu.CompilerParams(vmem_limit_bytes=VMEM_LIMIT),
        name="merge",
    )(where, *near, *far)


def after(array, earlier):
    return lax.optimization_barrier((array, earlier))[0]


def shards(queries, fresh_keys, fresh_values, stale_keys, stale_values, patch_starts, order_starts):
    devices = lax.axis_size("tok")
    rows = queries.shape[0]
    chips = devices // CORES
    members = min(chips // 2, HEADS)
    groups = chips // members
    heads = HEADS // members
    me = lax.axis_index("tok")
    core, chip = me % CORES, me // CORES
    group, member = chip // members, chip % members
    where = me[None].astype(jnp.int32)
    pairs = members // CORES

    def hop(array, far, near, side=0):
        flip = (far * members + near) * CORES + side
        if flip == 0:
            return array
        return lax.ppermute(array, "tok", [(i, i ^ flip) for i in range(devices)])

    def far_hop(array, far, pair):
        flips = [(far * members + pair * CORES + i % CORES) * CORES for i in range(devices)]
        return lax.ppermute(array, "tok", [(i, i ^ flips[i]) for i in range(devices)])

    def ranks(places):
        spots = [
            (((group ^ far) * members + (member ^ near)) * CORES + (core ^ side)) * rows
            + jnp.arange(rows, dtype=jnp.int32)
            for far, near, side in places
        ]
        return token_ranks(jnp.concatenate(spots), patch_starts, order_starts)

    tensors = (fresh_keys, fresh_values, stale_keys, stale_values)
    blocks, (mine, others) = split_columns(where, members, queries, tensors)
    order = list(range(members))[::-1]
    other_mine = hop(others, 0, 0, 1)
    arrived = {
        (far, pair): far_hop(jnp.stack([mine[pair], other_mine[pair]]), far, pair)
        for far in range(1, groups)
        for pair in range(pairs)[::-1]
    }
    keys = {}
    keys[0, 0] = blocks[0]
    keys[0, 1] = hop(after(blocks[0], other_mine), 0, 0, 1)
    for near in order[:-1]:
        keys[near, 0] = hop(blocks[near], 0, near)
        block = keys[near, 0]
        for pair in range(pairs):
            block = after(block, arrived[1, pair])
        keys[near, 1] = hop(block, 0, 0, 1)
    key_rank = ranks([(0, near, side) for near in range(members) for side in range(CORES)])
    key_blocks = [keys[near, side] for near in range(members) for side in range(CORES)]
    far_parts, near_parts = [], [None] * members
    for far in range(1, groups):
        for first in range(0, pairs, CHUNK // CORES):
            chunk = list(range(first, min(pairs, first + CHUNK // CORES)))
            query_rank = ranks(
                [(far, pair * CORES + core, side) for pair in chunk for side in range(CORES)]
            )
            waiting = [arrived[far, pair] for pair in chunk]
            picks = [(at, side) for at in range(len(chunk)) for side in range(CORES)]
            results = attend(waiting, picks, CORES, query_rank, key_blocks, key_rank)
            for pair, result in zip(chunk, results):
                back = far_hop(result, far, pair)
                far_parts += [back[:1], hop(back[1:], 0, 0, 1)]
    for first in range(0, members, CHUNK):
        chunk = list(range(first, min(members, first + CHUNK)))
        query_rank = ranks([(0, near, 0) for near in chunk])
        waiting = [keys[near, 0] for near in chunk]
        picks = [(at, len(tensors)) for at in range(len(chunk))]
        results = attend(waiting, picks, 1, query_rank, key_blocks, key_rank)
        for near, result in zip(chunk, results):
            near_parts[near] = hop(result, 0, near)
    return merge(where, near_parts, far_parts, rows, heads)


def solution(mesh):
    placed = (P(("groups", "tok"), None),) * 5 + (P("groups"),) * 2
    return jax.shard_map(
        shards, mesh=mesh, in_specs=placed, out_specs=P(("groups", "tok"), None), check_vma=False
    )
```

time: 53.9 us -> 51.2 us (0.950)
  starting transfers between devices: 27.8 us -> 15.4 us
  waiting for transfers between devices: 16.3 us -> 24.6 us
  local copies, waits for them, and re-layouts: 0.37 us -> 1.63 us
    ppermute x0 -> x4, waiting for transfers between devices: none -> 20.3 us  [far_hop(): lax.ppermute(array, 'tok', [(i, i ^ flips[i]) for i in range(devices)])]
    ppermute x21 -> x13, starting transfers between devices: 27.8 us -> 9.47 us  [hop(): return lax.ppermute(array, 'tok', [(i, i ^ flip) for i in range(devices)])]
    ppermute x21 -> x13, waiting for transfers between devices: 16.3 us -> 4.3 us  [hop(): return lax.ppermute(array, 'tok', [(i, i ^ flip) for i in range(devices)])]
    ppermute x0 -> x4, starting transfers between devices: none -> 5.91 us  [far_hop(): lax.ppermute(array, 'tok', [(i, i ^ flips[i]) for i in range(devices)])]
    unnamed x10 -> x8, local copies, waits for them, and re-layouts: 0.02 us -> 1.23 us
  transfers between devices with their start and end apart: 21 -> 17, of which waited for: 8 -> 8; matrix products, arithmetic and copies ran while one was open for 2% -> 2% of each run, Pallas kernels for 8% -> 4%
where the time goes in v3:
time: 51.2 us; the launch traced here: 51.1 us
  waiting for transfers between devices  24.6 us (48%)
  starting transfers between devices  15.4 us (30%)
  Pallas kernels  8.59 us (17%)
  local copies, waits for them, and re-layouts  1.63 us (3%)
  other arithmetic  0.66 us (1%)
    ppermute x4, waiting for transfers between devices, far_hop(): lax.ppermute(array, 'tok', [(i, i ^ flips[i]) for i in range(devices)])  20.3 us
    ppermute x13, starting transfers between devices, hop(): return lax.ppermute(array, 'tok', [(i, i ^ flip) for i in range(devices)])  9.47 us
    ppermute x4, starting transfers between devices, far_hop(): lax.ppermute(array, 'tok', [(i, i ^ flips[i]) for i in range(devices)])  5.91 us
    pallas_call x2, Pallas kernels, attend(): pl.pallas_call(functools.partial(attend_kernel, picks, len(arrays), block...  4.41 us
    ppermute x13, waiting for transfers between devices, hop(): return lax.ppermute(array, 'tok', [(i, i ^ flip) for i in range(devices)])  4.3 us
    pallas_call x1, Pallas kernels, split_columns(): pl.pallas_call(functools.partial(split_kernel, members, width), out_shape...  2.43 us
    pallas_call x1, Pallas kernels, merge(): pl.pallas_call(functools.partial(merge_kernel, parts, members, heads), ou...  1.75 us
    unnamed x8, local copies, waits for them, and re-layouts  1.23 us
  transfers between devices with their start and end apart: 17, of which 8 were waited for; matrix products, arithmetic and copies ran while one was open for 2% of the time, Pallas kernels for 4%

profile of v3, /device:TPU:0, one launch (start us, length us, event | category | flops | bytes accessed | tf_op | source)
XLA Modules:
  0.0 51.1 jit_solution(11337396258516638274)
XLA Ops:
  0.0 2.4 %split_columns.1 = (bf16[5,64,512]{2,1,0:T(8,128)(2,1)}, bf16[5,64,512]{2,1,0:T(8,128)(2,1)}, bf16[5,64,512]{2,1,0:T(8,128)(2,1)}, bf16[5,64,512]{2,1,0:T(8,128)...) custom-call(s32[1]{0:T(128)} %bitcast.where, bf16[64,2048]{1,0:T(8,128)(2,1)} %queries.1, ...), custom_call_target="tpu_custom_call" | custom-call | bytes 2621440 | tf_op jit(solution)/shard_map/split_columns/pallas_call | solution.py:76
  2.4 0.5 %collective-permute-start.3 = (bf16[2,64,512]{2,1,0:T(8,128)(2,1)}, bf16[2,64,512]{2,1,0:T(8,128)(2,1)S(1)}, u32[]{:S(2)}, u32[]{:S(2)}) collective-permute-start(bf16[2,64,512]{2,1,0:T(8,128)(2,1)} %get-tuple-element.28), channel_id=1, source_target_pairs={{0,1},{1,0},{2,3},{3,2},{4,5},{5,4},{6,7},{7,6},{8,9},{9,8},{10,11... | collective-permute-start | bytes 393224 | tf_op jit(solution)/shard_map/ppermute | solution.py:231
  3.0 3.6 %collective-permute-start.2 = (bf16[5,64,512]{2,1,0:T(8,128)(2,1)}, bf16[5,64,512]{2,1,0:T(8,128)(2,1)S(1)}, u32[]{:S(2)}, u32[]{:S(2)}) collective-permute-start(bf16[5,64,512]{2,1,0:T(8,128)(2,1)} %get-tuple-element.27), channel_id=1, source_target_pairs={{0,6},{1,7},{2,4},{3,5},{4,2},{5,3},{6,0},{7,1},{8,14},{9,15},{10,... | collective-permute-start | bytes 983048 | tf_op jit(solution)/shard_map/ppermute | solution.py:231
  6.5 0.4 collective-permute-start.1
  7.0 0.2 collective-permute-start
  7.4 0.6 %copy-done.2 = s32[16]{0:T(128)S(1)} copy-done((s32[16]{0:T(128)S(1)}, s32[16]{0:T(128)}, u32[]{:S(2)}) %copy-start.2) | copy-done | bytes 88
  8.0 0.1 convert_reduce_fusion.1
  8.1 0.6 %copy-done.3 = s32[16]{0:T(128)S(1)} copy-done((s32[16]{0:T(128)S(1)}, s32[16]{0:T(128)}, u32[]{:S(2)}) %copy-start.3) | copy-done | bytes 88
  8.8 0.1 select_reduce_fusion.3
  8.9 3.0 %collective-permute-start.5 = (bf16[2,64,512]{2,1,0:T(8,128)(2,1)S(1)}, bf16[2,64,512]{2,1,0:T(8,128)(2,1)S(1)}, u32[]{:S(2)}, u32[]{:S(2)}) collective-permute-start(bf16[2,64,512]{2,1,0:T(8,128)(2,1)S(1)} %pad_maximum_fusion), channel_id=1, source_target_pairs={{0,8},{1,11},{2,10},{3,9},{4,12},{5,15},{6,14},{7,13},{8,0},{9,3},... | collective-permute-start | bytes 393224 | tf_op jit(solution)/shard_map/ppermute | solution.py:235
  11.9 1.4 %collective-permute-start.6 = (bf16[2,64,512]{2,1,0:T(8,128)(2,1)S(1)}, bf16[2,64,512]{2,1,0:T(8,128)(2,1)S(1)}, u32[]{:S(2)}, u32[]{:S(2)}) collective-permute-start(bf16[2,64,512]{2,1,0:T(8,128)(2,1)S(1)} %pad_maximum_fusion.1), channel_id=1, source_target_pairs={{0,12},{1,15},{2,14},{3,13},{4,8},{5,11},{6,10},{7,9},{8,4},{9,7},... | collective-permute-start | bytes 393224 | tf_op jit(solution)/shard_map/ppermute | solution.py:235
  13.4 0.1 copy.11.query_rank
  13.6 0.1 convert_reduce_fusion
  13.7 10.9 %collective-permute-done.5.refs_0_ = bf16[2,64,512]{2,1,0:T(8,128)(2,1)S(1)} collective-permute-done((bf16[2,64,512]{2,1,0:T(8,128)(2,1)S(1)}, bf16[2,64,512]{2,1,0:T(8,128)(2,1)S(1)}, u32[]{:S(2)}, u32[]{:S(2)}) %collective-permute-start.5) | collective-permute-done | bytes 131104 | tf_op jit(solution)/shard_map/ppermute | solution.py:235
  24.7 5.3 %collective-permute-done.6.refs_1_ = bf16[2,64,512]{2,1,0:T(8,128)(2,1)S(1)} collective-permute-done((bf16[2,64,512]{2,1,0:T(8,128)(2,1)S(1)}, bf16[2,64,512]{2,1,0:T(8,128)(2,1)S(1)}, u32[]{:S(2)}, u32[]{:S(2)}) %collective-permute-start.6) | collective-permute-done | bytes 131104 | tf_op jit(solution)/shard_map/ppermute | solution.py:235
  30.0 0.5 collective-permute-start.8
  30.5 0.1 select_reduce_fusion
  30.6 0.9 %collective-permute-done.9.refs_11_.refs_9_ = bf16[5,64,512]{2,1,0:T(8,128)(2,1)S(1)} collective-permute-done((bf16[5,64,512]{2,1,0:T(8,128)(2,1)S(1)}, bf16[5,64,512]{2,1,0:T(8,128)(2,1)S(1)}, u32[]{:S(2)}, u32[]{:S(2)}) %collective-permute-start.9) | collective-permute-done | bytes 327712 | tf_op jit(solution)/shard_map/ppermute | solution.py:231
  31.6 0.5 collective-permute-done.8.refs_9_.refs_7_
  32.0 0.5 collective-permute-done.7.refs_7_.refs_5_
  32.5 2.2 %attend.3 = (bf16[2,272,128]{2,1,0:T(8,128)(2,1)S(1)}, bf16[2,272,128]{2,1,0:T(8,128)(2,1)S(1)}) custom-call(s32[1,512]{1,0:T(1,128)S(1)} %bitcast.4, s32[256,1]{1,0:T(8,128)S(1)} %copy.11.query_rank, bf16[2,64,512]{2,1,0:T(8,128)(2,1)S(1)} %collective-permute-done.5.refs_0_, bf16[2,64,512]{2,1,0:T(8,128)(2,1)S(1)} %collective-permute-done.6.refs_1_, ...), custom_call_target="tpu_custom_call" | custom-call | flops 536870912 | bytes 3145728 | tf_op jit(solution)/shard_map/attend/pallas_call | solution.py:145
  34.7 0.1 copy.10.query_rank
  34.9 1.5 %collective-permute-start.15 = (bf16[2,272,128]{2,1,0:T(8,128)(2,1)S(1)}, bf16[2,272,128]{2,1,0:T(8,128)(2,1)S(1)}, u32[]{:S(2)}, u32[]{:S(2)}) collective-permute-start(bf16[2,272,128]{2,1,0:T(8,128)(2,1)S(1)} %get-tuple-element.42), channel_id=1, source_target_pairs={{0,12},{1,15},{2,14},{3,13},{4,8},{5,11},{6,10},{7,9},{8,4},{9,7},... | collective-permute-start | bytes 417800 | tf_op jit(solution)/shard_map/ppermute | solution.py:235
  36.4 2.2 %attend.2 = (bf16[1,272,128]{2,1,0:T(8,128)(2,1)S(1)}, bf16[1,272,128]{2,1,0:T(8,128)(2,1)S(1)}, bf16[1,272,128]{2,1,0:T(8,128)(2,1)S(1)}, bf16[1,272,128]{2,1,0:T(8,128)(2,1)S(1)}) custom-call(s32[1,512]{1,0:T(1,128)S(1)} %bitcast.5, s32[256,1]{1,0:T(8,128)S(1)} %copy.10.query_rank, bf16[5,64,512]{2,1,0:T(8,128)(2,1)S(1)} %copy-done, ...), custom_call_target="tpu_custom_call" | custom-call | flops 536870912 | bytes 3145728 | tf_op jit(solution)/shard_map/attend/pallas_call | solution.py:145
  38.6 0.5 %collective-permute-start.10 = (bf16[1,272,128]{2,1,0:T(8,128)(2,1)S(1)}, bf16[1,272,128]{2,1,0:T(8,128)(2,1)S(1)}, u32[]{:S(2)}, u32[]{:S(2)}) collective-permute-start(bf16[1,272,128]{2,1,0:T(8,128)(2,1)S(1)} %get-tuple-element.38), channel_id=1, source_target_pairs={{0,2},{1,3},{2,0},{3,1},{4,6},{5,7},{6,4},{7,5},{8,10},{9,11},{10,... | collective-permute-start | bytes 208904 | tf_op jit(solution)/shard_map/ppermute | solution.py:231
  39.1 2.0 %collective-permute-start.11 = (bf16[1,272,128]{2,1,0:T(8,128)(2,1)S(1)}, bf16[1,272,128]{2,1,0:T(8,128)(2,1)S(1)}, u32[]{:S(2)}, u32[]{:S(2)}) collective-permute-start(bf16[1,272,128]{2,1,0:T(8,128)(2,1)S(1)} %get-tuple-element.39), channel_id=1, source_target_pairs={{0,4},{1,5},{2,6},{3,7},{4,0},{5,1},{6,2},{7,3},{8,12},{9,13},{10,... | collective-permute-start | bytes 208904 | tf_op jit(solution)/shard_map/ppermute | solution.py:231
  41.2 0.9 %collective-permute-start.12 = (bf16[1,272,128]{2,1,0:T(8,128)(2,1)S(1)}, bf16[1,272,128]{2,1,0:T(8,128)(2,1)S(1)}, u32[]{:S(2)}, u32[]{:S(2)}) collective-permute-start(bf16[1,272,128]{2,1,0:T(8,128)(2,1)S(1)} %get-tuple-element.40), channel_id=1, source_target_pairs={{0,6},{1,7},{2,4},{3,5},{4,2},{5,3},{6,0},{7,1},{8,14},{9,15},{10,... | collective-permute-start | bytes 208904 | tf_op jit(solution)/shard_map/ppermute | solution.py:231
  42.1 4.1 %collective-permute-done.13 = bf16[2,272,128]{2,1,0:T(8,128)(2,1)S(1)} collective-permute-done((bf16[2,272,128]{2,1,0:T(8,128)(2,1)S(1)}, bf16[2,272,128]{2,1,0:T(8,128)(2,1)S(1)}, u32[]{:S(2)}, u32[]{:S(2)}) %collective-permute-start.13) | collective-permute-done | bytes 139296 | tf_op jit(solution)/shard_map/ppermute | solution.py:235
  46.4 0.5 %collective-permute-start.16 = (bf16[1,272,128]{2,1,0:T(8,128)(2,1)S(1)}, bf16[1,272,128]{2,1,0:T(8,128)(2,1)S(1)}, u32[]{:S(2)}, u32[]{:S(2)}) collective-permute-start(bf16[1,272,128]{2,1,0:T(8,128)(2,1)S(1)} %get-tuple-element.47), channel_id=1, source_target_pairs={{0,1},{1,0},{2,3},{3,2},{4,5},{5,4},{6,7},{7,6},{8,9},{9,8},{10,11... | collective-permute-start | bytes 208904 | tf_op jit(solution)/shard_map/ppermute | solution.py:231
  46.9 0.7 %collective-permute-done.11.refs_2_ = bf16[1,272,128]{2,1,0:T(8,128)(2,1)S(1)} collective-permute-done((bf16[1,272,128]{2,1,0:T(8,128)(2,1)S(1)}, bf16[1,272,128]{2,1,0:T(8,128)(2,1)S(1)}, u32[]{:S(2)}, u32[]{:S(2)}) %collective-permute-start.11) | collective-permute-done | bytes 69664 | tf_op jit(solution)/shard_map/ppermute | solution.py:231
  47.6 1.7 %collective-permute-done.12.refs_3_ = bf16[1,272,128]{2,1,0:T(8,128)(2,1)S(1)} collective-permute-done((bf16[1,272,128]{2,1,0:T(8,128)(2,1)S(1)}, bf16[1,272,128]{2,1,0:T(8,128)(2,1)S(1)}, u32[]{:S(2)}, u32[]{:S(2)}) %collective-permute-start.12) | collective-permute-done | bytes 69664 | tf_op jit(solution)/shard_map/ppermute | solution.py:231
  49.3 1.7 %merge.1 = bf16[64,2048]{1,0:T(8,128)(2,1)} custom-call(s32[1]{0:T(128)} %bitcast.where, bf16[1,272,128]{2,1,0:T(8,128)(2,1)S(1)} %get-tuple-element.37.refs_0_, bf16[1,272,128]{2,1,0:T(8,128)(2,1)S(1)} %collective-permute-done.10.refs_1_, bf16[1,272,128]{2,1,0:T(8,128)(2,1)S(1)} %collective-permute-done.11.refs_2_, ...), custom_call_target="tpu_custom_call" | custom-call | tf_op jit(solution)/shard_map/merge/pallas_call | solution.py:200
  (39 shorter events, 0.6 us)
Async XLA Ops:
  2.4 5.6 %copy-start.1 = (bf16[2,64,512]{2,1,0:T(8,128)(2,1)S(1)}, bf16[2,64,512]{2,1,0:T(8,128)(2,1)}, u32[]{:S(2)}) copy-start(bf16[2,64,512]{2,1,0:T(8,128)(2,1)} %get-tuple-element.30) | copy-start | bytes 393220
  2.4 6.4 %collective-permute-start.3 = (bf16[2,64,512]{2,1,0:T(8,128)(2,1)}, bf16[2,64,512]{2,1,0:T(8,128)(2,1)S(1)}, u32[]{:S(2)}, u32[]{:S(2)}) collective-permute-start(bf16[2,64,512]{2,1,0:T(8,128)(2,1)} %get-tuple-element.28), channel_id=1, source_target_pairs={{0,1},{1,0},{2,3},{3,2},{4,5},{5,4},{6,7},{7,6},{8,9},{9,8},{10,11... | collective-permute-start | bytes 393224 | tf_op jit(solution)/shard_map/ppermute | solution.py:231
  3.0 21.7 %collective-permute-start.2 = (bf16[5,64,512]{2,1,0:T(8,128)(2,1)}, bf16[5,64,512]{2,1,0:T(8,128)(2,1)S(1)}, u32[]{:S(2)}, u32[]{:S(2)}) collective-permute-start(bf16[5,64,512]{2,1,0:T(8,128)(2,1)} %get-tuple-element.27), channel_id=1, source_target_pairs={{0,6},{1,7},{2,4},{3,5},{4,2},{5,3},{6,0},{7,1},{8,14},{9,15},{10,... | collective-permute-start | bytes 983048 | tf_op jit(solution)/shard_map/ppermute | solution.py:231
  6.5 23.4 %collective-permute-start.1 = (bf16[5,64,512]{2,1,0:T(8,128)(2,1)}, bf16[5,64,512]{2,1,0:T(8,128)(2,1)S(1)}, u32[]{:S(2)}, u32[]{:S(2)}) collective-permute-start(bf16[5,64,512]{2,1,0:T(8,128)(2,1)} %get-tuple-element.26), channel_id=1, source_target_pairs={{0,4},{1,5},{2,6},{3,7},{4,0},{5,1},{6,2},{7,3},{8,12},{9,13},{10,... | collective-permute-start | bytes 983048 | tf_op jit(solution)/shard_map/ppermute | solution.py:231
  7.0 23.5 %collective-permute-start = (bf16[5,64,512]{2,1,0:T(8,128)(2,1)}, bf16[5,64,512]{2,1,0:T(8,128)(2,1)S(1)}, u32[]{:S(2)}, u32[]{:S(2)}) collective-permute-start(bf16[5,64,512]{2,1,0:T(8,128)(2,1)} %get-tuple-element.25), channel_id=1, source_target_pairs={{0,2},{1,3},{2,0},{3,1},{4,6},{5,7},{6,4},{7,5},{8,10},{9,11},{10,... | collective-permute-start | bytes 983048 | tf_op jit(solution)/shard_map/ppermute | solution.py:231
  7.3 0.7 %copy-start.2 = (s32[16]{0:T(128)S(1)}, s32[16]{0:T(128)}, u32[]{:S(2)}) copy-start(s32[16]{0:T(128)} %param.12) | copy-start | bytes 196
  8.1 0.7 %copy-start.3 = (s32[16]{0:T(128)S(1)}, s32[16]{0:T(128)}, u32[]{:S(2)}) copy-start(s32[16]{0:T(128)} %param.13) | copy-start | bytes 196
  8.9 15.8 %copy-start = (bf16[5,64,512]{2,1,0:T(8,128)(2,1)S(1)}, bf16[5,64,512]{2,1,0:T(8,128)(2,1)}, u32[]{:S(2)}) copy-start(bf16[5,64,512]{2,1,0:T(8,128)(2,1)} %get-tuple-element.29.refs_0_.refs_4_.refs_2_) | copy-start | bytes 983044
  8.9 15.7 %collective-permute-start.5 = (bf16[2,64,512]{2,1,0:T(8,128)(2,1)S(1)}, bf16[2,64,512]{2,1,0:T(8,128)(2,1)S(1)}, u32[]{:S(2)}, u32[]{:S(2)}) collective-permute-start(bf16[2,64,512]{2,1,0:T(8,128)(2,1)S(1)} %pad_maximum_fusion), channel_id=1, source_target_pairs={{0,8},{1,11},{2,10},{3,9},{4,12},{5,15},{6,14},{7,13},{8,0},{9,3},... | collective-permute-start | bytes 393224 | tf_op jit(solution)/shard_map/ppermute | solution.py:235
  11.9 18.0 %collective-permute-start.6 = (bf16[2,64,512]{2,1,0:T(8,128)(2,1)S(1)}, bf16[2,64,512]{2,1,0:T(8,128)(2,1)S(1)}, u32[]{:S(2)}, u32[]{:S(2)}) collective-permute-start(bf16[2,64,512]{2,1,0:T(8,128)(2,1)S(1)} %pad_maximum_fusion.1), channel_id=1, source_target_pairs={{0,12},{1,15},{2,14},{3,13},{4,8},{5,11},{6,10},{7,9},{8,4},{9,7},... | collective-permute-start | bytes 393224 | tf_op jit(solution)/shard_map/ppermute | solution.py:235
  24.7 6.0 %collective-permute-start.4 = (bf16[5,64,512]{2,1,0:T(8,128)(2,1)S(1)}, bf16[5,64,512]{2,1,0:T(8,128)(2,1)S(1)}, u32[]{:S(2)}, u32[]{:S(2)}) collective-permute-start(bf16[5,64,512]{2,1,0:T(8,128)(2,1)S(1)} %copy-done), channel_id=1, source_target_pairs={{0,1},{1,0},{2,3},{3,2},{4,5},{5,4},{6,7},{7,6},{8,9},{9,8},{10,11... | collective-permute-start | bytes 983048 | tf_op jit(solution)/shard_map/ppermute | solution.py:231
  29.9 1.6 %collective-permute-start.9 = (bf16[5,64,512]{2,1,0:T(8,128)(2,1)S(1)}, bf16[5,64,512]{2,1,0:T(8,128)(2,1)S(1)}, u32[]{:S(2)}, u32[]{:S(2)}) collective-permute-start(bf16[5,64,512]{2,1,0:T(8,128)(2,1)S(1)} %collective-permute-done.2.refs_3_.refs_10_.refs_8_), channel_id=1, source_target_pairs={{0,1},{1,0},{2,3},{3,2},{4,5},{5,4},{6,7},{7,6},{8,9},{9,8},{10,11... | collective-permute-start | bytes 983048 | tf_op jit(solution)/shard_map/ppermute | solution.py:231
  30.0 2.1 %collective-permute-start.8 = (bf16[5,64,512]{2,1,0:T(8,128)(2,1)S(1)}, bf16[5,64,512]{2,1,0:T(8,128)(2,1)S(1)}, u32[]{:S(2)}, u32[]{:S(2)}) collective-permute-start(bf16[5,64,512]{2,1,0:T(8,128)(2,1)S(1)} %collective-permute-done.1.refs_2_.refs_8_.refs_6_), channel_id=1, source_target_pairs={{0,1},{1,0},{2,3},{3,2},{4,5},{5,4},{6,7},{7,6},{8,9},{9,8},{10,11... | collective-permute-start | bytes 983048 | tf_op jit(solution)/shard_map/ppermute | solution.py:231
  30.5 2.0 %collective-permute-start.7 = (bf16[5,64,512]{2,1,0:T(8,128)(2,1)S(1)}, bf16[5,64,512]{2,1,0:T(8,128)(2,1)S(1)}, u32[]{:S(2)}, u32[]{:S(2)}) collective-permute-start(bf16[5,64,512]{2,1,0:T(8,128)(2,1)S(1)} %collective-permute-done.refs_1_.refs_6_.refs_4_), channel_id=1, source_target_pairs={{0,1},{1,0},{2,3},{3,2},{4,5},{5,4},{6,7},{7,6},{8,9},{9,8},{10,11... | collective-permute-start | bytes 983048 | tf_op jit(solution)/shard_map/ppermute | solution.py:231
  34.7 11.5 %collective-permute-start.13 = (bf16[2,272,128]{2,1,0:T(8,128)(2,1)S(1)}, bf16[2,272,128]{2,1,0:T(8,128)(2,1)S(1)}, u32[]{:S(2)}, u32[]{:S(2)}) collective-permute-start(bf16[2,272,128]{2,1,0:T(8,128)(2,1)S(1)} %get-tuple-element.41), channel_id=1, source_target_pairs={{0,8},{1,11},{2,10},{3,9},{4,12},{5,15},{6,14},{7,13},{8,0},{9,3},... | collective-permute-start | bytes 417800 | tf_op jit(solution)/shard_map/ppermute | solution.py:235
  34.9 11.5 %collective-permute-start.15 = (bf16[2,272,128]{2,1,0:T(8,128)(2,1)S(1)}, bf16[2,272,128]{2,1,0:T(8,128)(2,1)S(1)}, u32[]{:S(2)}, u32[]{:S(2)}) collective-permute-start(bf16[2,272,128]{2,1,0:T(8,128)(2,1)S(1)} %get-tuple-element.42), channel_id=1, source_target_pairs={{0,12},{1,15},{2,14},{3,13},{4,8},{5,11},{6,10},{7,9},{8,4},{9,7},... | collective-permute-start | bytes 417800 | tf_op jit(solution)/shard_map/ppermute | solution.py:235
  38.6 8.3 %collective-permute-start.10 = (bf16[1,272,128]{2,1,0:T(8,128)(2,1)S(1)}, bf16[1,272,128]{2,1,0:T(8,128)(2,1)S(1)}, u32[]{:S(2)}, u32[]{:S(2)}) collective-permute-start(bf16[1,272,128]{2,1,0:T(8,128)(2,1)S(1)} %get-tuple-element.38), channel_id=1, source_target_pairs={{0,2},{1,3},{2,0},{3,1},{4,6},{5,7},{6,4},{7,5},{8,10},{9,11},{10,... | collective-permute-start | bytes 208904 | tf_op jit(solution)/shard_map/ppermute | solution.py:231
  39.1 8.5 %collective-permute-start.11 = (bf16[1,272,128]{2,1,0:T(8,128)(2,1)S(1)}, bf16[1,272,128]{2,1,0:T(8,128)(2,1)S(1)}, u32[]{:S(2)}, u32[]{:S(2)}) collective-permute-start(bf16[1,272,128]{2,1,0:T(8,128)(2,1)S(1)} %get-tuple-element.39), channel_id=1, source_target_pairs={{0,4},{1,5},{2,6},{3,7},{4,0},{5,1},{6,2},{7,3},{8,12},{9,13},{10,... | collective-permute-start | bytes 208904 | tf_op jit(solution)/shard_map/ppermute | solution.py:231
  41.2 8.1 %collective-permute-start.12 = (bf16[1,272,128]{2,1,0:T(8,128)(2,1)S(1)}, bf16[1,272,128]{2,1,0:T(8,128)(2,1)S(1)}, u32[]{:S(2)}, u32[]{:S(2)}) collective-permute-start(bf16[1,272,128]{2,1,0:T(8,128)(2,1)S(1)} %get-tuple-element.40), channel_id=1, source_target_pairs={{0,6},{1,7},{2,4},{3,5},{4,2},{5,3},{6,0},{7,1},{8,14},{9,15},{10,... | collective-permute-start | bytes 208904 | tf_op jit(solution)/shard_map/ppermute | solution.py:231
  46.2 3.1 %collective-permute-start.14 = (bf16[1,272,128]{2,1,0:T(8,128)(2,1)S(1)}, bf16[1,272,128]{2,1,0:T(8,128)(2,1)S(1)}, u32[]{:S(2)}, u32[]{:S(2)}) collective-permute-start(bf16[1,272,128]{2,1,0:T(8,128)(2,1)S(1)} %get-tuple-element.49), channel_id=1, source_target_pairs={{0,1},{1,0},{2,3},{3,2},{4,5},{5,4},{6,7},{7,6},{8,9},{9,8},{10,11... | collective-permute-start | bytes 208904 | tf_op jit(solution)/shard_map/ppermute | solution.py:231
  46.4 3.0 %collective-permute-start.16 = (bf16[1,272,128]{2,1,0:T(8,128)(2,1)S(1)}, bf16[1,272,128]{2,1,0:T(8,128)(2,1)S(1)}, u32[]{:S(2)}, u32[]{:S(2)}) collective-permute-start(bf16[1,272,128]{2,1,0:T(8,128)(2,1)S(1)} %get-tuple-element.47), channel_id=1, source_target_pairs={{0,1},{1,0},{2,3},{3,2},{4,5},{5,4},{6,7},{7,6},{8,9},{9,8},{10,11... | collective-permute-start | bytes 208904 | tf_op jit(solution)/shard_map/ppermute | solution.py:231

commit v4 on v3

--- a/solution.py
+++ b/solution.py
@@ -240,7 +240,7 @@
             + jnp.arange(rows, dtype=jnp.int32)
             for far, near, side in places
         ]
-        return token_ranks(jnp.concatenate(spots), patch_starts, order_starts)
+        return token_ranks(jnp.concatenate(spots), starts_later, order_starts)
 
     tensors = (fresh_keys, fresh_values, stale_keys, stale_values)
     blocks, (mine, others) = split_columns(where, members, queries, tensors)
@@ -257,9 +257,9 @@
     for near in order[:-1]:
         keys[near, 0] = hop(blocks[near], 0, near)
         block = keys[near, 0]
-        for pair in range(pairs):
-            block = after(block, arrived[1, pair])
+        block = after(block, arrived[1, 0])
         keys[near, 1] = hop(block, 0, 0, 1)
+    starts_later = after(patch_starts, keys[order[0], 0])
     key_rank = ranks([(0, near, side) for near in range(members) for side in range(CORES)])
     key_blocks = [keys[near, side] for near in range(members) for side in range(CORES)]
     far_parts, near_parts = [], [None] * members

time: 51.2 us -> 48.5 us (0.947)
  waiting for transfers between devices: 24.6 us -> 17.4 us
  starting transfers between devices: 15.4 us -> 20.5 us
  local copies, waits for them, and re-layouts: 1.63 us -> 0.9 us
    ppermute x4, waiting for transfers between devices: 20.3 us -> 8.85 us  [far_hop(): lax.ppermute(array, 'tok', [(i, i ^ flips[i]) for i in range(devices)])]
    ppermute x4, starting transfers between devices: 5.91 us -> 10.6 us  [far_hop(): lax.ppermute(array, 'tok', [(i, i ^ flips[i]) for i in range(devices)])]
    ppermute x13, waiting for transfers between devices: 4.3 us -> 8.54 us  [hop(): return lax.ppermute(array, 'tok', [(i, i ^ flip) for i in range(devices)])]
    unnamed x8, local copies, waits for them, and re-layouts: 1.23 us -> 0.52 us
  transfers between devices with their start and end apart: 17 -> 17, of which waited for: 8 -> 6; matrix products, arithmetic and copies ran while one was open for 2% -> 2% of each run, Pallas kernels for 4% -> 5%
where the time goes in v4:
time: 48.5 us; the launch traced here: 48.2 us
  starting transfers between devices  20.5 us (42%)
  waiting for transfers between devices  17.4 us (36%)
  Pallas kernels  8.59 us (18%)
  local copies, waits for them, and re-layouts  0.9 us (2%)
  other arithmetic  0.67 us (1%)
    ppermute x4, starting transfers between devices, far_hop(): lax.ppermute(array, 'tok', [(i, i ^ flips[i]) for i in range(devices)])  10.6 us
    ppermute x13, starting transfers between devices, hop(): return lax.ppermute(array, 'tok', [(i, i ^ flip) for i in range(devices)])  9.86 us
    ppermute x4, waiting for transfers between devices, far_hop(): lax.ppermute(array, 'tok', [(i, i ^ flips[i]) for i in range(devices)])  8.85 us
    ppermute x13, waiting for transfers between devices, hop(): return lax.ppermute(array, 'tok', [(i, i ^ flip) for i in range(devices)])  8.54 us
    pallas_call x2, Pallas kernels, attend(): pl.pallas_call(functools.partial(attend_kernel, picks, len(arrays), block...  4.42 us
    pallas_call x1, Pallas kernels, split_columns(): pl.pallas_call(functools.partial(split_kernel, members, width), out_shape...  2.43 us
    pallas_call x1, Pallas kernels, merge(): pl.pallas_call(functools.partial(merge_kernel, parts, members, heads), ou...  1.75 us
  transfers between devices with their start and end apart: 17, of which 6 were waited for; matrix products, arithmetic and copies ran while one was open for 2% of the time, Pallas kernels for 5%

profile of v4, /device:TPU:0, one launch (start us, length us, event | category | flops | bytes accessed | tf_op | source)
XLA Modules:
  0.0 48.2 jit_solution(2562968460458323621)
XLA Ops:
  0.0 2.4 %split_columns.1 = (bf16[5,64,512]{2,1,0:T(8,128)(2,1)}, bf16[5,64,512]{2,1,0:T(8,128)(2,1)}, bf16[5,64,512]{2,1,0:T(8,128)(2,1)}, bf16[5,64,512]{2,1,0:T(8,128)...) custom-call(s32[1]{0:T(128)} %bitcast.where, bf16[64,2048]{1,0:T(8,128)(2,1)} %queries.1, ...), custom_call_target="tpu_custom_call" | custom-call | bytes 2621440 | tf_op jit(solution)/shard_map/split_columns/pallas_call | solution.py:76
  2.4 4.0 %collective-permute-start = (bf16[5,64,512]{2,1,0:T(8,128)(2,1)}, bf16[5,64,512]{2,1,0:T(8,128)(2,1)S(1)}, u32[]{:S(2)}, u32[]{:S(2)}) collective-permute-start(bf16[5,64,512]{2,1,0:T(8,128)(2,1)} %get-tuple-element.22), channel_id=1, source_target_pairs={{0,6},{1,7},{2,4},{3,5},{4,2},{5,3},{6,0},{7,1},{8,14},{9,15},{10,... | collective-permute-start | bytes 983048 | tf_op jit(solution)/shard_map/ppermute | solution.py:231
  6.5 0.4 collective-permute-start.2
  6.9 0.3 collective-permute-start.1
  7.5 0.5 %collective-permute-done.3 = bf16[2,64,512]{2,1,0:T(8,128)(2,1)S(1)} collective-permute-done((bf16[2,64,512]{2,1,0:T(8,128)(2,1)}, bf16[2,64,512]{2,1,0:T(8,128)(2,1)S(1)}, u32[]{:S(2)}, u32[]{:S(2)}) %collective-permute-start.3) | collective-permute-done | bytes 131104 | tf_op jit(solution)/shard_map/ppermute | solution.py:231
  8.1 2.7 %collective-permute-start.5 = (bf16[2,64,512]{2,1,0:T(8,128)(2,1)S(1)}, bf16[2,64,512]{2,1,0:T(8,128)(2,1)S(1)}, u32[]{:S(2)}, u32[]{:S(2)}) collective-permute-start(bf16[2,64,512]{2,1,0:T(8,128)(2,1)S(1)} %pad_maximum_fusion), channel_id=1, source_target_pairs={{0,8},{1,11},{2,10},{3,9},{4,12},{5,15},{6,14},{7,13},{8,0},{9,3},... | collective-permute-start | bytes 393224 | tf_op jit(solution)/shard_map/ppermute | solution.py:235
  10.7 0.4 collective-permute-start.4
  11.1 7.0 %collective-permute-done.refs_3_.refs_10_.refs_8_ = bf16[5,64,512]{2,1,0:T(8,128)(2,1)S(1)} collective-permute-done((bf16[5,64,512]{2,1,0:T(8,128)(2,1)}, bf16[5,64,512]{2,1,0:T(8,128)(2,1)S(1)}, u32[]{:S(2)}, u32[]{:S(2)}) %collective-permute-start) | collective-permute-done | bytes 327712 | tf_op jit(solution)/shard_map/ppermute | solution.py:231
  18.1 4.1 %collective-permute-start.12 = (bf16[2,64,512]{2,1,0:T(8,128)(2,1)S(1)}, bf16[2,64,512]{2,1,0:T(8,128)(2,1)S(1)}, u32[]{:S(2)}, u32[]{:S(2)}) collective-permute-start(bf16[2,64,512]{2,1,0:T(8,128)(2,1)S(1)} %pad_maximum_fusion.1), channel_id=1, source_target_pairs={{0,12},{1,15},{2,14},{3,13},{4,8},{5,11},{6,10},{7,9},{8,4},{9,7},... | collective-permute-start | bytes 393224 | tf_op jit(solution)/shard_map/ppermute | solution.py:235
  22.2 0.1 convert_reduce_fusion.1
  22.3 2.4 %collective-permute-done.5.refs_0_ = bf16[2,64,512]{2,1,0:T(8,128)(2,1)S(1)} collective-permute-done((bf16[2,64,512]{2,1,0:T(8,128)(2,1)S(1)}, bf16[2,64,512]{2,1,0:T(8,128)(2,1)S(1)}, u32[]{:S(2)}, u32[]{:S(2)}) %collective-permute-start.5) | collective-permute-done | bytes 131104 | tf_op jit(solution)/shard_map/ppermute | solution.py:235
  24.7 0.5 %collective-permute-start.7 = (bf16[5,64,512]{2,1,0:T(8,128)(2,1)S(1)}, bf16[5,64,512]{2,1,0:T(8,128)(2,1)S(1)}, u32[]{:S(2)}, u32[]{:S(2)}) collective-permute-start(bf16[5,64,512]{2,1,0:T(8,128)(2,1)S(1)} %collective-permute-done.2.refs_2_.refs_8_.refs_6_), channel_id=1, source_target_pairs={{0,1},{1,0},{2,3},{3,2},{4,5},{5,4},{6,7},{7,6},{8,9},{9,8},{10,11... | collective-permute-start | bytes 983048 | tf_op jit(solution)/shard_map/ppermute | solution.py:231
  25.2 0.1 convert_reduce_fusion
  25.3 0.1 collective-permute-start.6
  25.5 0.5 %copy-done.3 = s32[16]{0:T(128)S(1)} copy-done((s32[16]{0:T(128)S(1)}, s32[16]{0:T(128)}, u32[]{:S(2)}) %copy-start.3) | copy-done | bytes 88
  26.0 0.1 select_reduce_fusion.3
  26.1 0.1 select_reduce_fusion.1
  26.1 0.1 copy.11.query_rank
  26.3 0.1 select_reduce_fusion
  26.4 2.9 %collective-permute-done.12.refs_1_ = bf16[2,64,512]{2,1,0:T(8,128)(2,1)S(1)} collective-permute-done((bf16[2,64,512]{2,1,0:T(8,128)(2,1)S(1)}, bf16[2,64,512]{2,1,0:T(8,128)(2,1)S(1)}, u32[]{:S(2)}, u32[]{:S(2)}) %collective-permute-start.12) | collective-permute-done | bytes 131104 | tf_op jit(solution)/shard_map/ppermute | solution.py:235
  29.3 2.2 %attend.3 = (bf16[2,272,128]{2,1,0:T(8,128)(2,1)S(1)}, bf16[2,272,128]{2,1,0:T(8,128)(2,1)S(1)}) custom-call(s32[1,512]{1,0:T(1,128)S(1)} %bitcast.4, s32[256,1]{1,0:T(8,128)S(1)} %copy.11.query_rank, bf16[2,64,512]{2,1,0:T(8,128)(2,1)S(1)} %collective-permute-done.5.refs_0_, bf16[2,64,512]{2,1,0:T(8,128)(2,1)S(1)} %collective-permute-done.12.refs_1_, ...), custom_call_target="tpu_custom_call" | custom-call | flops 536870912 | bytes 3145728 | tf_op jit(solution)/shard_map/attend/pallas_call | solution.py:145
  31.5 1.4 %collective-permute-start.13 = (bf16[2,272,128]{2,1,0:T(8,128)(2,1)S(1)}, bf16[2,272,128]{2,1,0:T(8,128)(2,1)S(1)}, u32[]{:S(2)}, u32[]{:S(2)}) collective-permute-start(bf16[2,272,128]{2,1,0:T(8,128)(2,1)S(1)} %get-tuple-element.37), channel_id=1, source_target_pairs={{0,8},{1,11},{2,10},{3,9},{4,12},{5,15},{6,14},{7,13},{8,0},{9,3},... | collective-permute-start | bytes 417800 | tf_op jit(solution)/shard_map/ppermute | solution.py:235
  32.9 0.1 copy.10.query_rank
  33.1 2.4 %collective-permute-start.15 = (bf16[2,272,128]{2,1,0:T(8,128)(2,1)S(1)}, bf16[2,272,128]{2,1,0:T(8,128)(2,1)S(1)}, u32[]{:S(2)}, u32[]{:S(2)}) collective-permute-start(bf16[2,272,128]{2,1,0:T(8,128)(2,1)S(1)} %get-tuple-element.38), channel_id=1, source_target_pairs={{0,12},{1,15},{2,14},{3,13},{4,8},{5,11},{6,10},{7,9},{8,4},{9,7},... | collective-permute-start | bytes 417800 | tf_op jit(solution)/shard_map/ppermute | solution.py:235
  35.5 2.2 %attend.2 = (bf16[1,272,128]{2,1,0:T(8,128)(2,1)S(1)}, bf16[1,272,128]{2,1,0:T(8,128)(2,1)S(1)}, bf16[1,272,128]{2,1,0:T(8,128)(2,1)S(1)}, bf16[1,272,128]{2,1,0:T(8,128)(2,1)S(1)}) custom-call(s32[1,512]{1,0:T(1,128)S(1)} %bitcast.5, s32[256,1]{1,0:T(8,128)S(1)} %copy.10.query_rank, bf16[5,64,512]{2,1,0:T(8,128)(2,1)S(1)} %copy-done, ...), custom_call_target="tpu_custom_call" | custom-call | flops 536870912 | bytes 3145728 | tf_op jit(solution)/shard_map/attend/pallas_call | solution.py:145
  37.7 0.4 collective-permute-start.10
  38.1 1.6 %collective-permute-start.11 = (bf16[1,272,128]{2,1,0:T(8,128)(2,1)S(1)}, bf16[1,272,128]{2,1,0:T(8,128)(2,1)S(1)}, u32[]{:S(2)}, u32[]{:S(2)}) collective-permute-start(bf16[1,272,128]{2,1,0:T(8,128)(2,1)S(1)} %get-tuple-element.36), channel_id=1, source_target_pairs={{0,6},{1,7},{2,4},{3,5},{4,2},{5,3},{6,0},{7,1},{8,14},{9,15},{10,... | collective-permute-start | bytes 208904 | tf_op jit(solution)/shard_map/ppermute | solution.py:231
  39.7 1.5 %collective-permute-start.9 = (bf16[1,272,128]{2,1,0:T(8,128)(2,1)S(1)}, bf16[1,272,128]{2,1,0:T(8,128)(2,1)S(1)}, u32[]{:S(2)}, u32[]{:S(2)}) collective-permute-start(bf16[1,272,128]{2,1,0:T(8,128)(2,1)S(1)} %get-tuple-element.34), channel_id=1, source_target_pairs={{0,2},{1,3},{2,0},{3,1},{4,6},{5,7},{6,4},{7,5},{8,10},{9,11},{10,... | collective-permute-start | bytes 208904 | tf_op jit(solution)/shard_map/ppermute | solution.py:231
  41.2 3.5 %collective-permute-done.13 = bf16[2,272,128]{2,1,0:T(8,128)(2,1)S(1)} collective-permute-done((bf16[2,272,128]{2,1,0:T(8,128)(2,1)S(1)}, bf16[2,272,128]{2,1,0:T(8,128)(2,1)S(1)}, u32[]{:S(2)}, u32[]{:S(2)}) %collective-permute-start.13) | collective-permute-done | bytes 139296 | tf_op jit(solution)/shard_map/ppermute | solution.py:235
  44.9 0.5 %collective-permute-start.16 = (bf16[1,272,128]{2,1,0:T(8,128)(2,1)S(1)}, bf16[1,272,128]{2,1,0:T(8,128)(2,1)S(1)}, u32[]{:S(2)}, u32[]{:S(2)}) collective-permute-start(bf16[1,272,128]{2,1,0:T(8,128)(2,1)S(1)} %get-tuple-element.43), channel_id=1, source_target_pairs={{0,1},{1,0},{2,3},{3,2},{4,5},{5,4},{6,7},{7,6},{8,9},{9,8},{10,11... | collective-permute-start | bytes 208904 | tf_op jit(solution)/shard_map/ppermute | solution.py:231
  45.4 1.1 %collective-permute-done.11.refs_3_ = bf16[1,272,128]{2,1,0:T(8,128)(2,1)S(1)} collective-permute-done((bf16[1,272,128]{2,1,0:T(8,128)(2,1)S(1)}, bf16[1,272,128]{2,1,0:T(8,128)(2,1)S(1)}, u32[]{:S(2)}, u32[]{:S(2)}) %collective-permute-start.11) | collective-permute-done | bytes 69664 | tf_op jit(solution)/shard_map/ppermute | solution.py:231
  46.5 1.7 %merge.1 = bf16[64,2048]{1,0:T(8,128)(2,1)} custom-call(s32[1]{0:T(128)} %bitcast.where, bf16[1,272,128]{2,1,0:T(8,128)(2,1)S(1)} %get-tuple-element.33.refs_0_, bf16[1,272,128]{2,1,0:T(8,128)(2,1)S(1)} %collective-permute-done.9.refs_1_, bf16[1,272,128]{2,1,0:T(8,128)(2,1)S(1)} %collective-permute-done.10.refs_2_, ...), custom_call_target="tpu_custom_call" | custom-call | tf_op jit(solution)/shard_map/merge/pallas_call | solution.py:200
  (39 shorter events, 0.5 us)
Async XLA Ops:
  2.4 4.8 %copy-start.1 = (bf16[2,64,512]{2,1,0:T(8,128)(2,1)S(1)}, bf16[2,64,512]{2,1,0:T(8,128)(2,1)}, u32[]{:S(2)}) copy-start(bf16[2,64,512]{2,1,0:T(8,128)(2,1)} %get-tuple-element.29) | copy-start | bytes 393220
  2.4 15.6 %collective-permute-start = (bf16[5,64,512]{2,1,0:T(8,128)(2,1)}, bf16[5,64,512]{2,1,0:T(8,128)(2,1)S(1)}, u32[]{:S(2)}, u32[]{:S(2)}) collective-permute-start(bf16[5,64,512]{2,1,0:T(8,128)(2,1)} %get-tuple-element.22), channel_id=1, source_target_pairs={{0,6},{1,7},{2,4},{3,5},{4,2},{5,3},{6,0},{7,1},{8,14},{9,15},{10,... | collective-permute-start | bytes 983048 | tf_op jit(solution)/shard_map/ppermute | solution.py:231
  6.5 1.6 %collective-permute-start.3 = (bf16[2,64,512]{2,1,0:T(8,128)(2,1)}, bf16[2,64,512]{2,1,0:T(8,128)(2,1)S(1)}, u32[]{:S(2)}, u32[]{:S(2)}) collective-permute-start(bf16[2,64,512]{2,1,0:T(8,128)(2,1)} %get-tuple-element.27), channel_id=1, source_target_pairs={{0,1},{1,0},{2,3},{3,2},{4,5},{5,4},{6,7},{7,6},{8,9},{9,8},{10,11... | collective-permute-start | bytes 393224 | tf_op jit(solution)/shard_map/ppermute | solution.py:231
  6.5 18.2 %collective-permute-start.2 = (bf16[5,64,512]{2,1,0:T(8,128)(2,1)}, bf16[5,64,512]{2,1,0:T(8,128)(2,1)S(1)}, u32[]{:S(2)}, u32[]{:S(2)}) collective-permute-start(bf16[5,64,512]{2,1,0:T(8,128)(2,1)} %get-tuple-element.26), channel_id=1, source_target_pairs={{0,4},{1,5},{2,6},{3,7},{4,0},{5,1},{6,2},{7,3},{8,12},{9,13},{10,... | collective-permute-start | bytes 983048 | tf_op jit(solution)/shard_map/ppermute | solution.py:231
  6.9 18.4 %collective-permute-start.1 = (bf16[5,64,512]{2,1,0:T(8,128)(2,1)}, bf16[5,64,512]{2,1,0:T(8,128)(2,1)S(1)}, u32[]{:S(2)}, u32[]{:S(2)}) collective-permute-start(bf16[5,64,512]{2,1,0:T(8,128)(2,1)} %get-tuple-element.25), channel_id=1, source_target_pairs={{0,2},{1,3},{2,0},{3,1},{4,6},{5,7},{6,4},{7,5},{8,10},{9,11},{10,... | collective-permute-start | bytes 983048 | tf_op jit(solution)/shard_map/ppermute | solution.py:231
  7.2 3.5 %copy-start = (bf16[5,64,512]{2,1,0:T(8,128)(2,1)S(1)}, bf16[5,64,512]{2,1,0:T(8,128)(2,1)}, u32[]{:S(2)}) copy-start(bf16[5,64,512]{2,1,0:T(8,128)(2,1)} %get-tuple-element.28.refs_0_.refs_4_.refs_2_) | copy-start | bytes 983044
  8.1 16.6 %collective-permute-start.5 = (bf16[2,64,512]{2,1,0:T(8,128)(2,1)S(1)}, bf16[2,64,512]{2,1,0:T(8,128)(2,1)S(1)}, u32[]{:S(2)}, u32[]{:S(2)}) collective-permute-start(bf16[2,64,512]{2,1,0:T(8,128)(2,1)S(1)} %pad_maximum_fusion), channel_id=1, source_target_pairs={{0,8},{1,11},{2,10},{3,9},{4,12},{5,15},{6,14},{7,13},{8,0},{9,3},... | collective-permute-start | bytes 393224 | tf_op jit(solution)/shard_map/ppermute | solution.py:235
  10.7 18.5 %collective-permute-start.4 = (bf16[5,64,512]{2,1,0:T(8,128)(2,1)S(1)}, bf16[5,64,512]{2,1,0:T(8,128)(2,1)S(1)}, u32[]{:S(2)}, u32[]{:S(2)}) collective-permute-start(bf16[5,64,512]{2,1,0:T(8,128)(2,1)S(1)} %copy-done), channel_id=1, source_target_pairs={{0,1},{1,0},{2,3},{3,2},{4,5},{5,4},{6,7},{7,6},{8,9},{9,8},{10,11... | collective-permute-start | bytes 983048 | tf_op jit(solution)/shard_map/ppermute | solution.py:231
  11.1 11.1 %copy-start.2 = (s32[16]{0:T(128)S(1)}, s32[16]{0:T(128)}, u32[]{:S(2)}) copy-start(s32[16]{0:T(128)} %param.12) | copy-start | bytes 196
  18.1 11.2 %collective-permute-start.12 = (bf16[2,64,512]{2,1,0:T(8,128)(2,1)S(1)}, bf16[2,64,512]{2,1,0:T(8,128)(2,1)S(1)}, u32[]{:S(2)}, u32[]{:S(2)}) collective-permute-start(bf16[2,64,512]{2,1,0:T(8,128)(2,1)S(1)} %pad_maximum_fusion.1), channel_id=1, source_target_pairs={{0,12},{1,15},{2,14},{3,13},{4,8},{5,11},{6,10},{7,9},{8,4},{9,7},... | collective-permute-start | bytes 393224 | tf_op jit(solution)/shard_map/ppermute | solution.py:235
  24.7 4.6 %collective-permute-start.8 = (bf16[5,64,512]{2,1,0:T(8,128)(2,1)S(1)}, bf16[5,64,512]{2,1,0:T(8,128)(2,1)S(1)}, u32[]{:S(2)}, u32[]{:S(2)}) collective-permute-start(bf16[5,64,512]{2,1,0:T(8,128)(2,1)S(1)} %collective-permute-done.refs_3_.refs_10_.refs_8_), channel_id=1, source_target_pairs={{0,1},{1,0},{2,3},{3,2},{4,5},{5,4},{6,7},{7,6},{8,9},{9,8},{10,11... | collective-permute-start | bytes 983048 | tf_op jit(solution)/shard_map/ppermute | solution.py:231
  24.7 4.5 %collective-permute-start.7 = (bf16[5,64,512]{2,1,0:T(8,128)(2,1)S(1)}, bf16[5,64,512]{2,1,0:T(8,128)(2,1)S(1)}, u32[]{:S(2)}, u32[]{:S(2)}) collective-permute-start(bf16[5,64,512]{2,1,0:T(8,128)(2,1)S(1)} %collective-permute-done.2.refs_2_.refs_8_.refs_6_), channel_id=1, source_target_pairs={{0,1},{1,0},{2,3},{3,2},{4,5},{5,4},{6,7},{7,6},{8,9},{9,8},{10,11... | collective-permute-start | bytes 983048 | tf_op jit(solution)/shard_map/ppermute | solution.py:231
  25.3 0.7 %copy-start.3 = (s32[16]{0:T(128)S(1)}, s32[16]{0:T(128)}, u32[]{:S(2)}) copy-start(s32[16]{0:T(128)} %param.13) | copy-start | bytes 196
  25.3 3.9 %collective-permute-start.6 = (bf16[5,64,512]{2,1,0:T(8,128)(2,1)S(1)}, bf16[5,64,512]{2,1,0:T(8,128)(2,1)S(1)}, u32[]{:S(2)}, u32[]{:S(2)}) collective-permute-start(bf16[5,64,512]{2,1,0:T(8,128)(2,1)S(1)} %collective-permute-done.1.refs_1_.refs_6_.refs_4_), channel_id=1, source_target_pairs={{0,1},{1,0},{2,3},{3,2},{4,5},{5,4},{6,7},{7,6},{8,9},{9,8},{10,11... | collective-permute-start | bytes 983048 | tf_op jit(solution)/shard_map/ppermute | solution.py:231
  31.5 13.2 %collective-permute-start.13 = (bf16[2,272,128]{2,1,0:T(8,128)(2,1)S(1)}, bf16[2,272,128]{2,1,0:T(8,128)(2,1)S(1)}, u32[]{:S(2)}, u32[]{:S(2)}) collective-permute-start(bf16[2,272,128]{2,1,0:T(8,128)(2,1)S(1)} %get-tuple-element.37), channel_id=1, source_target_pairs={{0,8},{1,11},{2,10},{3,9},{4,12},{5,15},{6,14},{7,13},{8,0},{9,3},... | collective-permute-start | bytes 417800 | tf_op jit(solution)/shard_map/ppermute | solution.py:235
  33.1 11.8 %collective-permute-start.15 = (bf16[2,272,128]{2,1,0:T(8,128)(2,1)S(1)}, bf16[2,272,128]{2,1,0:T(8,128)(2,1)S(1)}, u32[]{:S(2)}, u32[]{:S(2)}) collective-permute-start(bf16[2,272,128]{2,1,0:T(8,128)(2,1)S(1)} %get-tuple-element.38), channel_id=1, source_target_pairs={{0,12},{1,15},{2,14},{3,13},{4,8},{5,11},{6,10},{7,9},{8,4},{9,7},... | collective-permute-start | bytes 417800 | tf_op jit(solution)/shard_map/ppermute | solution.py:235
  37.7 7.7 %collective-permute-start.10 = (bf16[1,272,128]{2,1,0:T(8,128)(2,1)S(1)}, bf16[1,272,128]{2,1,0:T(8,128)(2,1)S(1)}, u32[]{:S(2)}, u32[]{:S(2)}) collective-permute-start(bf16[1,272,128]{2,1,0:T(8,128)(2,1)S(1)} %get-tuple-element.35), channel_id=1, source_target_pairs={{0,4},{1,5},{2,6},{3,7},{4,0},{5,1},{6,2},{7,3},{8,12},{9,13},{10,... | collective-permute-start | bytes 208904 | tf_op jit(solution)/shard_map/ppermute | solution.py:231
  38.1 8.3 %collective-permute-start.11 = (bf16[1,272,128]{2,1,0:T(8,128)(2,1)S(1)}, bf16[1,272,128]{2,1,0:T(8,128)(2,1)S(1)}, u32[]{:S(2)}, u32[]{:S(2)}) collective-permute-start(bf16[1,272,128]{2,1,0:T(8,128)(2,1)S(1)} %get-tuple-element.36), channel_id=1, source_target_pairs={{0,6},{1,7},{2,4},{3,5},{4,2},{5,3},{6,0},{7,1},{8,14},{9,15},{10,... | collective-permute-start | bytes 208904 | tf_op jit(solution)/shard_map/ppermute | solution.py:231
  39.7 6.7 %collective-permute-start.9 = (bf16[1,272,128]{2,1,0:T(8,128)(2,1)S(1)}, bf16[1,272,128]{2,1,0:T(8,128)(2,1)S(1)}, u32[]{:S(2)}, u32[]{:S(2)}) collective-permute-start(bf16[1,272,128]{2,1,0:T(8,128)(2,1)S(1)} %get-tuple-element.34), channel_id=1, source_target_pairs={{0,2},{1,3},{2,0},{3,1},{4,6},{5,7},{6,4},{7,5},{8,10},{9,11},{10,... | collective-permute-start | bytes 208904 | tf_op jit(solution)/shard_map/ppermute | solution.py:231
  44.7 1.7 %collective-permute-start.14 = (bf16[1,272,128]{2,1,0:T(8,128)(2,1)S(1)}, bf16[1,272,128]{2,1,0:T(8,128)(2,1)S(1)}, u32[]{:S(2)}, u32[]{:S(2)}) collective-permute-start(bf16[1,272,128]{2,1,0:T(8,128)(2,1)S(1)} %get-tuple-element.45), channel_id=1, source_target_pairs={{0,1},{1,0},{2,3},{3,2},{4,5},{5,4},{6,7},{7,6},{8,9},{9,8},{10,11... | collective-permute-start | bytes 208904 | tf_op jit(solution)/shard_map/ppermute | solution.py:231
  44.9 1.6 %collective-permute-start.16 = (bf16[1,272,128]{2,1,0:T(8,128)(2,1)S(1)}, bf16[1,272,128]{2,1,0:T(8,128)(2,1)S(1)}, u32[]{:S(2)}, u32[]{:S(2)}) collective-permute-start(bf16[1,272,128]{2,1,0:T(8,128)(2,1)S(1)} %get-tuple-element.43), channel_id=1, source_target_pairs={{0,1},{1,0},{2,3},{3,2},{4,5},{5,4},{6,7},{7,6},{8,9},{9,8},{10,11... | collective-permute-start | bytes 208904 | tf_op jit(solution)/shard_map/ppermute | solution.py:231

commit v5 on v4

--- a/solution.py
+++ b/solution.py
@@ -58,9 +58,10 @@
     for copy in arriving[:kinds]:
         copy.wait()
     for step in range(members)[::-1]:
-        for kind in range(kinds + 1):
+        depth = outs[step].shape[0]
+        for kind in range(depth):
             near_room[step, kind] = whole_room[kind, :, columns(step)]
-        send(near_room.at[step], outs[step])
+        send(near_room.at[step, pl.ds(0, depth)], outs[step])
     for copy in leaving:
         copy.wait()
 
@@ -75,7 +76,8 @@
     size = kinds * rows * columns * 2
     result = pl.pallas_call(
         functools.partial(split_kernel, members, width),
-        out_shape=[jax.ShapeDtypeStruct(near, queries.dtype)] * members
+        out_shape=[jax.ShapeDtypeStruct(near, queries.dtype)] * CORES
+        + [jax.ShapeDtypeStruct((kinds - 1,) + near[1:], queries.dtype)] * (members - CORES)
         + [jax.ShapeDtypeStruct(far, queries.dtype)] * CORES,
         in_specs=[pl.BlockSpec(memory_space=pltpu.SMEM)] + [anywhere] * kinds,
         out_specs=[anywhere] * (members + CORES),
@@ -134,77 +136,92 @@
         place[heads * rows :, :] = jnp.concatenate([mine, filler], axis=1)
 
 
-def attend(arrays, picks, per_out, query_rank, keys, key_rank):
+def attend(arrays, picks, depths, query_rank, keys, key_rank):
     blocks = len(keys)
-    kinds, rows, width = keys[0].shape
+    rows, width = keys[0].shape[1:]
     heads = width // HEAD_DIM
     query_count, key_count = len(picks) * rows, blocks * rows
     vmem = pl.BlockSpec(memory_space=pltpu.VMEM)
-    out = jax.ShapeDtypeStruct((per_out, heads * rows + STAT_ROWS, HEAD_DIM), jnp.bfloat16)
-    outs = len(picks) // per_out
+    tile = (heads * rows + STAT_ROWS, HEAD_DIM)
     return pl.pallas_call(
         functools.partial(attend_kernel, picks, len(arrays), blocks, heads),
-        out_shape=[out] * outs,
+        out_shape=[jax.ShapeDtypeStruct((depth,) + tile, jnp.bfloat16) for depth in depths],
         in_specs=[vmem] * (2 + len(arrays) + blocks),
-        out_specs=[vmem] * outs,
+        out_specs=[vmem] * len(depths),
         compiler_params=pltpu.CompilerParams(vmem_limit_bytes=VMEM_LIMIT),
         cost_estimate=pl.CostEstimate(
             flops=8 * heads * query_count * key_count * HEAD_DIM,
-            bytes_accessed=2 * width * (query_count * 2 + key_count * kinds),
+            bytes_accessed=2 * width * (query_count * 2 + key_count * 4),
             transcendentals=heads * query_count * key_count,
         ),
         name="attend",
     )(key_rank[None, :], query_rank[:, None], *arrays, *keys)
 
 
-def merge_kernel(parts, members, heads, where, *refs):
-    out = refs[-1]
+def merge_kernel(chosen, parts, members, heads, where, *refs):
+    out, room, sems = refs[-3:]
     rows = out.shape[0]
-    near, far = refs[:members], refs[members:-1]
+    width = heads * HEAD_DIM
     member, core = where[0] // CORES % members, where[0] % CORES
-    for step in range(members):
-        pair, side = step // CORES, step % CORES
-        group = [near[pair * CORES].at[0][...]]
-        for other in range(1, CORES):
-            wanted = (core ^ side) == other
-            group[0] = jnp.where(wanted, near[pair * CORES + other].at[0][...], group[0])
-        for part in range(parts - 1):
-            group.append(far[(part * (members // CORES) + pair) * CORES + side].at[0][...])
-        start = (member ^ (pair * CORES + (core ^ side))) * heads * HEAD_DIM
-        levels = [one[heads * rows :].astype(jnp.float32).T[:rows] for one in group]
-        for head in range(heads):
-            lane = head * STAT_TERMS
-            level = [
-                one[:, lane : lane + 1] + one[:, lane + 1 : lane + 2] + one[:, lane + 2 : lane + 3]
-                for one in levels
-            ]
-            top = functools.reduce(jnp.maximum, level)
-            shares = [jnp.exp2(one - top) for one in level]
-            total = functools.reduce(jnp.add, shares)
-            mixed = functools.reduce(
-                jnp.add,
-                [
-                    one[head * rows : (head + 1) * rows].astype(jnp.float32) * (share / total)
-                    for one, share in zip(group, shares)
-                ],
-            )
-            at = pl.multiple_of(start + head * HEAD_DIM, HEAD_DIM)
-            out[:, pl.ds(at, HEAD_DIM)] = mixed.astype(out.dtype)
-
-
-def merge(where, near, far, rows, heads):
-    members = len(near)
-    pairs = members // CORES
-    parts = 1 + len(far) // (pairs * CORES)
-    vmem = pl.BlockSpec(memory_space=pltpu.VMEM)
+    refs = list(refs)
+    leaving = []
+    for place, pair in enumerate(chosen):
+        direct = [refs.pop(0) for _ in range(CORES)] if pair == 0 else None
+        crossed = [refs.pop(0) for _ in range((parts if pair else parts - 1) * CORES)]
+        for side in range(CORES):
+            group = [one.at[0][...] for one in crossed[side::CORES]]
+            if pair == 0:
+                one = direct[0].at[0][...]
+                for step in range(1, CORES):
+                    one = jnp.where((core ^ side) == step, direct[step].at[0][...], one)
+                group.append(one)
+            at = place * CORES + side
+            levels = [one[heads * rows :].astype(jnp.float32).T[:rows] for one in group]
+            for head in range(heads):
+                lane = head * STAT_TERMS
+                level = [
+                    one[:, lane : lane + 1]
+                    + one[:, lane + 1 : lane + 2]
+                    + one[:, lane + 2 : lane + 3]
+                    for one in levels
+                ]
+                top = functools.reduce(jnp.maximum, level)
+                shares = [jnp.exp2(one - top) for one in level]
+                total = functools.reduce(jnp.add, shares)
+                mixed = functools.reduce(
+                    jnp.add,
+                    [
+                        one[head * rows : (head + 1) * rows].astype(jnp.float32) * (share / total)
+                        for one, share in zip(group, shares)
+                    ],
+                )
+                room[at, :, head * HEAD_DIM : (head + 1) * HEAD_DIM] = mixed.astype(out.dtype)
+            start = pl.multiple_of((member ^ (pair * CORES + (core ^ side))) * width, width)
+            columns = out.at[:, pl.ds(start, width)]
+            leaving.append(pltpu.make_async_copy(room.at[at], columns, sems.at[at]))
+            leaving[-1].start()
+    for copy in leaving:
+        copy.wait()
+
+
+def merge(where, partials, chosen, parts, members, rows, heads, earlier=None):
+    vmem, anywhere = pl.BlockSpec(memory_space=pltpu.VMEM), pl.BlockSpec(memory_space=pl.ANY)
+    blocks = len(chosen) * CORES
+    operands = [where] + partials + ([] if earlier is None else [earlier])
+    specs = [pl.BlockSpec(memory_space=pltpu.SMEM)] + [vmem] * len(partials)
     return pl.pallas_call(
-        functools.partial(merge_kernel, parts, members, heads),
+        functools.partial(merge_kernel, chosen, parts, members, heads),
         out_shape=jax.ShapeDtypeStruct((rows, members * heads * HEAD_DIM), jnp.bfloat16),
-        in_specs=[pl.BlockSpec(memory_space=pltpu.SMEM)] + [vmem] * (len(near) + len(far)),
-        out_specs=vmem,
+        in_specs=specs + ([] if earlier is None else [anywhere]),
+        out_specs=anywhere,
+        scratch_shapes=[
+            pltpu.VMEM((blocks, rows, heads * HEAD_DIM), jnp.bfloat16),
+            pltpu.SemaphoreType.DMA((blocks,)),
+        ],
+        input_output_aliases={} if earlier is None else {len(operands) - 1: 0},
         compiler_params=pltpu.CompilerParams(vmem_limit_bytes=VMEM_LIMIT),
         name="merge",
-    )(where, *near, *far)
+    )(*operands)
 
 
 def after(array, earlier):
@@ -246,44 +263,67 @@
     blocks, (mine, others) = split_columns(where, members, queries, tensors)
     order = list(range(members))[::-1]
     other_mine = hop(others, 0, 0, 1)
+    payload = [jnp.stack([mine[pair], other_mine[pair]]) for pair in range(pairs)]
     arrived = {
-        (far, pair): far_hop(jnp.stack([mine[pair], other_mine[pair]]), far, pair)
+        (far, pair): far_hop(payload[pair], far, pair)
         for far in range(1, groups)
         for pair in range(pairs)[::-1]
     }
+    first_far = arrived[1, 0]
+    for pair in range(1, pairs):
+        arrived[0, pair] = far_hop(after(payload[pair], first_far), 0, pair)
     keys = {}
     keys[0, 0] = blocks[0]
     keys[0, 1] = hop(after(blocks[0], other_mine), 0, 0, 1)
     for near in order[:-1]:
         keys[near, 0] = hop(blocks[near], 0, near)
-        block = keys[near, 0]
-        block = after(block, arrived[1, 0])
-        keys[near, 1] = hop(block, 0, 0, 1)
+        keys[near, 1] = hop(after(after(keys[near, 0], first_far), keys[0, 1]), 0, 0, 1)
     starts_later = after(patch_starts, keys[order[0], 0])
     key_rank = ranks([(0, near, side) for near in range(members) for side in range(CORES)])
     key_blocks = [keys[near, side] for near in range(members) for side in range(CORES)]
-    far_parts, near_parts = [], [None] * members
+
+    def crossing(far, chunk):
+        places = [(far, pair * CORES + core, side) for pair in chunk for side in range(CORES)]
+        picks = [(at, side) for at in range(len(chunk)) for side in range(CORES)]
+        return [arrived[far, pair] for pair in chunk], places, picks
+
+    crossed = {}
+
+    def give_back(result, far, pair):
+        back = far_hop(result, far, pair)
+        crossed[far, pair] = [back[:1], hop(back[1:], 0, 0, 1)]
+
+    size = CHUNK // CORES
     for far in range(1, groups):
-        for first in range(0, pairs, CHUNK // CORES):
-            chunk = list(range(first, min(pairs, first + CHUNK // CORES)))
-            query_rank = ranks(
-                [(far, pair * CORES + core, side) for pair in chunk for side in range(CORES)]
-            )
-            waiting = [arrived[far, pair] for pair in chunk]
-            picks = [(at, side) for at in range(len(chunk)) for side in range(CORES)]
-            results = attend(waiting, picks, CORES, query_rank, key_blocks, key_rank)
+        for first in range(0, pairs, size):
+            chunk = list(range(first, min(pairs, first + size)))
+            waiting, places, picks = crossing(far, chunk)
+            depths = [CORES] * len(chunk)
+            results = attend(waiting, picks, depths, ranks(places), key_blocks, key_rank)
             for pair, result in zip(chunk, results):
-                back = far_hop(result, far, pair)
-                far_parts += [back[:1], hop(back[1:], 0, 0, 1)]
-    for first in range(0, members, CHUNK):
-        chunk = list(range(first, min(members, first + CHUNK)))
-        query_rank = ranks([(0, near, 0) for near in chunk])
-        waiting = [keys[near, 0] for near in chunk]
-        picks = [(at, len(tensors)) for at in range(len(chunk))]
-        results = attend(waiting, picks, 1, query_rank, key_blocks, key_rank)
-        for near, result in zip(chunk, results):
-            near_parts[near] = hop(result, 0, near)
-    return merge(where, near_parts, far_parts, rows, heads)
+                give_back(result, far, pair)
+    direct = [None] * CORES
+    for first in range(0, pairs, size):
+        chunk = list(range(max(first, 1), min(pairs, first + size)))
+        waiting, places, picks = crossing(0, chunk)
+        depths = [CORES] * len(chunk)
+        if first == 0:
+            depths += [1] * CORES
+            picks += [(len(chunk) + step, len(tensors)) for step in range(CORES)]
+            places += [(0, step, 0) for step in range(CORES)]
+            waiting = waiting + [keys[step, 0] for step in range(CORES)]
+        results = attend(waiting, picks, depths, ranks(places), key_blocks, key_rank)
+        for pair, result in zip(chunk, results):
+            give_back(result, 0, pair)
+        for step, result in enumerate(results[len(chunk) :]):
+            direct[step] = hop(result, 0, step)
+    first = direct + [one for far in range(1, groups) for one in crossed[far, 0]]
+    rest = [
+        one for pair in range(1, pairs) for far in range(groups) for one in crossed[far, pair]
+    ]
+    chosen = list(range(1, pairs))
+    merged = merge(where, rest, chosen, groups, members, rows, heads)
+    return merge(where, first, [0], groups, members, rows, heads, merged)
 
 
 def solution(mesh):

time: 48.5 us -> 48 us (0.990)
  waiting for transfers between devices: 17.4 us -> 15.6 us
  starting transfers between devices: 20.5 us -> 22 us
  local copies, waits for them, and re-layouts: 0.9 us -> 0.41 us
    ppermute x4 -> x6, starting transfers between devices: 10.6 us -> 15.9 us  [far_hop(): lax.ppermute(array, 'tok', [(i, i ^ flips[i]) for i in range(devices)])]
    ppermute x13 -> x12, starting transfers between devices: 9.86 us -> 6.08 us  [hop(): return lax.ppermute(array, 'tok', [(i, i ^ flip) for i in range(devices)])]
    ppermute x13 -> x12, waiting for transfers between devices: 8.54 us -> 6.19 us  [hop(): return lax.ppermute(array, 'tok', [(i, i ^ flip) for i in range(devices)])]
    ppermute x4 -> x6, waiting for transfers between devices: 8.85 us -> 9.38 us  [far_hop(): lax.ppermute(array, 'tok', [(i, i ^ flips[i]) for i in range(devices)])]
    unnamed x8, local copies, waits for them, and re-layouts: 0.52 us -> 0.02 us
    pallas_call x1 -> x2, Pallas kernels: 1.75 us -> 2.13 us  [merge(): pl.pallas_call(functools.partial(merge_kernel, chosen, parts, members, he...]
  transfers between devices with their start and end apart: 17 -> 18, of which waited for: 6 -> 7; matrix products, arithmetic and copies ran while one was open for 2% -> 2% of each run, Pallas kernels for 5% -> 11%
where the time goes in v5:
time: 48 us; the launch traced here: 47.9 us
  starting transfers between devices  22 us (46%)
  waiting for transfers between devices  15.6 us (32%)
  Pallas kernels  8.93 us (19%)
  other arithmetic  0.68 us (1%)
    ppermute x6, starting transfers between devices, far_hop(): lax.ppermute(array, 'tok', [(i, i ^ flips[i]) for i in range(devices)])  15.9 us
    ppermute x6, waiting for transfers between devices, far_hop(): lax.ppermute(array, 'tok', [(i, i ^ flips[i]) for i in range(devices)])  9.38 us
    ppermute x12, waiting for transfers between devices, hop(): return lax.ppermute(array, 'tok', [(i, i ^ flip) for i in range(devices)])  6.19 us
    ppermute x12, starting transfers between devices, hop(): return lax.ppermute(array, 'tok', [(i, i ^ flip) for i in range(devices)])  6.08 us
    pallas_call x2, Pallas kernels, attend(): pl.pallas_call(functools.partial(attend_kernel, picks, len(arrays), block...  4.42 us
    pallas_call x1, Pallas kernels, split_columns(): pl.pallas_call(functools.partial(split_kernel, members, width), out_shape...  2.39 us
    pallas_call x2, Pallas kernels, merge(): pl.pallas_call(functools.partial(merge_kernel, chosen, parts, members, he...  2.13 us
  transfers between devices with their start and end apart: 18, of which 7 were waited for; matrix products, arithmetic and copies ran while one was open for 2% of the time, Pallas kernels for 11%

profile of v5, /device:TPU:0, one launch (start us, length us, event | category | flops | bytes accessed | tf_op | source)
XLA Modules:
  0.0 47.9 jit_solution(16333633578407770495)
XLA Ops:
  0.0 2.4 %split_columns.1 = (bf16[5,64,512]{2,1,0:T(8,128)(2,1)}, bf16[5,64,512]{2,1,0:T(8,128)(2,1)}, bf16[4,64,512]{2,1,0:T(8,128)(2,1)}, bf16[4,64,512]{2,1,0:T(8,128)...) custom-call(s32[1]{0:T(128)} %bitcast.where, bf16[64,2048]{1,0:T(8,128)(2,1)} %queries.1, ...), custom_call_target="tpu_custom_call" | custom-call | bytes 2621440 | tf_op jit(solution)/shard_map/split_columns/pallas_call | solution.py:77
  2.4 4.0 %collective-permute-start = (bf16[4,64,512]{2,1,0:T(8,128)(2,1)}, bf16[4,64,512]{2,1,0:T(8,128)(2,1)S(1)}, u32[]{:S(2)}, u32[]{:S(2)}) collective-permute-start(bf16[4,64,512]{2,1,0:T(8,128)(2,1)} %get-tuple-element.25), channel_id=1, source_target_pairs={{0,6},{1,7},{2,4},{3,5},{4,2},{5,3},{6,0},{7,1},{8,14},{9,15},{10,... | collective-permute-start | bytes 786440 | tf_op jit(solution)/shard_map/ppermute | solution.py:248
  6.4 0.4 collective-permute-start.7
  6.9 0.3 collective-permute-start.4
  7.3 0.1 concatenate.9
  7.5 0.5 %collective-permute-done.1 = bf16[2,64,512]{2,1,0:T(8,128)(2,1)S(1)} collective-permute-done((bf16[2,64,512]{2,1,0:T(8,128)(2,1)}, bf16[2,64,512]{2,1,0:T(8,128)(2,1)S(1)}, u32[]{:S(2)}, u32[]{:S(2)}) %collective-permute-start.1) | collective-permute-done | bytes 131104 | tf_op jit(solution)/shard_map/ppermute | solution.py:248
  8.0 2.7 %collective-permute-start.2 = (bf16[2,64,512]{2,1,0:T(8,128)(2,1)S(1)}, bf16[2,64,512]{2,1,0:T(8,128)(2,1)S(1)}, u32[]{:S(2)}, u32[]{:S(2)}) collective-permute-start(bf16[2,64,512]{2,1,0:T(8,128)(2,1)S(1)} %pad_maximum_fusion.1), channel_id=1, source_target_pairs={{0,8},{1,11},{2,10},{3,9},{4,12},{5,15},{6,14},{7,13},{8,0},{9,3},... | collective-permute-start | bytes 393224 | tf_op jit(solution)/shard_map/ppermute | solution.py:252
  10.7 0.4 collective-permute-start.5
  11.1 5.5 %collective-permute-done.refs_9_.refs_8_ = bf16[4,64,512]{2,1,0:T(8,128)(2,1)S(1)} collective-permute-done((bf16[4,64,512]{2,1,0:T(8,128)(2,1)}, bf16[4,64,512]{2,1,0:T(8,128)(2,1)S(1)}, u32[]{:S(2)}, u32[]{:S(2)}) %collective-permute-start) | collective-permute-done | bytes 262176 | tf_op jit(solution)/shard_map/ppermute | solution.py:248
  16.6 4.1 %collective-permute-start.11 = (bf16[2,64,512]{2,1,0:T(8,128)(2,1)S(1)}, bf16[2,64,512]{2,1,0:T(8,128)(2,1)S(1)}, u32[]{:S(2)}, u32[]{:S(2)}) collective-permute-start(bf16[2,64,512]{2,1,0:T(8,128)(2,1)S(1)} %pad_maximum_fusion), channel_id=1, source_target_pairs={{0,12},{1,15},{2,14},{3,13},{4,8},{5,11},{6,10},{7,9},{8,4},{9,7},... | collective-permute-start | bytes 393224 | tf_op jit(solution)/shard_map/ppermute | solution.py:252
  20.7 0.1 convert_reduce_fusion.1
  20.8 1.1 %collective-permute-done.2.refs_0_ = bf16[2,64,512]{2,1,0:T(8,128)(2,1)S(1)} collective-permute-done((bf16[2,64,512]{2,1,0:T(8,128)(2,1)S(1)}, bf16[2,64,512]{2,1,0:T(8,128)(2,1)S(1)}, u32[]{:S(2)}, u32[]{:S(2)}) %collective-permute-start.2) | collective-permute-done | bytes 131104 | tf_op jit(solution)/shard_map/ppermute | solution.py:252
  21.9 0.1 convert_reduce_fusion
  22.1 0.5 %collective-permute-start.8 = (bf16[4,64,512]{2,1,0:T(8,128)(2,1)S(1)}, bf16[4,64,512]{2,1,0:T(8,128)(2,1)S(1)}, u32[]{:S(2)}, u32[]{:S(2)}) collective-permute-start(bf16[4,64,512]{2,1,0:T(8,128)(2,1)S(1)} %collective-permute-done.7.refs_7_.refs_6_), channel_id=1, source_target_pairs={{0,1},{1,0},{2,3},{3,2},{4,5},{5,4},{6,7},{7,6},{8,9},{9,8},{10,11... | collective-permute-start | bytes 786440 | tf_op jit(solution)/shard_map/ppermute | solution.py:248
  22.6 0.1 collective-permute-start.6
  22.6 0.1 select_reduce_fusion.3
  22.7 0.1 select_reduce_fusion.1
  22.8 0.1 copy.12.query_rank
  23.0 3.6 %collective-permute-start.3 = (bf16[2,64,512]{2,1,0:T(8,128)(2,1)S(1)}, bf16[2,64,512]{2,1,0:T(8,128)(2,1)S(1)}, u32[]{:S(2)}, u32[]{:S(2)}) collective-permute-start(bf16[2,64,512]{2,1,0:T(8,128)(2,1)S(1)} %pad_maximum_fusion), channel_id=1, source_target_pairs={{0,4},{1,7},{2,6},{3,5},{4,0},{5,3},{6,2},{7,1},{8,12},{9,15},{10,... | collective-permute-start | bytes 393224 | tf_op jit(solution)/shard_map/ppermute | solution.py:252
  26.6 0.1 select_reduce_fusion
  26.7 2.2 %attend.3 = (bf16[2,272,128]{2,1,0:T(8,128)(2,1)S(1)}, bf16[2,272,128]{2,1,0:T(8,128)(2,1)S(1)}) custom-call(s32[1,512]{1,0:T(1,128)S(1)} %bitcast.4, s32[256,1]{1,0:T(8,128)S(1)} %copy.12.query_rank, bf16[2,64,512]{2,1,0:T(8,128)(2,1)S(1)} %collective-permute-done.2.refs_0_, bf16[2,64,512]{2,1,0:T(8,128)(2,1)S(1)} %collective-permute-done.11.refs_1_, ...), custom_call_target="tpu_custom_call" | custom-call | flops 536870912 | bytes 2621440 | tf_op jit(solution)/shard_map/attend/pallas_call | solution.py:146
  28.9 3.9 %collective-permute-start.16 = (bf16[2,272,128]{2,1,0:T(8,128)(2,1)S(1)}, bf16[2,272,128]{2,1,0:T(8,128)(2,1)S(1)}, u32[]{:S(2)}, u32[]{:S(2)}) collective-permute-start(bf16[2,272,128]{2,1,0:T(8,128)(2,1)S(1)} %get-tuple-element.44), channel_id=1, source_target_pairs={{0,12},{1,15},{2,14},{3,13},{4,8},{5,11},{6,10},{7,9},{8,4},{9,7},... | collective-permute-start | bytes 417800 | tf_op jit(solution)/shard_map/ppermute | solution.py:252
  32.8 0.1 copy.11.query_rank
  32.9 2.2 %attend.2 = (bf16[2,272,128]{2,1,0:T(8,128)(2,1)S(1)}, bf16[1,272,128]{2,1,0:T(8,128)(2,1)S(1)}, bf16[1,272,128]{2,1,0:T(8,128)(2,1)S(1)}) custom-call(s32[1,512]{1,0:T(1,128)S(1)} %bitcast.5, s32[256,1]{1,0:T(8,128)S(1)} %copy.11.query_rank, bf16[2,64,512]{2,1,0:T(8,128)(2,1)S(1)} %collective-permute-done.3.refs_0_, bf16[5,64,512]{2,1,0:T(8,128)(2,1)S(1)} %copy-done, ...), custom_call_target="tpu_custom_call" | custom-call | flops 536870912 | bytes 2621440 | tf_op jit(solution)/shard_map/attend/pallas_call | solution.py:146
  35.1 1.8 %collective-permute-start.12 = (bf16[2,272,128]{2,1,0:T(8,128)(2,1)S(1)}, bf16[2,272,128]{2,1,0:T(8,128)(2,1)S(1)}, u32[]{:S(2)}, u32[]{:S(2)}) collective-permute-start(bf16[2,272,128]{2,1,0:T(8,128)(2,1)S(1)} %get-tuple-element.42), channel_id=1, source_target_pairs={{0,8},{1,11},{2,10},{3,9},{4,12},{5,15},{6,14},{7,13},{8,0},{9,3},... | collective-permute-start | bytes 417800 | tf_op jit(solution)/shard_map/ppermute | solution.py:252
  36.9 0.5 collective-permute-done.16
  37.4 0.2 collective-permute-start.17
  37.5 5.8 %collective-permute-done.14 = bf16[2,272,128]{2,1,0:T(8,128)(2,1)S(1)} collective-permute-done((bf16[2,272,128]{2,1,0:T(8,128)(2,1)S(1)}, bf16[2,272,128]{2,1,0:T(8,128)(2,1)S(1)}, u32[]{:S(2)}, u32[]{:S(2)}) %collective-permute-start.14) | collective-permute-done | bytes 139296 | tf_op jit(solution)/shard_map/ppermute | solution.py:252
  43.4 2.0 %collective-permute-done.12 = bf16[2,272,128]{2,1,0:T(8,128)(2,1)S(1)} collective-permute-done((bf16[2,272,128]{2,1,0:T(8,128)(2,1)S(1)}, bf16[2,272,128]{2,1,0:T(8,128)(2,1)S(1)}, u32[]{:S(2)}, u32[]{:S(2)}) %collective-permute-start.12) | collective-permute-done | bytes 139296 | tf_op jit(solution)/shard_map/ppermute | solution.py:252
  45.6 1.1 %merge.2.refs_4_ = bf16[64,2048]{1,0:T(8,128)(2,1)} custom-call(s32[1]{0:T(128)} %bitcast.where, bf16[1,272,128]{2,1,0:T(8,128)(2,1)S(1)} %get-tuple-element.52.refs_0_, bf16[1,272,128]{2,1,0:T(8,128)(2,1)S(1)} %collective-permute-done.15.refs_1_, bf16[1,272,128]{2,1,0:T(8,128)(2,1)S(1)} %get-tuple-element.50.refs_2_, ...), custom_call_target="tpu_custom_call" | custom-call | tf_op jit(solution)/shard_map/merge/pallas_call | solution.py:212
  46.7 0.1 collective-permute-done.13.refs_3_
  46.8 1.1 %merge.3 = bf16[64,2048]{1,0:T(8,128)(2,1)} custom-call(s32[1]{0:T(128)} %bitcast.where, bf16[1,272,128]{2,1,0:T(8,128)(2,1)S(1)} %get-tuple-element.40.refs_0_, bf16[1,272,128]{2,1,0:T(8,128)(2,1)S(1)} %collective-permute-done.10.refs_1_, bf16[1,272,128]{2,1,0:T(8,128)(2,1)S(1)} %get-tuple-element.54.refs_2_, ...), custom_call_target="tpu_custom_call", output_to_operand_aliasing={{}: (5, {})} | custom-call | tf_op jit(solution)/shard_map/merge/pallas_call | solution.py:212
  (44 shorter events, 0.6 us)
Async XLA Ops:
  2.4 4.8 %copy-start.1 = (bf16[2,64,512]{2,1,0:T(8,128)(2,1)S(1)}, bf16[2,64,512]{2,1,0:T(8,128)(2,1)}, u32[]{:S(2)}) copy-start(bf16[2,64,512]{2,1,0:T(8,128)(2,1)} %get-tuple-element.27) | copy-start | bytes 393220
  2.4 14.2 %collective-permute-start = (bf16[4,64,512]{2,1,0:T(8,128)(2,1)}, bf16[4,64,512]{2,1,0:T(8,128)(2,1)S(1)}, u32[]{:S(2)}, u32[]{:S(2)}) collective-permute-start(bf16[4,64,512]{2,1,0:T(8,128)(2,1)} %get-tuple-element.25), channel_id=1, source_target_pairs={{0,6},{1,7},{2,4},{3,5},{4,2},{5,3},{6,0},{7,1},{8,14},{9,15},{10,... | collective-permute-start | bytes 786440 | tf_op jit(solution)/shard_map/ppermute | solution.py:248
  6.4 1.6 %collective-permute-start.1 = (bf16[2,64,512]{2,1,0:T(8,128)(2,1)}, bf16[2,64,512]{2,1,0:T(8,128)(2,1)S(1)}, u32[]{:S(2)}, u32[]{:S(2)}) collective-permute-start(bf16[2,64,512]{2,1,0:T(8,128)(2,1)} %get-tuple-element.28), channel_id=1, source_target_pairs={{0,1},{1,0},{2,3},{3,2},{4,5},{5,4},{6,7},{7,6},{8,9},{9,8},{10,11... | collective-permute-start | bytes 393224 | tf_op jit(solution)/shard_map/ppermute | solution.py:248
  6.4 15.4 %collective-permute-start.7 = (bf16[4,64,512]{2,1,0:T(8,128)(2,1)}, bf16[4,64,512]{2,1,0:T(8,128)(2,1)S(1)}, u32[]{:S(2)}, u32[]{:S(2)}) collective-permute-start(bf16[4,64,512]{2,1,0:T(8,128)(2,1)} %get-tuple-element.35), channel_id=1, source_target_pairs={{0,4},{1,5},{2,6},{3,7},{4,0},{5,1},{6,2},{7,3},{8,12},{9,13},{10,... | collective-permute-start | bytes 786440 | tf_op jit(solution)/shard_map/ppermute | solution.py:248
  6.9 15.1 %collective-permute-start.4 = (bf16[5,64,512]{2,1,0:T(8,128)(2,1)}, bf16[5,64,512]{2,1,0:T(8,128)(2,1)S(1)}, u32[]{:S(2)}, u32[]{:S(2)}) collective-permute-start(bf16[5,64,512]{2,1,0:T(8,128)(2,1)} %get-tuple-element.31), channel_id=1, source_target_pairs={{0,2},{1,3},{2,0},{3,1},{4,6},{5,7},{6,4},{7,5},{8,10},{9,11},{10,... | collective-permute-start | bytes 983048 | tf_op jit(solution)/shard_map/ppermute | solution.py:248
  7.2 3.5 %copy-start = (bf16[5,64,512]{2,1,0:T(8,128)(2,1)S(1)}, bf16[5,64,512]{2,1,0:T(8,128)(2,1)}, u32[]{:S(2)}) copy-start(bf16[5,64,512]{2,1,0:T(8,128)(2,1)} %get-tuple-element.32.refs_1_.refs_3_.refs_2_) | copy-start | bytes 983044
  8.0 13.8 %collective-permute-start.2 = (bf16[2,64,512]{2,1,0:T(8,128)(2,1)S(1)}, bf16[2,64,512]{2,1,0:T(8,128)(2,1)S(1)}, u32[]{:S(2)}, u32[]{:S(2)}) collective-permute-start(bf16[2,64,512]{2,1,0:T(8,128)(2,1)S(1)} %pad_maximum_fusion.1), channel_id=1, source_target_pairs={{0,8},{1,11},{2,10},{3,9},{4,12},{5,15},{6,14},{7,13},{8,0},{9,3},... | collective-permute-start | bytes 393224 | tf_op jit(solution)/shard_map/ppermute | solution.py:252
  10.7 11.3 %collective-permute-start.5 = (bf16[5,64,512]{2,1,0:T(8,128)(2,1)S(1)}, bf16[5,64,512]{2,1,0:T(8,128)(2,1)S(1)}, u32[]{:S(2)}, u32[]{:S(2)}) collective-permute-start(bf16[5,64,512]{2,1,0:T(8,128)(2,1)S(1)} %copy-done), channel_id=1, source_target_pairs={{0,1},{1,0},{2,3},{3,2},{4,5},{5,4},{6,7},{7,6},{8,9},{9,8},{10,11... | collective-permute-start | bytes 983048 | tf_op jit(solution)/shard_map/ppermute | solution.py:248
  11.1 9.6 %copy-start.2 = (s32[16]{0:T(128)S(1)}, s32[16]{0:T(128)}, u32[]{:S(2)}) copy-start(s32[16]{0:T(128)} %param.12) | copy-start | bytes 196
  16.6 10.1 %collective-permute-start.11 = (bf16[2,64,512]{2,1,0:T(8,128)(2,1)S(1)}, bf16[2,64,512]{2,1,0:T(8,128)(2,1)S(1)}, u32[]{:S(2)}, u32[]{:S(2)}) collective-permute-start(bf16[2,64,512]{2,1,0:T(8,128)(2,1)S(1)} %pad_maximum_fusion), channel_id=1, source_target_pairs={{0,12},{1,15},{2,14},{3,13},{4,8},{5,11},{6,10},{7,9},{8,4},{9,7},... | collective-permute-start | bytes 393224 | tf_op jit(solution)/shard_map/ppermute | solution.py:252
  22.0 0.7 %copy-start.3 = (s32[16]{0:T(128)S(1)}, s32[16]{0:T(128)}, u32[]{:S(2)}) copy-start(s32[16]{0:T(128)} %param.13) | copy-start | bytes 196
  22.0 4.7 %collective-permute-start.9 = (bf16[4,64,512]{2,1,0:T(8,128)(2,1)S(1)}, bf16[4,64,512]{2,1,0:T(8,128)(2,1)S(1)}, u32[]{:S(2)}, u32[]{:S(2)}) collective-permute-start(bf16[4,64,512]{2,1,0:T(8,128)(2,1)S(1)} %collective-permute-done.refs_9_.refs_8_), channel_id=1, source_target_pairs={{0,1},{1,0},{2,3},{3,2},{4,5},{5,4},{6,7},{7,6},{8,9},{9,8},{10,11... | collective-permute-start | bytes 786440 | tf_op jit(solution)/shard_map/ppermute | solution.py:248
  22.1 4.6 %collective-permute-start.8 = (bf16[4,64,512]{2,1,0:T(8,128)(2,1)S(1)}, bf16[4,64,512]{2,1,0:T(8,128)(2,1)S(1)}, u32[]{:S(2)}, u32[]{:S(2)}) collective-permute-start(bf16[4,64,512]{2,1,0:T(8,128)(2,1)S(1)} %collective-permute-done.7.refs_7_.refs_6_), channel_id=1, source_target_pairs={{0,1},{1,0},{2,3},{3,2},{4,5},{5,4},{6,7},{7,6},{8,9},{9,8},{10,11... | collective-permute-start | bytes 786440 | tf_op jit(solution)/shard_map/ppermute | solution.py:248
  22.6 4.1 %collective-permute-start.6 = (bf16[5,64,512]{2,1,0:T(8,128)(2,1)S(1)}, bf16[5,64,512]{2,1,0:T(8,128)(2,1)S(1)}, u32[]{:S(2)}, u32[]{:S(2)}) collective-permute-start(bf16[5,64,512]{2,1,0:T(8,128)(2,1)S(1)} %collective-permute-done.4.refs_2_.refs_5_.refs_4_), channel_id=1, source_target_pairs={{0,1},{1,0},{2,3},{3,2},{4,5},{5,4},{6,7},{7,6},{8,9},{9,8},{10,11... | collective-permute-start | bytes 983048 | tf_op jit(solution)/shard_map/ppermute | solution.py:248
  23.0 9.9 %collective-permute-start.3 = (bf16[2,64,512]{2,1,0:T(8,128)(2,1)S(1)}, bf16[2,64,512]{2,1,0:T(8,128)(2,1)S(1)}, u32[]{:S(2)}, u32[]{:S(2)}) collective-permute-start(bf16[2,64,512]{2,1,0:T(8,128)(2,1)S(1)} %pad_maximum_fusion), channel_id=1, source_target_pairs={{0,4},{1,7},{2,6},{3,5},{4,0},{5,3},{6,2},{7,1},{8,12},{9,15},{10,... | collective-permute-start | bytes 393224 | tf_op jit(solution)/shard_map/ppermute | solution.py:252
  28.9 8.4 %collective-permute-start.16 = (bf16[2,272,128]{2,1,0:T(8,128)(2,1)S(1)}, bf16[2,272,128]{2,1,0:T(8,128)(2,1)S(1)}, u32[]{:S(2)}, u32[]{:S(2)}) collective-permute-start(bf16[2,272,128]{2,1,0:T(8,128)(2,1)S(1)} %get-tuple-element.44), channel_id=1, source_target_pairs={{0,12},{1,15},{2,14},{3,13},{4,8},{5,11},{6,10},{7,9},{8,4},{9,7},... | collective-permute-start | bytes 417800 | tf_op jit(solution)/shard_map/ppermute | solution.py:252
  35.1 8.2 %collective-permute-start.14 = (bf16[2,272,128]{2,1,0:T(8,128)(2,1)S(1)}, bf16[2,272,128]{2,1,0:T(8,128)(2,1)S(1)}, u32[]{:S(2)}, u32[]{:S(2)}) collective-permute-start(bf16[2,272,128]{2,1,0:T(8,128)(2,1)S(1)} %get-tuple-element.43), channel_id=1, source_target_pairs={{0,4},{1,7},{2,6},{3,5},{4,0},{5,3},{6,2},{7,1},{8,12},{9,15},{10,... | collective-permute-start | bytes 417800 | tf_op jit(solution)/shard_map/ppermute | solution.py:252
  35.1 10.3 %collective-permute-start.12 = (bf16[2,272,128]{2,1,0:T(8,128)(2,1)S(1)}, bf16[2,272,128]{2,1,0:T(8,128)(2,1)S(1)}, u32[]{:S(2)}, u32[]{:S(2)}) collective-permute-start(bf16[2,272,128]{2,1,0:T(8,128)(2,1)S(1)} %get-tuple-element.42), channel_id=1, source_target_pairs={{0,8},{1,11},{2,10},{3,9},{4,12},{5,15},{6,14},{7,13},{8,0},{9,3},... | collective-permute-start | bytes 417800 | tf_op jit(solution)/shard_map/ppermute | solution.py:252
  36.9 9.8 %collective-permute-start.10 = (bf16[1,272,128]{2,1,0:T(8,128)(2,1)S(1)}, bf16[1,272,128]{2,1,0:T(8,128)(2,1)S(1)}, u32[]{:S(2)}, u32[]{:S(2)}) collective-permute-start(bf16[1,272,128]{2,1,0:T(8,128)(2,1)S(1)} %get-tuple-element.41), channel_id=1, source_target_pairs={{0,2},{1,3},{2,0},{3,1},{4,6},{5,7},{6,4},{7,5},{8,10},{9,11},{10,... | collective-permute-start | bytes 208904 | tf_op jit(solution)/shard_map/ppermute | solution.py:248
  37.4 8.2 %collective-permute-start.17 = (bf16[1,272,128]{2,1,0:T(8,128)(2,1)S(1)}, bf16[1,272,128]{2,1,0:T(8,128)(2,1)S(1)}, u32[]{:S(2)}, u32[]{:S(2)}) collective-permute-start(bf16[1,272,128]{2,1,0:T(8,128)(2,1)S(1)} %get-tuple-element.49), channel_id=1, source_target_pairs={{0,1},{1,0},{2,3},{3,2},{4,5},{5,4},{6,7},{7,6},{8,9},{9,8},{10,11... | collective-permute-start | bytes 208904 | tf_op jit(solution)/shard_map/ppermute | solution.py:248
  43.4 2.2 %collective-permute-start.15 = (bf16[1,272,128]{2,1,0:T(8,128)(2,1)S(1)}, bf16[1,272,128]{2,1,0:T(8,128)(2,1)S(1)}, u32[]{:S(2)}, u32[]{:S(2)}) collective-permute-start(bf16[1,272,128]{2,1,0:T(8,128)(2,1)S(1)} %get-tuple-element.51), channel_id=1, source_target_pairs={{0,1},{1,0},{2,3},{3,2},{4,5},{5,4},{6,7},{7,6},{8,9},{9,8},{10,11... | collective-permute-start | bytes 208904 | tf_op jit(solution)/shard_map/ppermute | solution.py:248
  45.5 1.3 %collective-permute-start.13 = (bf16[1,272,128]{2,1,0:T(8,128)(2,1)S(1)}, bf16[1,272,128]{2,1,0:T(8,128)(2,1)S(1)}, u32[]{:S(2)}, u32[]{:S(2)}) collective-permute-start(bf16[1,272,128]{2,1,0:T(8,128)(2,1)S(1)} %get-tuple-element.53), channel_id=1, source_target_pairs={{0,1},{1,0},{2,3},{3,2},{4,5},{5,4},{6,7},{7,6},{8,9},{9,8},{10,11... | collective-permute-start | bytes 208904 | tf_op jit(solution)/shard_map/ppermute | solution.py:248

commit v6 on v5

--- a/solution.py
+++ b/solution.py
@@ -271,13 +271,13 @@
     }
     first_far = arrived[1, 0]
     for pair in range(1, pairs):
-        arrived[0, pair] = far_hop(after(payload[pair], first_far), 0, pair)
+        arrived[0, pair] = far_hop(payload[pair], 0, pair)
     keys = {}
     keys[0, 0] = blocks[0]
     keys[0, 1] = hop(after(blocks[0], other_mine), 0, 0, 1)
     for near in order[:-1]:
         keys[near, 0] = hop(blocks[near], 0, near)
-        keys[near, 1] = hop(after(after(keys[near, 0], first_far), keys[0, 1]), 0, 0, 1)
+        keys[near, 1] = hop(after(keys[near, 0], first_far), 0, 0, 1)
     starts_later = after(patch_starts, keys[order[0], 0])
     key_rank = ranks([(0, near, side) for near in range(members) for side in range(CORES)])
     key_blocks = [keys[near, side] for near in range(members) for side in range(CORES)]

time: 48 us -> 47.5 us (0.990)
  starting transfers between devices: 22 us -> 18.9 us
  waiting for transfers between devices: 15.6 us -> 17.7 us
  local copies, waits for them, and re-layouts: 0.41 us -> 0.91 us
    ppermute x6, starting transfers between devices: 15.9 us -> 12.5 us  [far_hop(): lax.ppermute(array, 'tok', [(i, i ^ flips[i]) for i in range(devices)])]
    ppermute x6, waiting for transfers between devices: 9.38 us -> 11.5 us  [far_hop(): lax.ppermute(array, 'tok', [(i, i ^ flips[i]) for i in range(devices)])]
    unnamed x8, local copies, waits for them, and re-layouts: 0.02 us -> 0.51 us
  transfers between devices with their start and end apart: 18 -> 18, of which waited for: 7 -> 8; matrix products, arithmetic and copies ran while one was open for 2% -> 2% of each run, Pallas kernels for 11% -> 12%
where the time goes in v6:
time: 47.5 us; the launch traced here: 47.4 us
  starting transfers between devices  18.9 us (40%)
  waiting for transfers between devices  17.7 us (37%)
  Pallas kernels  8.93 us (19%)
  local copies, waits for them, and re-layouts  0.91 us (2%)
  other arithmetic  0.68 us (1%)
    ppermute x6, starting transfers between devices, far_hop(): lax.ppermute(array, 'tok', [(i, i ^ flips[i]) for i in range(devices)])  12.5 us
    ppermute x6, waiting for transfers between devices, far_hop(): lax.ppermute(array, 'tok', [(i, i ^ flips[i]) for i in range(devices)])  11.5 us
    ppermute x12, starting transfers between devices, hop(): return lax.ppermute(array, 'tok', [(i, i ^ flip) for i in range(devices)])  6.4 us
    ppermute x12, waiting for transfers between devices, hop(): return lax.ppermute(array, 'tok', [(i, i ^ flip) for i in range(devices)])  6.19 us
    pallas_call x2, Pallas kernels, attend(): pl.pallas_call(functools.partial(attend_kernel, picks, len(arrays), block...  4.42 us
    pallas_call x1, Pallas kernels, split_columns(): pl.pallas_call(functools.partial(split_kernel, members, width), out_shape...  2.39 us
    pallas_call x2, Pallas kernels, merge(): pl.pallas_call(functools.partial(merge_kernel, chosen, parts, members, he...  2.13 us
  transfers between devices with their start and end apart: 18, of which 8 were waited for; matrix products, arithmetic and copies ran while one was open for 2% of the time, Pallas kernels for 12%

profile of v6, /device:TPU:0, one launch (start us, length us, event | category | flops | bytes accessed | tf_op | source)
XLA Modules:
  0.0 47.4 jit_solution(6131206004933717621)
XLA Ops:
  0.0 2.4 %split_columns.1 = (bf16[5,64,512]{2,1,0:T(8,128)(2,1)}, bf16[5,64,512]{2,1,0:T(8,128)(2,1)}, bf16[4,64,512]{2,1,0:T(8,128)(2,1)}, bf16[4,64,512]{2,1,0:T(8,128)...) custom-call(s32[1]{0:T(128)} %bitcast.where, bf16[64,2048]{1,0:T(8,128)(2,1)} %queries.1, ...), custom_call_target="tpu_custom_call" | custom-call | bytes 2621440 | tf_op jit(solution)/shard_map/split_columns/pallas_call | solution.py:77
  2.4 4.0 %collective-permute-start = (bf16[4,64,512]{2,1,0:T(8,128)(2,1)}, bf16[4,64,512]{2,1,0:T(8,128)(2,1)S(1)}, u32[]{:S(2)}, u32[]{:S(2)}) collective-permute-start(bf16[4,64,512]{2,1,0:T(8,128)(2,1)} %get-tuple-element.21), channel_id=1, source_target_pairs={{0,6},{1,7},{2,4},{3,5},{4,2},{5,3},{6,0},{7,1},{8,14},{9,15},{10,... | collective-permute-start | bytes 786440 | tf_op jit(solution)/shard_map/ppermute | solution.py:248
  6.4 0.4 collective-permute-start.7
  6.9 0.3 collective-permute-start.3
  7.5 0.5 %collective-permute-done.1 = bf16[2,64,512]{2,1,0:T(8,128)(2,1)S(1)} collective-permute-done((bf16[2,64,512]{2,1,0:T(8,128)(2,1)}, bf16[2,64,512]{2,1,0:T(8,128)(2,1)S(1)}, u32[]{:S(2)}, u32[]{:S(2)}) %collective-permute-start.1) | collective-permute-done | bytes 131104 | tf_op jit(solution)/shard_map/ppermute | solution.py:248
  8.0 2.7 %collective-permute-start.5 = (bf16[2,64,512]{2,1,0:T(8,128)(2,1)S(1)}, bf16[2,64,512]{2,1,0:T(8,128)(2,1)S(1)}, u32[]{:S(2)}, u32[]{:S(2)}) collective-permute-start(bf16[2,64,512]{2,1,0:T(8,128)(2,1)S(1)} %pad_maximum_fusion.1), channel_id=1, source_target_pairs={{0,8},{1,11},{2,10},{3,9},{4,12},{5,15},{6,14},{7,13},{8,0},{9,3},... | collective-permute-start | bytes 393224 | tf_op jit(solution)/shard_map/ppermute | solution.py:252
  10.7 0.4 collective-permute-start.4
  11.1 5.5 %collective-permute-done.refs_9_.refs_8_ = bf16[4,64,512]{2,1,0:T(8,128)(2,1)S(1)} collective-permute-done((bf16[4,64,512]{2,1,0:T(8,128)(2,1)}, bf16[4,64,512]{2,1,0:T(8,128)(2,1)S(1)}, u32[]{:S(2)}, u32[]{:S(2)}) %collective-permute-start) | collective-permute-done | bytes 262176 | tf_op jit(solution)/shard_map/ppermute | solution.py:248
  16.6 4.1 %collective-permute-start.11 = (bf16[2,64,512]{2,1,0:T(8,128)(2,1)S(1)}, bf16[2,64,512]{2,1,0:T(8,128)(2,1)S(1)}, u32[]{:S(2)}, u32[]{:S(2)}) collective-permute-start(bf16[2,64,512]{2,1,0:T(8,128)(2,1)S(1)} %pad_maximum_fusion), channel_id=1, source_target_pairs={{0,12},{1,15},{2,14},{3,13},{4,8},{5,11},{6,10},{7,9},{8,4},{9,7},... | collective-permute-start | bytes 393224 | tf_op jit(solution)/shard_map/ppermute | solution.py:252
  20.8 1.1 %collective-permute-done.5.refs_0_ = bf16[2,64,512]{2,1,0:T(8,128)(2,1)S(1)} collective-permute-done((bf16[2,64,512]{2,1,0:T(8,128)(2,1)S(1)}, bf16[2,64,512]{2,1,0:T(8,128)(2,1)S(1)}, u32[]{:S(2)}, u32[]{:S(2)}) %collective-permute-start.5) | collective-permute-done | bytes 131104 | tf_op jit(solution)/shard_map/ppermute | solution.py:252
  21.9 0.5 %collective-permute-start.8 = (bf16[4,64,512]{2,1,0:T(8,128)(2,1)S(1)}, bf16[4,64,512]{2,1,0:T(8,128)(2,1)S(1)}, u32[]{:S(2)}, u32[]{:S(2)}) collective-permute-start(bf16[4,64,512]{2,1,0:T(8,128)(2,1)S(1)} %collective-permute-done.7.refs_7_.refs_6_), channel_id=1, source_target_pairs={{0,1},{1,0},{2,3},{3,2},{4,5},{5,4},{6,7},{7,6},{8,9},{9,8},{10,11... | collective-permute-start | bytes 786440 | tf_op jit(solution)/shard_map/ppermute | solution.py:248
  22.5 0.1 collective-permute-start.6
  22.6 0.5 %copy-done.3 = s32[16]{0:T(128)S(1)} copy-done((s32[16]{0:T(128)S(1)}, s32[16]{0:T(128)}, u32[]{:S(2)}) %copy-start.3) | copy-done | bytes 88
  23.2 0.1 select_reduce_fusion.1
  23.3 0.1 copy.12.query_rank
  23.4 0.1 select_reduce_fusion
  23.5 3.0 %collective-permute-done.11.refs_1_ = bf16[2,64,512]{2,1,0:T(8,128)(2,1)S(1)} collective-permute-done((bf16[2,64,512]{2,1,0:T(8,128)(2,1)S(1)}, bf16[2,64,512]{2,1,0:T(8,128)(2,1)S(1)}, u32[]{:S(2)}, u32[]{:S(2)}) %collective-permute-start.11) | collective-permute-done | bytes 131104 | tf_op jit(solution)/shard_map/ppermute | solution.py:252
  26.5 1.1 %collective-permute-start.2 = (bf16[2,64,512]{2,1,0:T(8,128)(2,1)S(1)}, bf16[2,64,512]{2,1,0:T(8,128)(2,1)S(1)}, u32[]{:S(2)}, u32[]{:S(2)}) collective-permute-start(bf16[2,64,512]{2,1,0:T(8,128)(2,1)S(1)} %pad_maximum_fusion), channel_id=1, source_target_pairs={{0,4},{1,7},{2,6},{3,5},{4,0},{5,3},{6,2},{7,1},{8,12},{9,15},{10,... | collective-permute-start | bytes 393224 | tf_op jit(solution)/shard_map/ppermute | solution.py:252
  27.6 2.2 %attend.3 = (bf16[2,272,128]{2,1,0:T(8,128)(2,1)S(1)}, bf16[2,272,128]{2,1,0:T(8,128)(2,1)S(1)}) custom-call(s32[1,512]{1,0:T(1,128)S(1)} %bitcast.4, s32[256,1]{1,0:T(8,128)S(1)} %copy.12.query_rank, bf16[2,64,512]{2,1,0:T(8,128)(2,1)S(1)} %collective-permute-done.5.refs_0_, bf16[2,64,512]{2,1,0:T(8,128)(2,1)S(1)} %collective-permute-done.11.refs_1_, ...), custom_call_target="tpu_custom_call" | custom-call | flops 536870912 | bytes 2621440 | tf_op jit(solution)/shard_map/attend/pallas_call | solution.py:146
  29.9 2.3 %collective-permute-start.16 = (bf16[2,272,128]{2,1,0:T(8,128)(2,1)S(1)}, bf16[2,272,128]{2,1,0:T(8,128)(2,1)S(1)}, u32[]{:S(2)}, u32[]{:S(2)}) collective-permute-start(bf16[2,272,128]{2,1,0:T(8,128)(2,1)S(1)} %get-tuple-element.36), channel_id=1, source_target_pairs={{0,12},{1,15},{2,14},{3,13},{4,8},{5,11},{6,10},{7,9},{8,4},{9,7},... | collective-permute-start | bytes 417800 | tf_op jit(solution)/shard_map/ppermute | solution.py:252
  32.2 0.1 copy.11.query_rank
  32.3 2.2 %attend.2 = (bf16[2,272,128]{2,1,0:T(8,128)(2,1)S(1)}, bf16[1,272,128]{2,1,0:T(8,128)(2,1)S(1)}, bf16[1,272,128]{2,1,0:T(8,128)(2,1)S(1)}) custom-call(s32[1,512]{1,0:T(1,128)S(1)} %bitcast.5, s32[256,1]{1,0:T(8,128)S(1)} %copy.11.query_rank, bf16[2,64,512]{2,1,0:T(8,128)(2,1)S(1)} %collective-permute-done.2.refs_0_, bf16[5,64,512]{2,1,0:T(8,128)(2,1)S(1)} %copy-done, ...), custom_call_target="tpu_custom_call" | custom-call | flops 536870912 | bytes 2621440 | tf_op jit(solution)/shard_map/attend/pallas_call | solution.py:146
  34.6 0.4 collective-permute-start.14
  34.9 2.0 %collective-permute-start.12 = (bf16[2,272,128]{2,1,0:T(8,128)(2,1)S(1)}, bf16[2,272,128]{2,1,0:T(8,128)(2,1)S(1)}, u32[]{:S(2)}, u32[]{:S(2)}) collective-permute-start(bf16[2,272,128]{2,1,0:T(8,128)(2,1)S(1)} %get-tuple-element.34), channel_id=1, source_target_pairs={{0,8},{1,11},{2,10},{3,9},{4,12},{5,15},{6,14},{7,13},{8,0},{9,3},... | collective-permute-start | bytes 417800 | tf_op jit(solution)/shard_map/ppermute | solution.py:252
  37.0 0.2 collective-permute-start.10
  37.1 0.4 collective-permute-done.16
  37.6 0.3 collective-permute-start.17
  37.9 5.0 %collective-permute-done.14 = bf16[2,272,128]{2,1,0:T(8,128)(2,1)S(1)} collective-permute-done((bf16[2,272,128]{2,1,0:T(8,128)(2,1)S(1)}, bf16[2,272,128]{2,1,0:T(8,128)(2,1)S(1)}, u32[]{:S(2)}, u32[]{:S(2)}) %collective-permute-start.14) | collective-permute-done | bytes 139296 | tf_op jit(solution)/shard_map/ppermute | solution.py:252
  43.0 2.0 %collective-permute-done.12 = bf16[2,272,128]{2,1,0:T(8,128)(2,1)S(1)} collective-permute-done((bf16[2,272,128]{2,1,0:T(8,128)(2,1)S(1)}, bf16[2,272,128]{2,1,0:T(8,128)(2,1)S(1)}, u32[]{:S(2)}, u32[]{:S(2)}) %collective-permute-start.12) | collective-permute-done | bytes 139296 | tf_op jit(solution)/shard_map/ppermute | solution.py:252
  45.1 1.1 %merge.2.refs_4_ = bf16[64,2048]{1,0:T(8,128)(2,1)} custom-call(s32[1]{0:T(128)} %bitcast.where, bf16[1,272,128]{2,1,0:T(8,128)(2,1)S(1)} %get-tuple-element.44.refs_0_, bf16[1,272,128]{2,1,0:T(8,128)(2,1)S(1)} %collective-permute-done.15.refs_1_, bf16[1,272,128]{2,1,0:T(8,128)(2,1)S(1)} %get-tuple-element.42.refs_2_, ...), custom_call_target="tpu_custom_call" | custom-call | tf_op jit(solution)/shard_map/merge/pallas_call | solution.py:212
  46.2 0.1 collective-permute-done.13.refs_3_
  46.3 1.1 %merge.3 = bf16[64,2048]{1,0:T(8,128)(2,1)} custom-call(s32[1]{0:T(128)} %bitcast.where, bf16[1,272,128]{2,1,0:T(8,128)(2,1)S(1)} %get-tuple-element.32.refs_0_, bf16[1,272,128]{2,1,0:T(8,128)(2,1)S(1)} %collective-permute-done.10.refs_1_, bf16[1,272,128]{2,1,0:T(8,128)(2,1)S(1)} %get-tuple-element.46.refs_2_, ...), custom_call_target="tpu_custom_call", output_to_operand_aliasing={{}: (5, {})} | custom-call | tf_op jit(solution)/shard_map/merge/pallas_call | solution.py:212
  (44 shorter events, 0.8 us)
Async XLA Ops:
  2.4 4.8 %copy-start.1 = (bf16[2,64,512]{2,1,0:T(8,128)(2,1)S(1)}, bf16[2,64,512]{2,1,0:T(8,128)(2,1)}, u32[]{:S(2)}) copy-start(bf16[2,64,512]{2,1,0:T(8,128)(2,1)} %get-tuple-element.23) | copy-start | bytes 393220
  2.4 14.2 %collective-permute-start = (bf16[4,64,512]{2,1,0:T(8,128)(2,1)}, bf16[4,64,512]{2,1,0:T(8,128)(2,1)S(1)}, u32[]{:S(2)}, u32[]{:S(2)}) collective-permute-start(bf16[4,64,512]{2,1,0:T(8,128)(2,1)} %get-tuple-element.21), channel_id=1, source_target_pairs={{0,6},{1,7},{2,4},{3,5},{4,2},{5,3},{6,0},{7,1},{8,14},{9,15},{10,... | collective-permute-start | bytes 786440 | tf_op jit(solution)/shard_map/ppermute | solution.py:248
  6.4 1.6 %collective-permute-start.1 = (bf16[2,64,512]{2,1,0:T(8,128)(2,1)}, bf16[2,64,512]{2,1,0:T(8,128)(2,1)S(1)}, u32[]{:S(2)}, u32[]{:S(2)}) collective-permute-start(bf16[2,64,512]{2,1,0:T(8,128)(2,1)} %get-tuple-element.24), channel_id=1, source_target_pairs={{0,1},{1,0},{2,3},{3,2},{4,5},{5,4},{6,7},{7,6},{8,9},{9,8},{10,11... | collective-permute-start | bytes 393224 | tf_op jit(solution)/shard_map/ppermute | solution.py:248
  6.4 15.4 %collective-permute-start.7 = (bf16[4,64,512]{2,1,0:T(8,128)(2,1)}, bf16[4,64,512]{2,1,0:T(8,128)(2,1)S(1)}, u32[]{:S(2)}, u32[]{:S(2)}) collective-permute-start(bf16[4,64,512]{2,1,0:T(8,128)(2,1)} %get-tuple-element.29), channel_id=1, source_target_pairs={{0,4},{1,5},{2,6},{3,7},{4,0},{5,1},{6,2},{7,3},{8,12},{9,13},{10,... | collective-permute-start | bytes 786440 | tf_op jit(solution)/shard_map/ppermute | solution.py:248
  6.9 15.6 %collective-permute-start.3 = (bf16[5,64,512]{2,1,0:T(8,128)(2,1)}, bf16[5,64,512]{2,1,0:T(8,128)(2,1)S(1)}, u32[]{:S(2)}, u32[]{:S(2)}) collective-permute-start(bf16[5,64,512]{2,1,0:T(8,128)(2,1)} %get-tuple-element.26), channel_id=1, source_target_pairs={{0,2},{1,3},{2,0},{3,1},{4,6},{5,7},{6,4},{7,5},{8,10},{9,11},{10,... | collective-permute-start | bytes 983048 | tf_op jit(solution)/shard_map/ppermute | solution.py:248
  7.2 3.5 %copy-start = (bf16[5,64,512]{2,1,0:T(8,128)(2,1)S(1)}, bf16[5,64,512]{2,1,0:T(8,128)(2,1)}, u32[]{:S(2)}) copy-start(bf16[5,64,512]{2,1,0:T(8,128)(2,1)} %get-tuple-element.27.refs_1_.refs_3_.refs_2_) | copy-start | bytes 983044
  8.0 13.8 %collective-permute-start.5 = (bf16[2,64,512]{2,1,0:T(8,128)(2,1)S(1)}, bf16[2,64,512]{2,1,0:T(8,128)(2,1)S(1)}, u32[]{:S(2)}, u32[]{:S(2)}) collective-permute-start(bf16[2,64,512]{2,1,0:T(8,128)(2,1)S(1)} %pad_maximum_fusion.1), channel_id=1, source_target_pairs={{0,8},{1,11},{2,10},{3,9},{4,12},{5,15},{6,14},{7,13},{8,0},{9,3},... | collective-permute-start | bytes 393224 | tf_op jit(solution)/shard_map/ppermute | solution.py:252
  10.7 17.0 %collective-permute-start.4 = (bf16[5,64,512]{2,1,0:T(8,128)(2,1)S(1)}, bf16[5,64,512]{2,1,0:T(8,128)(2,1)S(1)}, u32[]{:S(2)}, u32[]{:S(2)}) collective-permute-start(bf16[5,64,512]{2,1,0:T(8,128)(2,1)S(1)} %copy-done), channel_id=1, source_target_pairs={{0,1},{1,0},{2,3},{3,2},{4,5},{5,4},{6,7},{7,6},{8,9},{9,8},{10,11... | collective-permute-start | bytes 983048 | tf_op jit(solution)/shard_map/ppermute | solution.py:248
  11.1 9.6 %copy-start.2 = (s32[16]{0:T(128)S(1)}, s32[16]{0:T(128)}, u32[]{:S(2)}) copy-start(s32[16]{0:T(128)} %param.12) | copy-start | bytes 196
  16.6 9.9 %collective-permute-start.11 = (bf16[2,64,512]{2,1,0:T(8,128)(2,1)S(1)}, bf16[2,64,512]{2,1,0:T(8,128)(2,1)S(1)}, u32[]{:S(2)}, u32[]{:S(2)}) collective-permute-start(bf16[2,64,512]{2,1,0:T(8,128)(2,1)S(1)} %pad_maximum_fusion), channel_id=1, source_target_pairs={{0,12},{1,15},{2,14},{3,13},{4,8},{5,11},{6,10},{7,9},{8,4},{9,7},... | collective-permute-start | bytes 393224 | tf_op jit(solution)/shard_map/ppermute | solution.py:252
  21.9 5.8 %collective-permute-start.9 = (bf16[4,64,512]{2,1,0:T(8,128)(2,1)S(1)}, bf16[4,64,512]{2,1,0:T(8,128)(2,1)S(1)}, u32[]{:S(2)}, u32[]{:S(2)}) collective-permute-start(bf16[4,64,512]{2,1,0:T(8,128)(2,1)S(1)} %collective-permute-done.refs_9_.refs_8_), channel_id=1, source_target_pairs={{0,1},{1,0},{2,3},{3,2},{4,5},{5,4},{6,7},{7,6},{8,9},{9,8},{10,11... | collective-permute-start | bytes 786440 | tf_op jit(solution)/shard_map/ppermute | solution.py:248
  21.9 5.8 %collective-permute-start.8 = (bf16[4,64,512]{2,1,0:T(8,128)(2,1)S(1)}, bf16[4,64,512]{2,1,0:T(8,128)(2,1)S(1)}, u32[]{:S(2)}, u32[]{:S(2)}) collective-permute-start(bf16[4,64,512]{2,1,0:T(8,128)(2,1)S(1)} %collective-permute-done.7.refs_7_.refs_6_), channel_id=1, source_target_pairs={{0,1},{1,0},{2,3},{3,2},{4,5},{5,4},{6,7},{7,6},{8,9},{9,8},{10,11... | collective-permute-start | bytes 786440 | tf_op jit(solution)/shard_map/ppermute | solution.py:248
  22.5 0.7 %copy-start.3 = (s32[16]{0:T(128)S(1)}, s32[16]{0:T(128)}, u32[]{:S(2)}) copy-start(s32[16]{0:T(128)} %param.13) | copy-start | bytes 196
  22.5 5.2 %collective-permute-start.6 = (bf16[5,64,512]{2,1,0:T(8,128)(2,1)S(1)}, bf16[5,64,512]{2,1,0:T(8,128)(2,1)S(1)}, u32[]{:S(2)}, u32[]{:S(2)}) collective-permute-start(bf16[5,64,512]{2,1,0:T(8,128)(2,1)S(1)} %collective-permute-done.3.refs_2_.refs_5_.refs_4_), channel_id=1, source_target_pairs={{0,1},{1,0},{2,3},{3,2},{4,5},{5,4},{6,7},{7,6},{8,9},{9,8},{10,11... | collective-permute-start | bytes 983048 | tf_op jit(solution)/shard_map/ppermute | solution.py:248
  26.5 5.8 %collective-permute-start.2 = (bf16[2,64,512]{2,1,0:T(8,128)(2,1)S(1)}, bf16[2,64,512]{2,1,0:T(8,128)(2,1)S(1)}, u32[]{:S(2)}, u32[]{:S(2)}) collective-permute-start(bf16[2,64,512]{2,1,0:T(8,128)(2,1)S(1)} %pad_maximum_fusion), channel_id=1, source_target_pairs={{0,4},{1,7},{2,6},{3,5},{4,0},{5,3},{6,2},{7,1},{8,12},{9,15},{10,... | collective-permute-start | bytes 393224 | tf_op jit(solution)/shard_map/ppermute | solution.py:252
  29.9 7.7 %collective-permute-start.16 = (bf16[2,272,128]{2,1,0:T(8,128)(2,1)S(1)}, bf16[2,272,128]{2,1,0:T(8,128)(2,1)S(1)}, u32[]{:S(2)}, u32[]{:S(2)}) collective-permute-start(bf16[2,272,128]{2,1,0:T(8,128)(2,1)S(1)} %get-tuple-element.36), channel_id=1, source_target_pairs={{0,12},{1,15},{2,14},{3,13},{4,8},{5,11},{6,10},{7,9},{8,4},{9,7},... | collective-permute-start | bytes 417800 | tf_op jit(solution)/shard_map/ppermute | solution.py:252
  34.6 8.3 %collective-permute-start.14 = (bf16[2,272,128]{2,1,0:T(8,128)(2,1)S(1)}, bf16[2,272,128]{2,1,0:T(8,128)(2,1)S(1)}, u32[]{:S(2)}, u32[]{:S(2)}) collective-permute-start(bf16[2,272,128]{2,1,0:T(8,128)(2,1)S(1)} %get-tuple-element.35), channel_id=1, source_target_pairs={{0,4},{1,7},{2,6},{3,5},{4,0},{5,3},{6,2},{7,1},{8,12},{9,15},{10,... | collective-permute-start | bytes 417800 | tf_op jit(solution)/shard_map/ppermute | solution.py:252
  34.9 10.0 %collective-permute-start.12 = (bf16[2,272,128]{2,1,0:T(8,128)(2,1)S(1)}, bf16[2,272,128]{2,1,0:T(8,128)(2,1)S(1)}, u32[]{:S(2)}, u32[]{:S(2)}) collective-permute-start(bf16[2,272,128]{2,1,0:T(8,128)(2,1)S(1)} %get-tuple-element.34), channel_id=1, source_target_pairs={{0,8},{1,11},{2,10},{3,9},{4,12},{5,15},{6,14},{7,13},{8,0},{9,3},... | collective-permute-start | bytes 417800 | tf_op jit(solution)/shard_map/ppermute | solution.py:252
  37.0 9.2 %collective-permute-start.10 = (bf16[1,272,128]{2,1,0:T(8,128)(2,1)S(1)}, bf16[1,272,128]{2,1,0:T(8,128)(2,1)S(1)}, u32[]{:S(2)}, u32[]{:S(2)}) collective-permute-start(bf16[1,272,128]{2,1,0:T(8,128)(2,1)S(1)} %get-tuple-element.33), channel_id=1, source_target_pairs={{0,2},{1,3},{2,0},{3,1},{4,6},{5,7},{6,4},{7,5},{8,10},{9,11},{10,... | collective-permute-start | bytes 208904 | tf_op jit(solution)/shard_map/ppermute | solution.py:248
  37.6 7.5 %collective-permute-start.17 = (bf16[1,272,128]{2,1,0:T(8,128)(2,1)S(1)}, bf16[1,272,128]{2,1,0:T(8,128)(2,1)S(1)}, u32[]{:S(2)}, u32[]{:S(2)}) collective-permute-start(bf16[1,272,128]{2,1,0:T(8,128)(2,1)S(1)} %get-tuple-element.41), channel_id=1, source_target_pairs={{0,1},{1,0},{2,3},{3,2},{4,5},{5,4},{6,7},{7,6},{8,9},{9,8},{10,11... | collective-permute-start | bytes 208904 | tf_op jit(solution)/shard_map/ppermute | solution.py:248
  42.9 2.2 %collective-permute-start.15 = (bf16[1,272,128]{2,1,0:T(8,128)(2,1)S(1)}, bf16[1,272,128]{2,1,0:T(8,128)(2,1)S(1)}, u32[]{:S(2)}, u32[]{:S(2)}) collective-permute-start(bf16[1,272,128]{2,1,0:T(8,128)(2,1)S(1)} %get-tuple-element.43), channel_id=1, source_target_pairs={{0,1},{1,0},{2,3},{3,2},{4,5},{5,4},{6,7},{7,6},{8,9},{9,8},{10,11... | collective-permute-start | bytes 208904 | tf_op jit(solution)/shard_map/ppermute | solution.py:248
  45.0 1.3 %collective-permute-start.13 = (bf16[1,272,128]{2,1,0:T(8,128)(2,1)S(1)}, bf16[1,272,128]{2,1,0:T(8,128)(2,1)S(1)}, u32[]{:S(2)}, u32[]{:S(2)}) collective-permute-start(bf16[1,272,128]{2,1,0:T(8,128)(2,1)S(1)} %get-tuple-element.45), channel_id=1, source_target_pairs={{0,1},{1,0},{2,3},{3,2},{4,5},{5,4},{6,7},{7,6},{8,9},{9,8},{10,11... | collective-permute-start | bytes 208904 | tf_op jit(solution)/shard_map/ppermute | solution.py:248

commit v7 on v6

--- a/solution.py
+++ b/solution.py
@@ -277,7 +277,7 @@
     keys[0, 1] = hop(after(blocks[0], other_mine), 0, 0, 1)
     for near in order[:-1]:
         keys[near, 0] = hop(blocks[near], 0, near)
-        keys[near, 1] = hop(after(keys[near, 0], first_far), 0, 0, 1)
+        keys[near, 1] = hop(after(after(keys[near, 0], first_far), keys[0, 1]), 0, 0, 1)
     starts_later = after(patch_starts, keys[order[0], 0])
     key_rank = ranks([(0, near, side) for near in range(members) for side in range(CORES)])
     key_blocks = [keys[near, side] for near in range(members) for side in range(CORES)]

time: 47.5 us -> 52 us (1.095)
  waiting for transfers between devices: 17.7 us -> 22.7 us
    ppermute x6, waiting for transfers between devices: 11.5 us -> 17.1 us  [far_hop(): lax.ppermute(array, 'tok', [(i, i ^ flips[i]) for i in range(devices)])]
    ppermute x6, starting transfers between devices: 12.5 us -> 11.8 us  [far_hop(): lax.ppermute(array, 'tok', [(i, i ^ flips[i]) for i in range(devices)])]
    ppermute x12, starting transfers between devices: 6.4 us -> 7.11 us  [hop(): return lax.ppermute(array, 'tok', [(i, i ^ flip) for i in range(devices)])]
    ppermute x12, waiting for transfers between devices: 6.19 us -> 5.65 us  [hop(): return lax.ppermute(array, 'tok', [(i, i ^ flip) for i in range(devices)])]
  transfers between devices with their start and end apart: 18 -> 18, of which waited for: 8 -> 9; matrix products, arithmetic and copies ran while one was open for 2% -> 2% of each run, Pallas kernels for 12% -> 11%
where the time goes in v7:
time: 52 us; the launch traced here: 51.9 us
  waiting for transfers between devices  22.7 us (44%)
  starting transfers between devices  18.9 us (36%)
  Pallas kernels  8.93 us (17%)
  other arithmetic  0.68 us (1%)
    ppermute x6, waiting for transfers between devices, far_hop(): lax.ppermute(array, 'tok', [(i, i ^ flips[i]) for i in range(devices)])  17.1 us
    ppermute x6, starting transfers between devices, far_hop(): lax.ppermute(array, 'tok', [(i, i ^ flips[i]) for i in range(devices)])  11.8 us
    ppermute x12, starting transfers between devices, hop(): return lax.ppermute(array, 'tok', [(i, i ^ flip) for i in range(devices)])  7.11 us
    ppermute x12, waiting for transfers between devices, hop(): return lax.ppermute(array, 'tok', [(i, i ^ flip) for i in range(devices)])  5.65 us
    pallas_call x2, Pallas kernels, attend(): pl.pallas_call(functools.partial(attend_kernel, picks, len(arrays), block...  4.41 us
    pallas_call x1, Pallas kernels, split_columns(): pl.pallas_call(functools.partial(split_kernel, members, width), out_shape...  2.39 us
    pallas_call x2, Pallas kernels, merge(): pl.pallas_call(functools.partial(merge_kernel, chosen, parts, members, he...  2.13 us
  transfers between devices with their start and end apart: 18, of which 9 were waited for; matrix products, arithmetic and copies ran while one was open for 2% of the time, Pallas kernels for 11%

profile of v7, /device:TPU:0, one launch (start us, length us, event | category | flops | bytes accessed | tf_op | source)
XLA Modules:
  0.0 51.9 jit_solution(4613952143064134079)
XLA Ops:
  0.0 2.4 %split_columns.1 = (bf16[5,64,512]{2,1,0:T(8,128)(2,1)}, bf16[5,64,512]{2,1,0:T(8,128)(2,1)}, bf16[4,64,512]{2,1,0:T(8,128)(2,1)}, bf16[4,64,512]{2,1,0:T(8,128)...) custom-call(s32[1]{0:T(128)} %bitcast.where, bf16[64,2048]{1,0:T(8,128)(2,1)} %queries.1, ...), custom_call_target="tpu_custom_call" | custom-call | bytes 2621440 | tf_op jit(solution)/shard_map/split_columns/pallas_call | solution.py:77
  2.4 4.0 %collective-permute-start = (bf16[4,64,512]{2,1,0:T(8,128)(2,1)}, bf16[4,64,512]{2,1,0:T(8,128)(2,1)S(1)}, u32[]{:S(2)}, u32[]{:S(2)}) collective-permute-start(bf16[4,64,512]{2,1,0:T(8,128)(2,1)} %get-tuple-element.24), channel_id=1, source_target_pairs={{0,6},{1,7},{2,4},{3,5},{4,2},{5,3},{6,0},{7,1},{8,14},{9,15},{10,... | collective-permute-start | bytes 786440 | tf_op jit(solution)/shard_map/ppermute | solution.py:248
  6.4 0.4 collective-permute-start.7
  6.9 0.3 collective-permute-start.3
  7.5 0.5 collective-permute-done.1
  8.0 3.4 %collective-permute-start.11 = (bf16[2,64,512]{2,1,0:T(8,128)(2,1)S(1)}, bf16[2,64,512]{2,1,0:T(8,128)(2,1)S(1)}, u32[]{:S(2)}, u32[]{:S(2)}) collective-permute-start(bf16[2,64,512]{2,1,0:T(8,128)(2,1)S(1)} %pad_maximum_fusion), channel_id=1, source_target_pairs={{0,12},{1,15},{2,14},{3,13},{4,8},{5,11},{6,10},{7,9},{8,4},{9,7},... | collective-permute-start | bytes 393224 | tf_op jit(solution)/shard_map/ppermute | solution.py:252
  11.5 2.3 %collective-permute-done.refs_9_.refs_8_ = bf16[4,64,512]{2,1,0:T(8,128)(2,1)S(1)} collective-permute-done((bf16[4,64,512]{2,1,0:T(8,128)(2,1)}, bf16[4,64,512]{2,1,0:T(8,128)(2,1)S(1)}, u32[]{:S(2)}, u32[]{:S(2)}) %collective-permute-start) | collective-permute-done | bytes 262176 | tf_op jit(solution)/shard_map/ppermute | solution.py:248
  13.8 3.4 %collective-permute-start.5 = (bf16[2,64,512]{2,1,0:T(8,128)(2,1)S(1)}, bf16[2,64,512]{2,1,0:T(8,128)(2,1)S(1)}, u32[]{:S(2)}, u32[]{:S(2)}) collective-permute-start(bf16[2,64,512]{2,1,0:T(8,128)(2,1)S(1)} %pad_maximum_fusion.1), channel_id=1, source_target_pairs={{0,8},{1,11},{2,10},{3,9},{4,12},{5,15},{6,14},{7,13},{8,0},{9,3},... | collective-permute-start | bytes 393224 | tf_op jit(solution)/shard_map/ppermute | solution.py:252
  17.3 9.0 %collective-permute-done.5.refs_0_ = bf16[2,64,512]{2,1,0:T(8,128)(2,1)S(1)} collective-permute-done((bf16[2,64,512]{2,1,0:T(8,128)(2,1)S(1)}, bf16[2,64,512]{2,1,0:T(8,128)(2,1)S(1)}, u32[]{:S(2)}, u32[]{:S(2)}) %collective-permute-start.5) | collective-permute-done | bytes 131104 | tf_op jit(solution)/shard_map/ppermute | solution.py:252
  26.3 0.1 convert_reduce_fusion
  26.4 1.5 %collective-permute-done.4.refs_4_.refs_3_ = bf16[5,64,512]{2,1,0:T(8,128)(2,1)S(1)} collective-permute-done((bf16[5,64,512]{2,1,0:T(8,128)(2,1)S(1)}, bf16[5,64,512]{2,1,0:T(8,128)(2,1)S(1)}, u32[]{:S(2)}, u32[]{:S(2)}) %collective-permute-start.4) | collective-permute-done | bytes 327712 | tf_op jit(solution)/shard_map/ppermute | solution.py:248
  27.9 0.1 collective-permute-start.9
  28.1 0.4 collective-permute-start.8
  28.4 0.1 collective-permute-start.6
  28.7 0.1 select_reduce_fusion.1
  28.7 0.1 copy.12.query_rank
  29.0 0.5 collective-permute-done.9.refs_10_.refs_9_
  29.5 0.4 collective-permute-done.8.refs_8_.refs_7_
  29.8 0.5 collective-permute-done.6.refs_6_.refs_5_
  30.3 2.2 %attend.3 = (bf16[2,272,128]{2,1,0:T(8,128)(2,1)S(1)}, bf16[2,272,128]{2,1,0:T(8,128)(2,1)S(1)}) custom-call(s32[1,512]{1,0:T(1,128)S(1)} %bitcast.4, s32[256,1]{1,0:T(8,128)S(1)} %copy.12.query_rank, bf16[2,64,512]{2,1,0:T(8,128)(2,1)S(1)} %collective-permute-done.5.refs_0_, bf16[2,64,512]{2,1,0:T(8,128)(2,1)S(1)} %collective-permute-done.11.refs_1_, ...), custom_call_target="tpu_custom_call" | custom-call | flops 536870912 | bytes 2621440 | tf_op jit(solution)/shard_map/attend/pallas_call | solution.py:146
  32.5 2.5 %collective-permute-start.16 = (bf16[2,272,128]{2,1,0:T(8,128)(2,1)S(1)}, bf16[2,272,128]{2,1,0:T(8,128)(2,1)S(1)}, u32[]{:S(2)}, u32[]{:S(2)}) collective-permute-start(bf16[2,272,128]{2,1,0:T(8,128)(2,1)S(1)} %get-tuple-element.42), channel_id=1, source_target_pairs={{0,12},{1,15},{2,14},{3,13},{4,8},{5,11},{6,10},{7,9},{8,4},{9,7},... | collective-permute-start | bytes 417800 | tf_op jit(solution)/shard_map/ppermute | solution.py:252
  35.0 0.1 copy.11.query_rank
  35.1 2.2 %attend.2 = (bf16[2,272,128]{2,1,0:T(8,128)(2,1)S(1)}, bf16[1,272,128]{2,1,0:T(8,128)(2,1)S(1)}, bf16[1,272,128]{2,1,0:T(8,128)(2,1)S(1)}) custom-call(s32[1,512]{1,0:T(1,128)S(1)} %bitcast.5, s32[256,1]{1,0:T(8,128)S(1)} %copy.11.query_rank, bf16[2,64,512]{2,1,0:T(8,128)(2,1)S(1)} %collective-permute-done.2.refs_0_, bf16[5,64,512]{2,1,0:T(8,128)(2,1)S(1)} %copy-done, ...), custom_call_target="tpu_custom_call" | custom-call | flops 536870912 | bytes 2621440 | tf_op jit(solution)/shard_map/attend/pallas_call | solution.py:146
  37.3 1.5 %collective-permute-start.14 = (bf16[2,272,128]{2,1,0:T(8,128)(2,1)S(1)}, bf16[2,272,128]{2,1,0:T(8,128)(2,1)S(1)}, u32[]{:S(2)}, u32[]{:S(2)}) collective-permute-start(bf16[2,272,128]{2,1,0:T(8,128)(2,1)S(1)} %get-tuple-element.41), channel_id=1, source_target_pairs={{0,4},{1,7},{2,6},{3,5},{4,0},{5,3},{6,2},{7,1},{8,12},{9,15},{10,... | collective-permute-start | bytes 417800 | tf_op jit(solution)/shard_map/ppermute | solution.py:252
  38.8 1.1 %collective-permute-start.12 = (bf16[2,272,128]{2,1,0:T(8,128)(2,1)S(1)}, bf16[2,272,128]{2,1,0:T(8,128)(2,1)S(1)}, u32[]{:S(2)}, u32[]{:S(2)}) collective-permute-start(bf16[2,272,128]{2,1,0:T(8,128)(2,1)S(1)} %get-tuple-element.40), channel_id=1, source_target_pairs={{0,8},{1,11},{2,10},{3,9},{4,12},{5,15},{6,14},{7,13},{8,0},{9,3},... | collective-permute-start | bytes 417800 | tf_op jit(solution)/shard_map/ppermute | solution.py:252
  39.9 0.5 %collective-permute-start.10 = (bf16[1,272,128]{2,1,0:T(8,128)(2,1)S(1)}, bf16[1,272,128]{2,1,0:T(8,128)(2,1)S(1)}, u32[]{:S(2)}, u32[]{:S(2)}) collective-permute-start(bf16[1,272,128]{2,1,0:T(8,128)(2,1)S(1)} %get-tuple-element.39), channel_id=1, source_target_pairs={{0,2},{1,3},{2,0},{3,1},{4,6},{5,7},{6,4},{7,5},{8,10},{9,11},{10,... | collective-permute-start | bytes 208904 | tf_op jit(solution)/shard_map/ppermute | solution.py:248
  40.4 0.4 collective-permute-start.17
  40.8 5.5 %collective-permute-done.14 = bf16[2,272,128]{2,1,0:T(8,128)(2,1)S(1)} collective-permute-done((bf16[2,272,128]{2,1,0:T(8,128)(2,1)S(1)}, bf16[2,272,128]{2,1,0:T(8,128)(2,1)S(1)}, u32[]{:S(2)}, u32[]{:S(2)}) %collective-permute-start.14) | collective-permute-done | bytes 139296 | tf_op jit(solution)/shard_map/ppermute | solution.py:252
  46.5 2.5 %collective-permute-done.12 = bf16[2,272,128]{2,1,0:T(8,128)(2,1)S(1)} collective-permute-done((bf16[2,272,128]{2,1,0:T(8,128)(2,1)S(1)}, bf16[2,272,128]{2,1,0:T(8,128)(2,1)S(1)}, u32[]{:S(2)}, u32[]{:S(2)}) %collective-permute-start.12) | collective-permute-done | bytes 139296 | tf_op jit(solution)/shard_map/ppermute | solution.py:252
  49.0 0.7 %collective-permute-start.13 = (bf16[1,272,128]{2,1,0:T(8,128)(2,1)S(1)}, bf16[1,272,128]{2,1,0:T(8,128)(2,1)S(1)}, u32[]{:S(2)}, u32[]{:S(2)}) collective-permute-start(bf16[1,272,128]{2,1,0:T(8,128)(2,1)S(1)} %get-tuple-element.51), channel_id=1, source_target_pairs={{0,1},{1,0},{2,3},{3,2},{4,5},{5,4},{6,7},{7,6},{8,9},{9,8},{10,11... | collective-permute-start | bytes 208904 | tf_op jit(solution)/shard_map/ppermute | solution.py:248
  49.7 1.1 %merge.2.refs_4_ = bf16[64,2048]{1,0:T(8,128)(2,1)} custom-call(s32[1]{0:T(128)} %bitcast.where, bf16[1,272,128]{2,1,0:T(8,128)(2,1)S(1)} %get-tuple-element.50.refs_0_, bf16[1,272,128]{2,1,0:T(8,128)(2,1)S(1)} %collective-permute-done.15.refs_1_, bf16[1,272,128]{2,1,0:T(8,128)(2,1)S(1)} %get-tuple-element.48.refs_2_, ...), custom_call_target="tpu_custom_call" | custom-call | tf_op jit(solution)/shard_map/merge/pallas_call | solution.py:212
  50.8 1.1 %merge.3 = bf16[64,2048]{1,0:T(8,128)(2,1)} custom-call(s32[1]{0:T(128)} %bitcast.where, bf16[1,272,128]{2,1,0:T(8,128)(2,1)S(1)} %get-tuple-element.38.refs_0_, bf16[1,272,128]{2,1,0:T(8,128)(2,1)S(1)} %collective-permute-done.10.refs_1_, bf16[1,272,128]{2,1,0:T(8,128)(2,1)S(1)} %get-tuple-element.52.refs_2_, ...), custom_call_target="tpu_custom_call", output_to_operand_aliasing={{}: (5, {})} | custom-call | tf_op jit(solution)/shard_map/merge/pallas_call | solution.py:212
  (44 shorter events, 0.7 us)
Async XLA Ops:
  2.4 4.8 %copy-start.1 = (bf16[2,64,512]{2,1,0:T(8,128)(2,1)S(1)}, bf16[2,64,512]{2,1,0:T(8,128)(2,1)}, u32[]{:S(2)}) copy-start(bf16[2,64,512]{2,1,0:T(8,128)(2,1)} %get-tuple-element.26) | copy-start | bytes 393220
  2.4 11.4 %collective-permute-start = (bf16[4,64,512]{2,1,0:T(8,128)(2,1)}, bf16[4,64,512]{2,1,0:T(8,128)(2,1)S(1)}, u32[]{:S(2)}, u32[]{:S(2)}) collective-permute-start(bf16[4,64,512]{2,1,0:T(8,128)(2,1)} %get-tuple-element.24), channel_id=1, source_target_pairs={{0,6},{1,7},{2,4},{3,5},{4,2},{5,3},{6,0},{7,1},{8,14},{9,15},{10,... | collective-permute-start | bytes 786440 | tf_op jit(solution)/shard_map/ppermute | solution.py:248
  6.4 1.6 %collective-permute-start.1 = (bf16[2,64,512]{2,1,0:T(8,128)(2,1)}, bf16[2,64,512]{2,1,0:T(8,128)(2,1)S(1)}, u32[]{:S(2)}, u32[]{:S(2)}) collective-permute-start(bf16[2,64,512]{2,1,0:T(8,128)(2,1)} %get-tuple-element.27), channel_id=1, source_target_pairs={{0,1},{1,0},{2,3},{3,2},{4,5},{5,4},{6,7},{7,6},{8,9},{9,8},{10,11... | collective-permute-start | bytes 393224 | tf_op jit(solution)/shard_map/ppermute | solution.py:248
  6.4 19.9 %collective-permute-start.7 = (bf16[4,64,512]{2,1,0:T(8,128)(2,1)}, bf16[4,64,512]{2,1,0:T(8,128)(2,1)S(1)}, u32[]{:S(2)}, u32[]{:S(2)}) collective-permute-start(bf16[4,64,512]{2,1,0:T(8,128)(2,1)} %get-tuple-element.33), channel_id=1, source_target_pairs={{0,4},{1,5},{2,6},{3,7},{4,0},{5,1},{6,2},{7,3},{8,12},{9,13},{10,... | collective-permute-start | bytes 786440 | tf_op jit(solution)/shard_map/ppermute | solution.py:248
  6.9 19.5 %collective-permute-start.3 = (bf16[5,64,512]{2,1,0:T(8,128)(2,1)}, bf16[5,64,512]{2,1,0:T(8,128)(2,1)S(1)}, u32[]{:S(2)}, u32[]{:S(2)}) collective-permute-start(bf16[5,64,512]{2,1,0:T(8,128)(2,1)} %get-tuple-element.29), channel_id=1, source_target_pairs={{0,2},{1,3},{2,0},{3,1},{4,6},{5,7},{6,4},{7,5},{8,10},{9,11},{10,... | collective-permute-start | bytes 983048 | tf_op jit(solution)/shard_map/ppermute | solution.py:248
  8.0 18.3 %copy-start = (bf16[5,64,512]{2,1,0:T(8,128)(2,1)S(1)}, bf16[5,64,512]{2,1,0:T(8,128)(2,1)}, u32[]{:S(2)}) copy-start(bf16[5,64,512]{2,1,0:T(8,128)(2,1)} %get-tuple-element.30.refs_1_.refs_3_.refs_2_) | copy-start | bytes 983044
  8.0 21.0 %collective-permute-start.11 = (bf16[2,64,512]{2,1,0:T(8,128)(2,1)S(1)}, bf16[2,64,512]{2,1,0:T(8,128)(2,1)S(1)}, u32[]{:S(2)}, u32[]{:S(2)}) collective-permute-start(bf16[2,64,512]{2,1,0:T(8,128)(2,1)S(1)} %pad_maximum_fusion), channel_id=1, source_target_pairs={{0,12},{1,15},{2,14},{3,13},{4,8},{5,11},{6,10},{7,9},{8,4},{9,7},... | collective-permute-start | bytes 393224 | tf_op jit(solution)/shard_map/ppermute | solution.py:252
  11.5 23.7 %collective-permute-start.2 = (bf16[2,64,512]{2,1,0:T(8,128)(2,1)S(1)}, bf16[2,64,512]{2,1,0:T(8,128)(2,1)S(1)}, u32[]{:S(2)}, u32[]{:S(2)}) collective-permute-start(bf16[2,64,512]{2,1,0:T(8,128)(2,1)S(1)} %pad_maximum_fusion), channel_id=1, source_target_pairs={{0,4},{1,7},{2,6},{3,5},{4,0},{5,3},{6,2},{7,1},{8,12},{9,15},{10,... | collective-permute-start | bytes 393224 | tf_op jit(solution)/shard_map/ppermute | solution.py:252
  11.5 5.7 %copy-start.2 = (s32[16]{0:T(128)S(1)}, s32[16]{0:T(128)}, u32[]{:S(2)}) copy-start(s32[16]{0:T(128)} %param.12) | copy-start | bytes 196
  13.8 12.5 %collective-permute-start.5 = (bf16[2,64,512]{2,1,0:T(8,128)(2,1)S(1)}, bf16[2,64,512]{2,1,0:T(8,128)(2,1)S(1)}, u32[]{:S(2)}, u32[]{:S(2)}) collective-permute-start(bf16[2,64,512]{2,1,0:T(8,128)(2,1)S(1)} %pad_maximum_fusion.1), channel_id=1, source_target_pairs={{0,8},{1,11},{2,10},{3,9},{4,12},{5,15},{6,14},{7,13},{8,0},{9,3},... | collective-permute-start | bytes 393224 | tf_op jit(solution)/shard_map/ppermute | solution.py:252
  26.3 1.6 %collective-permute-start.4 = (bf16[5,64,512]{2,1,0:T(8,128)(2,1)S(1)}, bf16[5,64,512]{2,1,0:T(8,128)(2,1)S(1)}, u32[]{:S(2)}, u32[]{:S(2)}) collective-permute-start(bf16[5,64,512]{2,1,0:T(8,128)(2,1)S(1)} %copy-done), channel_id=1, source_target_pairs={{0,1},{1,0},{2,3},{3,2},{4,5},{5,4},{6,7},{7,6},{8,9},{9,8},{10,11... | collective-permute-start | bytes 983048 | tf_op jit(solution)/shard_map/ppermute | solution.py:248
  26.4 2.2 %copy-start.3 = (s32[16]{0:T(128)S(1)}, s32[16]{0:T(128)}, u32[]{:S(2)}) copy-start(s32[16]{0:T(128)} %param.13) | copy-start | bytes 196
  27.9 1.5 %collective-permute-start.9 = (bf16[4,64,512]{2,1,0:T(8,128)(2,1)S(1)}, bf16[4,64,512]{2,1,0:T(8,128)(2,1)S(1)}, u32[]{:S(2)}, u32[]{:S(2)}) collective-permute-start(bf16[4,64,512]{2,1,0:T(8,128)(2,1)S(1)} %collective-permute-done.refs_9_.refs_8_), channel_id=1, source_target_pairs={{0,1},{1,0},{2,3},{3,2},{4,5},{5,4},{6,7},{7,6},{8,9},{9,8},{10,11... | collective-permute-start | bytes 786440 | tf_op jit(solution)/shard_map/ppermute | solution.py:248
  28.1 1.8 %collective-permute-start.8 = (bf16[4,64,512]{2,1,0:T(8,128)(2,1)S(1)}, bf16[4,64,512]{2,1,0:T(8,128)(2,1)S(1)}, u32[]{:S(2)}, u32[]{:S(2)}) collective-permute-start(bf16[4,64,512]{2,1,0:T(8,128)(2,1)S(1)} %collective-permute-done.7.refs_7_.refs_6_), channel_id=1, source_target_pairs={{0,1},{1,0},{2,3},{3,2},{4,5},{5,4},{6,7},{7,6},{8,9},{9,8},{10,11... | collective-permute-start | bytes 786440 | tf_op jit(solution)/shard_map/ppermute | solution.py:248
  28.4 1.9 %collective-permute-start.6 = (bf16[5,64,512]{2,1,0:T(8,128)(2,1)S(1)}, bf16[5,64,512]{2,1,0:T(8,128)(2,1)S(1)}, u32[]{:S(2)}, u32[]{:S(2)}) collective-permute-start(bf16[5,64,512]{2,1,0:T(8,128)(2,1)S(1)} %collective-permute-done.3.refs_2_.refs_5_.refs_4_), channel_id=1, source_target_pairs={{0,1},{1,0},{2,3},{3,2},{4,5},{5,4},{6,7},{7,6},{8,9},{9,8},{10,11... | collective-permute-start | bytes 983048 | tf_op jit(solution)/shard_map/ppermute | solution.py:248
  32.5 7.9 %collective-permute-start.16 = (bf16[2,272,128]{2,1,0:T(8,128)(2,1)S(1)}, bf16[2,272,128]{2,1,0:T(8,128)(2,1)S(1)}, u32[]{:S(2)}, u32[]{:S(2)}) collective-permute-start(bf16[2,272,128]{2,1,0:T(8,128)(2,1)S(1)} %get-tuple-element.42), channel_id=1, source_target_pairs={{0,12},{1,15},{2,14},{3,13},{4,8},{5,11},{6,10},{7,9},{8,4},{9,7},... | collective-permute-start | bytes 417800 | tf_op jit(solution)/shard_map/ppermute | solution.py:252
  37.3 9.0 %collective-permute-start.14 = (bf16[2,272,128]{2,1,0:T(8,128)(2,1)S(1)}, bf16[2,272,128]{2,1,0:T(8,128)(2,1)S(1)}, u32[]{:S(2)}, u32[]{:S(2)}) collective-permute-start(bf16[2,272,128]{2,1,0:T(8,128)(2,1)S(1)} %get-tuple-element.41), channel_id=1, source_target_pairs={{0,4},{1,7},{2,6},{3,5},{4,0},{5,3},{6,2},{7,1},{8,12},{9,15},{10,... | collective-permute-start | bytes 417800 | tf_op jit(solution)/shard_map/ppermute | solution.py:252
  38.8 10.2 %collective-permute-start.12 = (bf16[2,272,128]{2,1,0:T(8,128)(2,1)S(1)}, bf16[2,272,128]{2,1,0:T(8,128)(2,1)S(1)}, u32[]{:S(2)}, u32[]{:S(2)}) collective-permute-start(bf16[2,272,128]{2,1,0:T(8,128)(2,1)S(1)} %get-tuple-element.40), channel_id=1, source_target_pairs={{0,8},{1,11},{2,10},{3,9},{4,12},{5,15},{6,14},{7,13},{8,0},{9,3},... | collective-permute-start | bytes 417800 | tf_op jit(solution)/shard_map/ppermute | solution.py:252
  39.9 10.9 %collective-permute-start.10 = (bf16[1,272,128]{2,1,0:T(8,128)(2,1)S(1)}, bf16[1,272,128]{2,1,0:T(8,128)(2,1)S(1)}, u32[]{:S(2)}, u32[]{:S(2)}) collective-permute-start(bf16[1,272,128]{2,1,0:T(8,128)(2,1)S(1)} %get-tuple-element.39), channel_id=1, source_target_pairs={{0,2},{1,3},{2,0},{3,1},{4,6},{5,7},{6,4},{7,5},{8,10},{9,11},{10,... | collective-permute-start | bytes 208904 | tf_op jit(solution)/shard_map/ppermute | solution.py:248
  40.4 9.3 %collective-permute-start.17 = (bf16[1,272,128]{2,1,0:T(8,128)(2,1)S(1)}, bf16[1,272,128]{2,1,0:T(8,128)(2,1)S(1)}, u32[]{:S(2)}, u32[]{:S(2)}) collective-permute-start(bf16[1,272,128]{2,1,0:T(8,128)(2,1)S(1)} %get-tuple-element.47), channel_id=1, source_target_pairs={{0,1},{1,0},{2,3},{3,2},{4,5},{5,4},{6,7},{7,6},{8,9},{9,8},{10,11... | collective-permute-start | bytes 208904 | tf_op jit(solution)/shard_map/ppermute | solution.py:248
  46.4 3.3 %collective-permute-start.15 = (bf16[1,272,128]{2,1,0:T(8,128)(2,1)S(1)}, bf16[1,272,128]{2,1,0:T(8,128)(2,1)S(1)}, u32[]{:S(2)}, u32[]{:S(2)}) collective-permute-start(bf16[1,272,128]{2,1,0:T(8,128)(2,1)S(1)} %get-tuple-element.49), channel_id=1, source_target_pairs={{0,1},{1,0},{2,3},{3,2},{4,5},{5,4},{6,7},{7,6},{8,9},{9,8},{10,11... | collective-permute-start | bytes 208904 | tf_op jit(solution)/shard_map/ppermute | solution.py:248
  49.0 1.8 %collective-permute-start.13 = (bf16[1,272,128]{2,1,0:T(8,128)(2,1)S(1)}, bf16[1,272,128]{2,1,0:T(8,128)(2,1)S(1)}, u32[]{:S(2)}, u32[]{:S(2)}) collective-permute-start(bf16[1,272,128]{2,1,0:T(8,128)(2,1)S(1)} %get-tuple-element.51), channel_id=1, source_target_pairs={{0,1},{1,0},{2,3},{3,2},{4,5},{5,4},{6,7},{7,6},{8,9},{9,8},{10,11... | collective-permute-start | bytes 208904 | tf_op jit(solution)/shard_map/ppermute | solution.py:248
